TPU v7x, 32 devices: a whole 2x2x4 slice. The times are simulated.
32 devices in a mesh: shard: 4 (over x, core), ctx: 2 (over y), tp: 4 (over z).
Axes of the slice: x: 2, y: 2, z: 4, core: 2. Of those that a mesh axis runs over, the one named last changes fastest.
Arguments:
- tokens: bfloat16 [8192, 2048], P(('shard', 'ctx')), may hold values from -6 to 6
- cotangent: bfloat16 [8192, 2048], P(('shard', 'ctx')), may hold values from -6 to 6
- lengths: int32 [4], P('shard'), may hold values from 1024 to 2048, as said below
- qkv_weight: float32 [3, 2048, 2048], P(None, ('shard', 'ctx'), 'tp'), may hold values from -0.125 to 0.125
- out_weight: float32 [2048, 2048], P('tp', ('shard', 'ctx')), may hold values from -2 to 2
- gate_up_weight: float32 [2, 2048, 8192], P(None, ('shard', 'ctx'), 'tp'), may hold values from -0.125 to 0.125
- down_weight: float32 [8192, 2048], P('tp', ('shard', 'ctx')), may hold values from -0.0625 to 0.0625
- norm_gains: float32 [2, 2048], P(None, ('shard', 'ctx')), may hold values from 0.5 to 1.5
- qkv_first: float32 [3, 2048, 2048], P(None, ('shard', 'ctx'), 'tp'), may hold values from -34.212654 to 34.212654
- out_first: float32 [2048, 2048], P('tp', ('shard', 'ctx')), may hold values from -0.6 to 0.6
- gate_up_first: float32 [2, 2048, 8192], P(None, ('shard', 'ctx'), 'tp'), may hold values from -0.6 to 0.6
- down_first: float32 [8192, 2048], P('tp', ('shard', 'ctx')), may hold values from -0.6 to 0.6
- gains_first: float32 [2, 2048], P(None, ('shard', 'ctx')), may hold values from -54.3058 to 54.3058
- qkv_second: float32 [3, 2048, 2048], P(None, ('shard', 'ctx'), 'tp'), may hold values from 491.52 to 1638.4
- out_second: float32 [2048, 2048], P('tp', ('shard', 'ctx')), may hold values from 44.2368 to 147.456
- gate_up_second: float32 [2, 2048, 8192], P(None, ('shard', 'ctx'), 'tp'), may hold values from 30.72 to 102.4
- down_second: float32 [8192, 2048], P('tp', ('shard', 'ctx')), may hold values from 122.88 to 409.6
- gains_second: float32 [2, 2048], P(None, ('shard', 'ctx')), may hold values from 491.52 to 1638.4
Outputs:
- out_tokens: bfloat16 [8192, 2048], P(('shard', 'ctx'))
- input_grad: bfloat16 [8192, 2048], P(('shard', 'ctx'))
- qkv_grad: float32 [3, 2048, 2048], P(None, ('shard', 'ctx'), 'tp')
- out_grad: float32 [2048, 2048], P('tp', ('shard', 'ctx'))
- gate_up_grad: float32 [2, 2048, 8192], P(None, ('shard', 'ctx'), 'tp')
- down_grad: float32 [8192, 2048], P('tp', ('shard', 'ctx'))
- gains_grad: float32 [2, 2048], P(None, ('shard', 'ctx'))
- qkv_new: float32 [3, 2048, 2048], P(None, ('shard', 'ctx'), 'tp')
- out_step: float32 [2048, 2048], P('tp', ('shard', 'ctx'))
- gate_up_new: float32 [2, 2048, 8192], P(None, ('shard', 'ctx'), 'tp')
- down_new: float32 [8192, 2048], P('tp', ('shard', 'ctx'))
- gains_step: float32 [2, 2048], P(None, ('shard', 'ctx'))
- qkv_first_new: float32 [3, 2048, 2048], P(None, ('shard', 'ctx'), 'tp')
- out_first_new: float32 [2048, 2048], P('tp', ('shard', 'ctx'))
- gate_up_first_new: float32 [2, 2048, 8192], P(None, ('shard', 'ctx'), 'tp')
- down_first_new: float32 [8192, 2048], P('tp', ('shard', 'ctx'))
- gains_first_new: float32 [2, 2048], P(None, ('shard', 'ctx'))
- qkv_second_new: float32 [3, 2048, 2048], P(None, ('shard', 'ctx'), 'tp')
- out_second_new: float32 [2048, 2048], P('tp', ('shard', 'ctx'))
- gate_up_second_new: float32 [2, 2048, 8192], P(None, ('shard', 'ctx'), 'tp')
- down_second_new: float32 [8192, 2048], P('tp', ('shard', 'ctx'))
- gains_second_new: float32 [2, 2048], P(None, ('shard', 'ctx'))
Inputs may be any that keep to these rules, and one draw needn't show every extreme that they name: lengths[s] is the length of the sequence of pack s; the first pack's sequence fills its whole pack of 2048 rows.
All inputs are finite; a program needn't handle non-finite values.
Results may differ from a plain program's by a relative error of at most 0.015.
The roundings to bfloat16 on the way count: a program that leaves them out, or rounds other values in their place, can miss the bound.
Values may be sent and summed in bfloat16 or wider, within the bound.
A program may use at most 384 MiB of HBM per device.

v0:
```python
import jax
import jax.numpy as jnp
from jax import lax
from jax.sharding import PartitionSpec as P

HEAD = 64


norm_eps = 1e-05
rope_base = 130000.0
beta_one = 0.9
beta_two = 0.95
learn_rate = 0.02
decay_rate = 0.1
adam_eps = 1e-08
step_count = 4.0


def rotation(position, head_size):
    half = head_size // 2
    freqs = rope_base ** (-(jnp.arange(half, dtype=jnp.float32) * 2.0) / head_size)
    angle = position.astype(jnp.float32)[:, None] * freqs[None, :]
    return (jnp.cos(angle)[:, None, :], jnp.sin(angle)[:, None, :])


def rotate(values, cosine, sine):
    half = values.shape[-1] // 2
    first, second = (values[..., :half], values[..., half:])
    return jnp.concatenate([first * cosine - second * sine, second * cosine + first * sine], -1)


def outer_sum(left, right):
    return lax.dot_general(
        left, right, (((0,), (0,)), ((), ())), preferred_element_type=jnp.float32
    )


def back_dot(grad, weight):
    return lax.dot_general(
        grad, weight, (((1,), (1,)), ((), ())), preferred_element_type=jnp.float32
    )


def normalize(stream, gain):
    scale = lax.rsqrt(jnp.mean(stream * stream, axis=-1, keepdims=True) + norm_eps)
    return ((stream * scale * gain).astype(jnp.bfloat16), scale)


def normalize_back(stream, scale, gain, upstream):
    gain_grad = jnp.sum(upstream * stream * scale, axis=0)
    inner = jnp.sum(upstream * gain * stream, axis=-1, keepdims=True)
    stream_grad = (
        scale * gain * upstream - stream * (scale * scale * scale / stream.shape[-1]) * inner
    )
    return (stream_grad, gain_grad)


def block_scores(rows_query, keys, key_mask):
    scores = (
        jnp.einsum("qhd,khd->hqk", rows_query, keys, preferred_element_type=jnp.float32) * 0.125
    )
    return jnp.where(key_mask[None], scores, -1e30)


def attend_forward(query, keys, values, key_mask, block):
    outputs = []
    totals = []
    for begin in range(0, query.shape[0], block):
        scores = block_scores(query[begin : begin + block], keys, key_mask[begin : begin + block])
        peak = jnp.max(scores, axis=-1, keepdims=True)
        expo = jnp.exp(scores - peak)
        denom = jnp.sum(expo, axis=-1, keepdims=True)
        probs = (expo / denom).astype(jnp.bfloat16)
        outputs.append(
            jnp.einsum("hqk,khd->qhd", probs, values, preferred_element_type=jnp.float32)
        )
        totals.append(peak + jnp.log(denom))
    return (jnp.concatenate(outputs, 0), jnp.concatenate(totals, 1))


def attend_back(query, keys, values, key_mask, totals, upstream, block):
    query_grads = []
    key_grad = jnp.zeros(keys.shape, jnp.float32)
    value_grad = jnp.zeros(values.shape, jnp.float32)
    for begin in range(0, query.shape[0], block):
        rows_query = query[begin : begin + block]
        rows_grad = upstream[begin : begin + block]
        scores = block_scores(rows_query, keys, key_mask[begin : begin + block])
        probs = jnp.exp(scores - totals[:, begin : begin + block])
        probs_low = probs.astype(jnp.bfloat16)
        prob_grad = jnp.einsum(
            "qhd,khd->hqk", rows_grad, values, preferred_element_type=jnp.float32
        )
        inner = jnp.sum(prob_grad * probs, axis=-1, keepdims=True)
        score_grad = (probs * (prob_grad - inner)).astype(jnp.bfloat16)
        query_grads.append(
            jnp.einsum("hqk,khd->qhd", score_grad, keys, preferred_element_type=jnp.float32) * 0.125
        )
        key_grad = (
            key_grad
            + jnp.einsum("hqk,qhd->khd", score_grad, rows_query, preferred_element_type=jnp.float32)
            * 0.125
        )
        value_grad = value_grad + jnp.einsum(
            "hqk,qhd->khd", probs_low, rows_grad, preferred_element_type=jnp.float32
        )
    return (jnp.concatenate(query_grads, 0), key_grad, value_grad)


def adam_update(weight, first, second, grad, decay):
    first_new = beta_one * first + (1.0 - beta_one) * grad
    second_new = beta_two * second + (1.0 - beta_two) * grad * grad
    first_hat = first_new / (1.0 - beta_one**step_count)
    second_hat = second_new / (1.0 - beta_two**step_count)
    update = learn_rate * (first_hat / (jnp.sqrt(second_hat) + adam_eps) + decay * weight)
    return (update, first_new, second_new)


def body(
    tokens,
    cotangent,
    lengths,
    qkv_weight,
    out_weight,
    gate_up_weight,
    down_weight,
    norm_gains,
    qkv_first,
    out_first,
    gate_up_first,
    down_first,
    gains_first,
    qkv_second,
    out_second,
    gate_up_second,
    down_second,
    gains_second,
):
    row_count = tokens.shape[0]
    group_rows = row_count * lax.axis_size("ctx")
    live = lengths[0]
    offset = lax.axis_index("ctx") * row_count
    query_index = offset + jnp.arange(row_count, dtype=jnp.int32)
    key_index = jnp.arange(group_rows, dtype=jnp.int32)
    key_mask = (key_index[None, :] <= query_index[:, None]) & (
        (query_index[:, None] < live) | (key_index[None, :] == query_index[:, None])
    )
    block = min(512, row_count)
    qkv_low = qkv_weight.astype(jnp.bfloat16)
    out_low = out_weight.astype(jnp.bfloat16)
    gate_up_low = gate_up_weight.astype(jnp.bfloat16)
    down_low = down_weight.astype(jnp.bfloat16)
    gains_low = norm_gains.astype(jnp.bfloat16)
    qkv_full, out_full, gate_up_full, down_full, gains_full = (
        lax.all_gather(qkv_low, ("shard", "ctx"), axis=1, tiled=True),
        lax.all_gather(out_low, ("shard", "ctx"), axis=1, tiled=True),
        lax.all_gather(gate_up_low, ("shard", "ctx"), axis=1, tiled=True),
        lax.all_gather(down_low, ("shard", "ctx"), axis=1, tiled=True),
        lax.all_gather(gains_low, ("shard", "ctx"), axis=1, tiled=True),
    )
    gain_one = gains_full[0].astype(jnp.float32)
    gain_two = gains_full[1].astype(jnp.float32)
    stream = tokens.astype(jnp.float32)
    normed_one, scale_one = normalize(stream, gain_one)
    cosine, sine = rotation(query_index, HEAD)
    local_width = qkv_full.shape[2]
    heads_local = local_width // HEAD
    shape3 = (row_count, heads_local, HEAD)
    query = rotate(
        jnp.dot(normed_one, qkv_full[0], preferred_element_type=jnp.float32).reshape(shape3),
        cosine,
        sine,
    ).astype(jnp.bfloat16)
    keys_own = (
        rotate(
            jnp.dot(normed_one, qkv_full[1], preferred_element_type=jnp.float32).reshape(shape3),
            cosine,
            sine,
        )
        .astype(jnp.bfloat16)
        .reshape(row_count, local_width)
    )
    values_own = jnp.dot(normed_one, qkv_full[2], preferred_element_type=jnp.float32).astype(
        jnp.bfloat16
    )
    keys_all, values_all = (
        lax.all_gather(keys_own, "ctx", axis=0, tiled=True),
        lax.all_gather(values_own, "ctx", axis=0, tiled=True),
    )
    keys_all = keys_all.reshape(group_rows, heads_local, HEAD)
    values_all = values_all.reshape(group_rows, heads_local, HEAD)
    mixed, totals = attend_forward(query, keys_all, values_all, key_mask, block)
    mixed_low = mixed.reshape(row_count, local_width).astype(jnp.bfloat16)
    attn_part = jnp.dot(mixed_low, out_full, preferred_element_type=jnp.float32)
    middle = stream + lax.psum(attn_part, "tp")
    normed_two, scale_two = normalize(middle, gain_two)
    gate = jnp.dot(normed_two, gate_up_full[0], preferred_element_type=jnp.float32)
    upward = jnp.dot(normed_two, gate_up_full[1], preferred_element_type=jnp.float32)
    sigma = jax.nn.sigmoid(gate)
    swish = gate * sigma
    hidden = (swish * upward).astype(jnp.bfloat16)
    mlp_part = jnp.dot(hidden, down_full, preferred_element_type=jnp.float32)
    out_tokens = (
        middle + lax.psum(mlp_part.astype(jnp.bfloat16), "tp").astype(jnp.float32)
    ).astype(jnp.bfloat16)
    qkv_use, out_use, gate_up_use, down_use = (qkv_full, out_full, gate_up_full, down_full)
    upstream = cotangent.astype(jnp.float32)
    upstream_low = upstream.astype(jnp.bfloat16)
    down_grad_local = outer_sum(hidden, upstream_low)
    hidden_grad = back_dot(upstream_low, down_use)
    gate_grad = (hidden_grad * upward * sigma * (1.0 + gate * (1.0 - sigma))).astype(jnp.bfloat16)
    upward_grad = (hidden_grad * swish).astype(jnp.bfloat16)
    gate_up_grad_local = jnp.stack(
        [outer_sum(normed_two, gate_grad), outer_sum(normed_two, upward_grad)]
    )
    mlp_back_part = back_dot(gate_grad, gate_up_use[0]) + back_dot(upward_grad, gate_up_use[1])
    normed_two_grad = lax.psum(mlp_back_part, "tp")
    middle_norm_grad, gain_two_grad = normalize_back(middle, scale_two, gain_two, normed_two_grad)
    middle_grad = upstream + middle_norm_grad
    middle_low = middle_grad.astype(jnp.bfloat16)
    out_grad_local = outer_sum(mixed_low, middle_low)
    mixed_grad = back_dot(middle_low, out_use).astype(jnp.bfloat16).reshape(shape3)
    query_grad, key_grad, value_grad = attend_back(
        query, keys_all, values_all, key_mask, totals, mixed_grad, block
    )
    key_own_grad, value_own_grad = (
        lax.psum_scatter(
            key_grad.reshape(group_rows, local_width), "ctx", scatter_dimension=0, tiled=True
        ),
        lax.psum_scatter(
            value_grad.reshape(group_rows, local_width), "ctx", scatter_dimension=0, tiled=True
        ),
    )
    query_low = (
        rotate(query_grad, cosine, -sine).reshape(row_count, local_width).astype(jnp.bfloat16)
    )
    key_low = (
        rotate(key_own_grad.reshape(shape3), cosine, -sine)
        .reshape(row_count, local_width)
        .astype(jnp.bfloat16)
    )
    value_low = value_own_grad.astype(jnp.bfloat16)
    qkv_grad_local = jnp.stack(
        [
            outer_sum(normed_one, query_low),
            outer_sum(normed_one, key_low),
            outer_sum(normed_one, value_low),
        ]
    )
    attn_back_part = (
        back_dot(query_low, qkv_use[0])
        + back_dot(key_low, qkv_use[1])
        + back_dot(value_low, qkv_use[2])
    )
    normed_one_grad = lax.psum(attn_back_part, "tp")
    stream_grad, gain_one_grad = normalize_back(stream, scale_one, gain_one, normed_one_grad)
    input_grad = (middle_grad + stream_grad).astype(jnp.bfloat16)
    gains_local = jnp.stack([gain_one_grad, gain_two_grad])
    qkv_grad, out_grad, gate_up_grad, down_grad, gains_grad = (
        lax.psum_scatter(qkv_grad_local, ("shard", "ctx"), scatter_dimension=1, tiled=True),
        lax.psum_scatter(out_grad_local, ("shard", "ctx"), scatter_dimension=1, tiled=True),
        lax.psum_scatter(gate_up_grad_local, ("shard", "ctx"), scatter_dimension=1, tiled=True),
        lax.psum_scatter(down_grad_local, ("shard", "ctx"), scatter_dimension=1, tiled=True),
        lax.psum_scatter(gains_local, ("shard", "ctx"), scatter_dimension=1, tiled=True),
    )
    qkv_step, qkv_first_new, qkv_second_new = adam_update(
        qkv_weight, qkv_first, qkv_second, qkv_grad, decay_rate
    )
    out_step, out_first_new, out_second_new = adam_update(
        out_weight, out_first, out_second, out_grad, decay_rate
    )
    gate_up_step, gate_up_first_new, gate_up_second_new = adam_update(
        gate_up_weight, gate_up_first, gate_up_second, gate_up_grad, decay_rate
    )
    down_step, down_first_new, down_second_new = adam_update(
        down_weight, down_first, down_second, down_grad, decay_rate
    )
    gains_step, gains_first_new, gains_second_new = adam_update(
        norm_gains, gains_first, gains_second, gains_grad, 0.0
    )
    qkv_new = qkv_weight - qkv_step
    gate_up_new = gate_up_weight - gate_up_step
    down_new = down_weight - down_step
    return (
        out_tokens,
        input_grad,
        qkv_grad,
        out_grad,
        gate_up_grad,
        down_grad,
        gains_grad,
        qkv_new,
        out_step,
        gate_up_new,
        down_new,
        gains_step,
        qkv_first_new,
        out_first_new,
        gate_up_first_new,
        down_first_new,
        gains_first_new,
        qkv_second_new,
        out_second_new,
        gate_up_second_new,
        down_second_new,
        gains_second_new,
    )


def solution(mesh):
    return jax.shard_map(
        body,
        mesh=mesh,
        in_specs=(
            P(("shard", "ctx"), None),
            P(("shard", "ctx"), None),
            P("shard"),
            P(None, ("shard", "ctx"), "tp"),
            P("tp", ("shard", "ctx")),
            P(None, ("shard", "ctx"), "tp"),
            P("tp", ("shard", "ctx")),
            P(None, ("shard", "ctx")),
            P(None, ("shard", "ctx"), "tp"),
            P("tp", ("shard", "ctx")),
            P(None, ("shard", "ctx"), "tp"),
            P("tp", ("shard", "ctx")),
            P(None, ("shard", "ctx")),
            P(None, ("shard", "ctx"), "tp"),
            P("tp", ("shard", "ctx")),
            P(None, ("shard", "ctx"), "tp"),
            P("tp", ("shard", "ctx")),
            P(None, ("shard", "ctx")),
        ),
        out_specs=(
            P(("shard", "ctx"), None),
            P(("shard", "ctx"), None),
            P(None, ("shard", "ctx"), "tp"),
            P("tp", ("shard", "ctx")),
            P(None, ("shard", "ctx"), "tp"),
            P("tp", ("shard", "ctx")),
            P(None, ("shard", "ctx")),
            P(None, ("shard", "ctx"), "tp"),
            P("tp", ("shard", "ctx")),
            P(None, ("shard", "ctx"), "tp"),
            P("tp", ("shard", "ctx")),
            P(None, ("shard", "ctx")),
            P(None, ("shard", "ctx"), "tp"),
            P("tp", ("shard", "ctx")),
            P(None, ("shard", "ctx"), "tp"),
            P("tp", ("shard", "ctx")),
            P(None, ("shard", "ctx")),
            P(None, ("shard", "ctx"), "tp"),
            P("tp", ("shard", "ctx")),
            P(None, ("shard", "ctx"), "tp"),
            P("tp", ("shard", "ctx")),
            P(None, ("shard", "ctx")),
        ),
        check_vma=False,
    )
```

profile of v0, /device:TPU:0, one launch (start us, length us, event | category | flops | bytes accessed | tf_op | source)
XLA Modules:
  0.0 2237.7 jit_solution(5836895930422642615)
XLA Ops:
  30.1 28.7 %all-gather.7.cloned.1.call-done = bf16[3,2048,512]{2,1,0:T(8,128)(2,1)} async-done(((bf16[3,256,512]{2,1,0:T(8,128)(2,1)}), bf16[3,2048,512]{2,1,0:T(8,128)(2,1)}) %all-gather.7.cloned.1.call-update) | async-done | bytes 6291472 | tf_op jit(solution)/shard_map/all_gather | solution.py:155
  90.3 21.7 all-gather.11.cloned.1.call-done
  112.0 16.5 fusion.91
  214.5 285.7 %all-reduce.5.cloned.1.call-done = f32[1024,2048]{1,0:T(8,128)} async-done(((f32[1024,2048]{1,0:T(8,128)}), f32[1024,2048]{1,0:T(8,128)}) %all-reduce.5.cloned.1.call-update) | async-done | bytes 8388624 | tf_op jit(solution)/shard_map/psum | solution.py:195
  512.6 78.9 %all-gather.15.cloned.1.call-done = bf16[2,2048,2048]{2,1,0:T(8,128)(2,1)} async-done(((bf16[2,256,2048]{2,1,0:T(8,128)(2,1)}), bf16[2,2048,2048]{2,1,0:T(8,128)(2,1)}) %all-gather.15.cloned.1.call-update) | async-done | bytes 16777232 | tf_op jit(solution)/shard_map/all_gather | solution.py:157
  591.5 15.8 fusion.26
  618.4 31.5 %all-gather.17.cloned.1.call-done = bf16[2048,2048]{1,0:T(8,128)(2,1)} async-done(((bf16[2048,256]{1,0:T(8,128)(2,1)}), bf16[2048,2048]{1,0:T(8,128)(2,1)}) %all-gather.17.cloned.1.call-update) | async-done | bytes 8388624 | tf_op jit(solution)/shard_map/all_gather | solution.py:158
  649.9 21.8 multiply_convert_fusion.2
  713.2 276.4 %all-reduce.9.cloned.1.call-done = f32[1024,2048]{1,0:T(8,128)} async-done(((f32[1024,2048]{1,0:T(8,128)}), f32[1024,2048]{1,0:T(8,128)}) %all-reduce.9.cloned.1.call-update) | async-done | bytes 8388624 | tf_op jit(solution)/shard_map/psum | solution.py:217
  997.4 149.2 %all-reduce.7.cloned.1.call-done = bf16[1024,2048]{1,0:T(8,128)(2,1)} async-done(((bf16[1024,2048]{1,0:T(8,128)(2,1)}), bf16[1024,2048]{1,0:T(8,128)(2,1)}) %all-reduce.7.cloned.1.call-update) | async-done | bytes 4194320 | tf_op jit(solution)/shard_map/psum | solution.py:204
  1162.8 22.3 multiply_reduce_fusion.1
  1185.2 27.9 %multiply_convert_fusion.1 = bf16[8,512,2048]{2,1,0:T(8,128)(2,1)} fusion(f32[8,512,2048]{2,1,0:T(8,128)} %get-tuple-element.80, f32[8,512,2048]{2,1,0:T(8,128)} %get-tuple-element.78, f32[8,512]{1,0:T(8,128)S(1)} %get-tuple-element.79, f32[8,512]{1,0:T(8,128)S(1)} %log_add_fusion.1), kind=kLoop, calls=%fused_computation.4 | loop fusion | flops 33554432 | bytes 83918848 | tf_op jit(solution)/shard_map/convert_element_type | solution.py:95
  1223.9 22.2 multiply_reduce_fusion
  1246.1 27.9 %multiply_convert_fusion = bf16[8,512,2048]{2,1,0:T(8,128)(2,1)} fusion(f32[8,512,2048]{2,1,0:T(8,128)} %get-tuple-element.82, f32[8,512,2048]{2,1,0:T(8,128)} %get-tuple-element.76, f32[8,512]{1,0:T(8,128)S(1)} %get-tuple-element.81, f32[8,512]{1,0:T(8,128)S(1)} %log_add_fusion), kind=kLoop, calls=%fused_computation.1 | loop fusion | flops 33554432 | bytes 83918848 | tf_op jit(solution)/shard_map/convert_element_type | solution.py:95
  1287.1 16.0 fusion.4
  1303.1 17.5 fusion.35
  1363.0 33.2 %reduce-scatter.12.cloned.1.call-done = f32[1024,512]{0,1:T(8,128)} async-done(((f32[2048,512]{0,1:T(8,128)}), f32[1024,512]{0,1:T(8,128)}) %reduce-scatter.12.cloned.1.call-update) | async-done | bytes 2097168 | tf_op jit(solution)/shard_map/reduce_scatter | solution.py:230
  1417.9 15.3 fusion.93
  1450.4 249.5 %all-reduce.11.cloned.1.call-done = f32[1024,2048]{1,0:T(8,128)} async-done(((f32[1024,2048]{1,0:T(8,128)}), f32[1024,2048]{1,0:T(8,128)}) %all-reduce.11.cloned.1.call-update) | async-done | bytes 8388624 | tf_op jit(solution)/shard_map/psum | solution.py:255
  1743.9 18.6 pad_maximum_fusion
  1766.7 107.8 %reduce-scatter.20.cloned.1.call-done = f32[2048,256]{1,0:T(8,128)} async-done(((f32[2048,2048]{1,0:T(8,128)}), f32[2048,256]{1,0:T(8,128)}) %reduce-scatter.20.cloned.1.call-update) | async-done | bytes 2097168 | tf_op jit(solution)/shard_map/reduce_scatter | solution.py:263
  1891.1 23.0 %reduce-scatter.22.cloned.1.call-done = f32[256,2]{1,0:T(8,128)} async-done(((f32[2048,2]{1,0:T(8,128)}), f32[256,2]{1,0:T(8,128)}) %reduce-scatter.22.cloned.1.call-update) | async-done | bytes 2064
  1915.7 94.7 %reduce-scatter.14.cloned.1.call-done = f32[3,256,512]{2,1,0:T(8,128)} async-done(((f32[3,2048,512]{2,1,0:T(8,128)}), f32[3,256,512]{2,1,0:T(8,128)}) %reduce-scatter.14.cloned.1.call-update) | async-done | bytes 1572880 | tf_op jit(solution)/shard_map/reduce_scatter | solution.py:260
  2015.4 204.3 %reduce-scatter.18.cloned.1.call-done = f32[2,256,2048]{2,1,0:T(8,128)} async-done(((f32[2,2048,2048]{2,1,0:T(8,128)}), f32[2,256,2048]{2,1,0:T(8,128)}) %reduce-scatter.18.cloned.1.call-update) | async-done | bytes 4194320 | tf_op jit(solution)/shard_map/reduce_scatter | solution.py:262
  (213 shorter events, 415.4 us)
Async XLA Ops:
  7.2 51.6 %all-gather.7.cloned.1.call-start = ((), (), s32[]{:S(2)}) async-start(), calls=%async_computation.7 | async-start | bytes 7077888 | tf_op jit(solution)/shard_map/all_gather | solution.py:155
  9.6 102.4 %all-gather.11.cloned.1.call-start = ((), (), s32[]{:S(2)}) async-start(), calls=%async_computation.9 | async-start | bytes 3145728 | tf_op jit(solution)/shard_map/all_gather | solution.py:187
  78.7 77.3 %all-gather.9.cloned.1.call-start = ((), (), s32[]{:S(2)}) async-start(), calls=%async_computation.8 | async-start | bytes 3145728 | tf_op jit(solution)/shard_map/all_gather | solution.py:188
  85.1 116.5 %all-gather.13.cloned.1.call-start = ((), (), s32[]{:S(2)}) async-start(), calls=%async_computation.10 | async-start | bytes 2359296 | tf_op jit(solution)/shard_map/all_gather | solution.py:156
  85.9 414.3 %all-reduce.5.cloned.1.call-start = ((), (), s32[]{:S(2)}) async-start(), calls=%async_computation.11 | async-start | bytes 16777216 | tf_op jit(solution)/shard_map/psum | solution.py:195
  209.2 382.2 %all-gather.15.cloned.1.call-start = ((), (), s32[]{:S(2)}) async-start(), calls=%async_computation.12 | async-start | bytes 18874368 | tf_op jit(solution)/shard_map/all_gather | solution.py:157
  213.3 436.6 %all-gather.17.cloned.1.call-start = ((), (), s32[]{:S(2)}) async-start(), calls=%async_computation.13 | async-start | bytes 9437184 | tf_op jit(solution)/shard_map/all_gather | solution.py:158
  214.4 295.4 %copy-start.35 = (f32[1,2048]{1,0:T(1,128)S(1)}, f32[1,2048]{1,0:T(1,128)}, u32[]{:S(2)}) copy-start(f32[1,2048]{1,0:T(1,128)} %get-tuple-element.66) | copy-start | bytes 24580
  214.4 775.1 %all-reduce.9.cloned.1.call-start = ((), (), s32[]{:S(2)}) async-start(), calls=%async_computation.15 | async-start | bytes 16777216 | tf_op jit(solution)/shard_map/psum | solution.py:217
  698.6 448.0 %all-reduce.7.cloned.1.call-start = ((), (), s32[]{:S(2)}) async-start(), calls=%async_computation.14 | async-start | bytes 8388608 | tf_op jit(solution)/shard_map/psum | solution.py:204
  712.4 632.8 %reduce-scatter.10.cloned.1.call-start = ((), (), s32[]{:S(2)}) async-start(), calls=%async_computation.16 | async-start | bytes 6291456 | tf_op jit(solution)/shard_map/reduce_scatter | solution.py:227
  1286.1 110.1 %reduce-scatter.12.cloned.1.call-start = ((), (), s32[]{:S(2)}) async-start(), calls=%async_computation.17 | async-start | bytes 6291456 | tf_op jit(solution)/shard_map/reduce_scatter | solution.py:230
  1320.6 379.2 %all-reduce.11.cloned.1.call-start = ((), (), s32[]{:S(2)}) async-start(), calls=%async_computation.18 | async-start | bytes 16777216 | tf_op jit(solution)/shard_map/psum | solution.py:255
  1408.9 353.7 %reduce-scatter.16.cloned.1.call-start = ((), (), s32[]{:S(2)}) async-start(), calls=%async_computation.20 | async-start | bytes 4718592 | tf_op jit(solution)/shard_map/reduce_scatter | solution.py:261
  1417.8 456.7 %reduce-scatter.20.cloned.1.call-start = ((), (), s32[]{:S(2)}) async-start(), calls=%async_computation.22 | async-start | bytes 18874368 | tf_op jit(solution)/shard_map/reduce_scatter | solution.py:263
  1433.2 480.9 %reduce-scatter.22.cloned.1.call-start = ((), (), s32[]{:S(2)}) async-start(), calls=%async_computation.23 | async-start | bytes 1179648
  1450.4 255.5 %copy-start.42 = (f32[2048]{0:T(1024)S(1)}, f32[2048]{0:T(1024)}, u32[]{:S(2)}) copy-start(f32[2048]{0:T(1024)} %get-tuple-element.22) | copy-start | bytes 24580
  1707.3 303.2 %reduce-scatter.14.cloned.1.call-start = ((), (), s32[]{:S(2)}) async-start(), calls=%async_computation.19 | async-start | bytes 14155776 | tf_op jit(solution)/shard_map/reduce_scatter | solution.py:260
  1718.9 500.8 %reduce-scatter.18.cloned.1.call-start = ((), (), s32[]{:S(2)}) async-start(), calls=%async_computation.21 | async-start | bytes 37748736 | tf_op jit(solution)/shard_map/reduce_scatter | solution.py:262
  1762.6 111.9 %copy-start.14 = (f32[2048,256]{1,0:T(8,128)S(1)}, f32[2048,256]{1,0:T(8,128)}, u32[]{:S(2)}) copy-start(f32[2048,256]{1,0:T(8,128)} %param.24) | copy-start | bytes 6291460
  1766.7 114.5 %copy-start.43 = (f32[1024]{0:T(1024)S(1)}, f32[1024]{0:T(1024)}, u32[]{:S(2)}) copy-start(f32[1024]{0:T(1024)} %get-tuple-element.71) | copy-start | bytes 12292
  1881.2 129.3 %copy-start.17 = (f32[3,256,512]{2,1,0:T(8,128)S(1)}, f32[3,256,512]{2,1,0:T(8,128)}, u32[]{:S(2)}) copy-start(f32[3,256,512]{2,1,0:T(8,128)} %param.21) | copy-start | bytes 4718596
  1881.2 129.3 %copy-start.26 = (f32[3,256,512]{2,1,0:T(8,128)S(1)}, f32[3,256,512]{2,1,0:T(8,128)}, u32[]{:S(2)}) copy-start(f32[3,256,512]{2,1,0:T(8,128)} %param.26) | copy-start | bytes 4718596
  1915.1 100.3 %copy-start.44 = (f32[2,256]{1,0:T(2,128)}, f32[2,256]{1,0:T(2,128)S(1)}, u32[]{:S(2)}) copy-start(f32[2,256]{1,0:T(2,128)S(1)} %copy.53) | copy-start | bytes 6148
  (45 other events, 724.7 us)
Sparse Core Ops, SparseCore 0:
  10.5 48.2 all-gather.6
  78.9 33.1 all-gather.10
  114.1 33.1 all-gather.8
  149.6 28.1 all-gather.12
  209.3 290.8 all-reduce.4
  502.6 88.8 all-gather.14
  593.9 55.9 all-gather.16
  698.7 290.8 all-reduce.8
  992.5 153.9 all-reduce.6
  1286.2 53.2 reduce-scatter.9
  1341.8 54.3 reduce-scatter.11
  1409.0 290.7 all-reduce.10
  1704.1 50.3 reduce-scatter.15
  1758.5 115.9 reduce-scatter.19
  1878.1 35.9 reduce-scatter.21
  1918.1 92.3 reduce-scatter.13
  2014.5 205.2 reduce-scatter.17
where the time goes:
time: 2250 us; the launch traced here: 2240 us
  waiting for transfers between devices  1580 us (70%)
  matrix products  388 us (17%)
  other arithmetic  206 us (9%)
  local copies, waits for them, and re-layouts  27 us (1%)
    psum x1, waiting for transfers between devices, body(): middle = stream + lax.psum(attn_part, 'tp')  286 us
    psum x1, waiting for transfers between devices, body(): normed_two_grad = lax.psum(mlp_back_part, 'tp')  276 us
    psum x1, waiting for transfers between devices, body(): normed_one_grad = lax.psum(attn_back_part, 'tp')  249 us
    reduce_scatter x1, waiting for transfers between devices, body(): lax.psum_scatter(gate_up_grad_local, ('shard', 'ctx'), scatter_dimension=...  204 us
    psum x1, waiting for transfers between devices, body(): lax.psum(mlp_part.astype(jnp.bfloat16), 'tp').astype(jnp.float32)  149 us
    reduce_scatter x1, waiting for transfers between devices, body(): lax.psum_scatter(down_grad_local, ('shard', 'ctx'), scatter_dimension=1,...  108 us
    reduce_scatter x1, waiting for transfers between devices, body(): lax.psum_scatter(qkv_grad_local, ('shard', 'ctx'), scatter_dimension=1, t...  94.7 us
    all_gather x1, waiting for transfers between devices, body(): lax.all_gather(gate_up_low, ('shard', 'ctx'), axis=1, tiled=True)  78.9 us
  transfers between devices with their start and end apart: 17, of which 13 were waited for; matrix products, arithmetic and copies ran while one was open for 17% of the time, Pallas kernels for 0%

commit v1 on v0

--- a/solution.py
+++ b/solution.py
@@ -1,9 +1,227 @@
 import jax
 import jax.numpy as jnp
 from jax import lax
+from jax.experimental import pallas as pl
+from jax.experimental.pallas import tpu as pltpu
 from jax.sharding import PartitionSpec as P
 
 HEAD = 64
+PAIR = 128
+BLOCK = 256
+MASKED = -1e30
+
+
+def dot(left, right, contract):
+    return lax.dot_general(
+        left, right, ((contract[:1], contract[1:]), ((), ())), preferred_element_type=jnp.float32
+    )
+
+
+def one_head(values, head):
+    lane = lax.broadcasted_iota(jnp.int32, values.shape, 1)
+    return jnp.where((lane < HEAD) == (head == 0), values, jnp.zeros_like(values))
+
+
+def causal(scores):
+    key = lax.broadcasted_iota(jnp.int32, scores.shape, 0)
+    query = lax.broadcasted_iota(jnp.int32, scores.shape, 1)
+    return jnp.where(key <= query, scores, MASKED)
+
+
+def attend_kernel(info, q_ref, k_ref, v_ref, kp_ref, vp_ref, o_ref, l_ref):
+    block = q_ref.shape[0]
+    blocks = k_ref.shape[0] // block
+    step = pl.program_id(1)
+    late = info[0]
+    first_row = late * k_ref.shape[0] + step * block
+
+    def run(own, with_prev):
+        query = q_ref[...]
+        mixed = []
+        for head in range(2):
+            rows = one_head(query, head)
+            parts = []
+            if with_prev:
+                parts.append((dot(kp_ref[...], rows, (1, 1)), vp_ref[...]))
+            if own:
+                parts.append(
+                    (dot(k_ref[: own * block], rows, (1, 1)), v_ref[: own * block])
+                )
+            diag = pl.ds(own * block, block)
+            parts.append((causal(dot(k_ref[diag], rows, (1, 1))), v_ref[diag]))
+            peak = parts[0][0].max(0, keepdims=True)
+            for scores, _ in parts[1:]:
+                peak = jnp.maximum(peak, scores.max(0, keepdims=True))
+            expo = [jnp.exp(scores - peak) for scores, _ in parts]
+            denom = expo[0].sum(0, keepdims=True)
+            for e in expo[1:]:
+                denom = denom + e.sum(0, keepdims=True)
+            inverse = 1.0 / denom
+            total = None
+            for e, (_, value) in zip(expo, parts):
+                probs = (e * inverse).astype(jnp.bfloat16)
+                term = dot(value, probs, (0, 0))
+                total = term if total is None else total + term
+            mixed.append(total[head * HEAD : (head + 1) * HEAD])
+            index = first_row + lax.broadcasted_iota(jnp.int32, peak.shape, 1)
+            l_ref[0, head : head + 1, :] = jnp.where(index < info[1], peak + jnp.log(denom), -MASKED)
+        result = jnp.concatenate(mixed, 0).T
+        index = first_row + lax.broadcasted_iota(jnp.int32, result.shape, 0)
+        own_value = v_ref[pl.ds(own * block, block)].astype(jnp.float32)
+        o_ref[...] = jnp.where(index < info[1], result, own_value).astype(jnp.bfloat16)
+
+    for own in range(blocks):
+        for with_prev in (False, True):
+            pl.when((step == own) & (late == int(with_prev)))(
+                lambda own=own, with_prev=with_prev: run(own, with_prev)
+            )
+
+
+def attend_forward(info, query, keys, values, keys_prev, values_prev):
+    rows, width = query.shape
+    block = min(BLOCK, rows)
+    pairs = width // PAIR
+    part = pl.BlockSpec((block, PAIR), lambda p, i, info: (i, p))
+    whole = pl.BlockSpec((rows, PAIR), lambda p, i, info: (0, p))
+    return pl.pallas_call(
+        attend_kernel,
+        out_shape=(
+            jax.ShapeDtypeStruct((rows, width), jnp.bfloat16),
+            jax.ShapeDtypeStruct((pairs, 2, rows), jnp.float32),
+        ),
+        grid_spec=pltpu.PrefetchScalarGridSpec(
+            num_scalar_prefetch=1,
+            grid=(pairs, rows // block),
+            in_specs=[part, whole, whole, whole, whole],
+            out_specs=[part, pl.BlockSpec((1, 2, block), lambda p, i, info: (p, 0, i))],
+        ),
+        compiler_params=pltpu.CompilerParams(vmem_limit_bytes=48 * 2**20),
+        cost_estimate=pl.CostEstimate(
+            flops=rows * rows * width * 6, bytes_accessed=8 * rows * width * 2,
+            transcendentals=rows * rows * width // HEAD,
+        ),
+        name="attend_forward",
+    )(info, query, keys, values, keys_prev, values_prev)
+
+
+def rotate_lanes(values, cosine, sine):
+    lane = lax.broadcasted_iota(jnp.int32, values.shape, 1) % HEAD
+    width = values.shape[1]
+    ahead = pltpu.roll(values, width - HEAD // 2, 1)
+    behind = pltpu.roll(values, HEAD // 2, 1)
+    return values * cosine + jnp.where(lane < HEAD // 2, -ahead, behind) * sine
+
+
+def attend_back_kernel(
+    info, q_ref, k_ref, v_ref, kp_ref, vp_ref, o_ref, do_ref, l_ref, cos_ref, sin_ref,
+    dq_ref, dk_ref, dv_ref, dkp_ref, dvp_ref, dkp_acc, dvp_acc,
+):
+    block = q_ref.shape[0]
+    blocks = k_ref.shape[0] // block
+    step = pl.program_id(1)
+    late = info[0]
+    first_row = late * k_ref.shape[0] + step * block
+
+    @pl.when(step == 0)
+    def _():
+        dk_ref[...] = jnp.zeros_like(dk_ref)
+        dv_ref[...] = jnp.zeros_like(dv_ref)
+        dkp_acc[...] = jnp.zeros_like(dkp_acc)
+        dvp_acc[...] = jnp.zeros_like(dvp_acc)
+
+    query = q_ref[...]
+    upstream = do_ref[...]
+    product = (upstream.astype(jnp.float32) * o_ref[...].astype(jnp.float32)).T
+    queries = [one_head(query, head) for head in range(2)]
+    upstreams = [one_head(upstream, head) for head in range(2)]
+    inner = [product[head * HEAD : (head + 1) * HEAD].sum(0, keepdims=True) for head in range(2)]
+    totals = [l_ref[0, head : head + 1, :] for head in range(2)]
+    query_both = jnp.concatenate(queries, 0)
+    upstream_both = jnp.concatenate(upstreams, 0)
+
+    def tile(keys, values, masked):
+        grads, probs_all, out = [], [], []
+        for head in range(2):
+            scores = dot(keys, queries[head], (1, 1))
+            if masked:
+                scores = causal(scores)
+            probs = jnp.exp(scores - totals[head])
+            prob_grad = dot(values, upstreams[head], (1, 1))
+            score_grad = (probs * (prob_grad - inner[head])).astype(jnp.bfloat16)
+            probs_all.append(probs.astype(jnp.bfloat16))
+            grads.append(score_grad)
+            out.append(dot(keys, score_grad, (0, 0))[head * HEAD : (head + 1) * HEAD])
+        key_grad = dot(jnp.concatenate(grads, 1), query_both, (1, 0))
+        value_grad = dot(jnp.concatenate(probs_all, 1), upstream_both, (1, 0))
+        return jnp.concatenate(out, 0), key_grad, value_grad
+
+    def run(own, with_prev):
+        diag = pl.ds(own * block, block)
+        query_grad, key_grad, value_grad = tile(k_ref[diag], v_ref[diag], True)
+        index = first_row + lax.broadcasted_iota(jnp.int32, upstream.shape, 0)
+        dk_ref[diag] += key_grad
+        dv_ref[diag] += value_grad + jnp.where(
+            index < info[1], 0.0, upstream.astype(jnp.float32)
+        )
+        for at in range(own):
+            here = pl.ds(at * block, block)
+            more, key_grad, value_grad = tile(k_ref[here], v_ref[here], False)
+            query_grad += more
+            dk_ref[here] += key_grad
+            dv_ref[here] += value_grad
+        if with_prev:
+            for at in range(blocks):
+                here = pl.ds(at * block, block)
+                more, key_grad, value_grad = tile(kp_ref[here], vp_ref[here], False)
+                query_grad += more
+                dkp_acc[here] += key_grad
+                dvp_acc[here] += value_grad
+        grad = rotate_lanes(query_grad.T * 0.125, cos_ref[...], -sin_ref[...])
+        dq_ref[...] = grad.astype(jnp.bfloat16)
+
+    for own in range(blocks):
+        for with_prev in (False, True):
+            pl.when((step == own) & (late == int(with_prev)))(
+                lambda own=own, with_prev=with_prev: run(own, with_prev)
+            )
+
+    @pl.when(step == blocks - 1)
+    def _():
+        dkp_ref[...] = dkp_acc[...].astype(jnp.bfloat16)
+        dvp_ref[...] = dvp_acc[...].astype(jnp.bfloat16)
+
+
+def attend_back(info, query, keys, values, keys_prev, values_prev, mixed, upstream, totals, cosine, sine):
+    rows, width = query.shape
+    block = min(BLOCK, rows)
+    pairs = width // PAIR
+    part = pl.BlockSpec((block, PAIR), lambda p, i, info: (i, p))
+    whole = pl.BlockSpec((rows, PAIR), lambda p, i, info: (0, p))
+    table = pl.BlockSpec((block, PAIR), lambda p, i, info: (i, 0))
+    return pl.pallas_call(
+        attend_back_kernel,
+        out_shape=(
+            jax.ShapeDtypeStruct((rows, width), jnp.bfloat16),
+            jax.ShapeDtypeStruct((rows, width), jnp.float32),
+            jax.ShapeDtypeStruct((rows, width), jnp.float32),
+            jax.ShapeDtypeStruct((rows, width), jnp.bfloat16),
+            jax.ShapeDtypeStruct((rows, width), jnp.bfloat16),
+        ),
+        grid_spec=pltpu.PrefetchScalarGridSpec(
+            num_scalar_prefetch=1,
+            grid=(pairs, rows // block),
+            in_specs=[part, whole, whole, whole, whole, part, part,
+                      pl.BlockSpec((1, 2, block), lambda p, i, info: (p, 0, i)), table, table],
+            out_specs=[part, whole, whole, whole, whole],
+            scratch_shapes=[pltpu.VMEM((rows, PAIR), jnp.float32)] * 2,
+        ),
+        compiler_params=pltpu.CompilerParams(vmem_limit_bytes=48 * 2**20),
+        cost_estimate=pl.CostEstimate(
+            flops=rows * rows * width * 15, bytes_accessed=16 * rows * width * 2,
+            transcendentals=rows * rows * width // HEAD,
+        ),
+        name="attend_back",
+    )(info, query, keys, values, keys_prev, values_prev, mixed, upstream, totals, cosine, sine)
 
 
 norm_eps = 1e-05
@@ -23,12 +241,6 @@
     return (jnp.cos(angle)[:, None, :], jnp.sin(angle)[:, None, :])
 
 
-def rotate(values, cosine, sine):
-    half = values.shape[-1] // 2
-    first, second = (values[..., :half], values[..., half:])
-    return jnp.concatenate([first * cosine - second * sine, second * cosine + first * sine], -1)
-
-
 def outer_sum(left, right):
     return lax.dot_general(
         left, right, (((0,), (0,)), ((), ())), preferred_element_type=jnp.float32
@@ -55,56 +267,10 @@
     return (stream_grad, gain_grad)
 
 
-def block_scores(rows_query, keys, key_mask):
-    scores = (
-        jnp.einsum("qhd,khd->hqk", rows_query, keys, preferred_element_type=jnp.float32) * 0.125
-    )
-    return jnp.where(key_mask[None], scores, -1e30)
-
-
-def attend_forward(query, keys, values, key_mask, block):
-    outputs = []
-    totals = []
-    for begin in range(0, query.shape[0], block):
-        scores = block_scores(query[begin : begin + block], keys, key_mask[begin : begin + block])
-        peak = jnp.max(scores, axis=-1, keepdims=True)
-        expo = jnp.exp(scores - peak)
-        denom = jnp.sum(expo, axis=-1, keepdims=True)
-        probs = (expo / denom).astype(jnp.bfloat16)
-        outputs.append(
-            jnp.einsum("hqk,khd->qhd", probs, values, preferred_element_type=jnp.float32)
-        )
-        totals.append(peak + jnp.log(denom))
-    return (jnp.concatenate(outputs, 0), jnp.concatenate(totals, 1))
-
-
-def attend_back(query, keys, values, key_mask, totals, upstream, block):
-    query_grads = []
-    key_grad = jnp.zeros(keys.shape, jnp.float32)
-    value_grad = jnp.zeros(values.shape, jnp.float32)
-    for begin in range(0, query.shape[0], block):
-        rows_query = query[begin : begin + block]
-        rows_grad = upstream[begin : begin + block]
-        scores = block_scores(rows_query, keys, key_mask[begin : begin + block])
-        probs = jnp.exp(scores - totals[:, begin : begin + block])
-        probs_low = probs.astype(jnp.bfloat16)
-        prob_grad = jnp.einsum(
-            "qhd,khd->hqk", rows_grad, values, preferred_element_type=jnp.float32
-        )
-        inner = jnp.sum(prob_grad * probs, axis=-1, keepdims=True)
-        score_grad = (probs * (prob_grad - inner)).astype(jnp.bfloat16)
-        query_grads.append(
-            jnp.einsum("hqk,khd->qhd", score_grad, keys, preferred_element_type=jnp.float32) * 0.125
-        )
-        key_grad = (
-            key_grad
-            + jnp.einsum("hqk,qhd->khd", score_grad, rows_query, preferred_element_type=jnp.float32)
-            * 0.125
-        )
-        value_grad = value_grad + jnp.einsum(
-            "hqk,qhd->khd", probs_low, rows_grad, preferred_element_type=jnp.float32
-        )
-    return (jnp.concatenate(query_grads, 0), key_grad, value_grad)
+def scatter_low(grad):
+    return lax.psum_scatter(
+        grad.astype(jnp.bfloat16), ("shard", "ctx"), scatter_dimension=1, tiled=True
+    ).astype(jnp.float32)
 
 
 def adam_update(weight, first, second, grad, decay):
@@ -137,15 +303,11 @@
     gains_second,
 ):
     row_count = tokens.shape[0]
-    group_rows = row_count * lax.axis_size("ctx")
     live = lengths[0]
     offset = lax.axis_index("ctx") * row_count
     query_index = offset + jnp.arange(row_count, dtype=jnp.int32)
-    key_index = jnp.arange(group_rows, dtype=jnp.int32)
-    key_mask = (key_index[None, :] <= query_index[:, None]) & (
-        (query_index[:, None] < live) | (key_index[None, :] == query_index[:, None])
-    )
-    block = min(512, row_count)
+    late = lax.axis_index("ctx")
+    info = jnp.stack([late.astype(jnp.int32), live])
     qkv_low = qkv_weight.astype(jnp.bfloat16)
     out_low = out_weight.astype(jnp.bfloat16)
     gate_up_low = gate_up_weight.astype(jnp.bfloat16)
@@ -163,36 +325,28 @@
     stream = tokens.astype(jnp.float32)
     normed_one, scale_one = normalize(stream, gain_one)
     cosine, sine = rotation(query_index, HEAD)
+    cosine, sine = (jnp.concatenate([c[:, 0]] * 4, 1) for c in (cosine, sine))
     local_width = qkv_full.shape[2]
-    heads_local = local_width // HEAD
-    shape3 = (row_count, heads_local, HEAD)
-    query = rotate(
-        jnp.dot(normed_one, qkv_full[0], preferred_element_type=jnp.float32).reshape(shape3),
-        cosine,
-        sine,
-    ).astype(jnp.bfloat16)
-    keys_own = (
-        rotate(
-            jnp.dot(normed_one, qkv_full[1], preferred_element_type=jnp.float32).reshape(shape3),
-            cosine,
-            sine,
-        )
-        .astype(jnp.bfloat16)
-        .reshape(row_count, local_width)
-    )
-    values_own = jnp.dot(normed_one, qkv_full[2], preferred_element_type=jnp.float32).astype(
-        jnp.bfloat16
-    )
-    keys_all, values_all = (
-        lax.all_gather(keys_own, "ctx", axis=0, tiled=True),
-        lax.all_gather(values_own, "ctx", axis=0, tiled=True),
-    )
-    keys_all = keys_all.reshape(group_rows, heads_local, HEAD)
-    values_all = values_all.reshape(group_rows, heads_local, HEAD)
-    mixed, totals = attend_forward(query, keys_all, values_all, key_mask, block)
-    mixed_low = mixed.reshape(row_count, local_width).astype(jnp.bfloat16)
+    wide = lambda table: jnp.concatenate([table] * (local_width // PAIR), 1)
+    cos_wide, sin_wide = wide(cosine), wide(sine)
+
+    def rotate_wide(values, sine_wide):
+        lane = lax.broadcasted_iota(jnp.int32, values.shape, 1) % HEAD
+        half = HEAD // 2
+        ahead = jnp.roll(values, -half, 1)
+        behind = jnp.roll(values, half, 1)
+        return values * cos_wide + jnp.where(lane < half, -ahead, behind) * sine_wide
+
+    products = [
+        jnp.dot(normed_one, qkv_full[i], preferred_element_type=jnp.float32) for i in range(3)
+    ]
+    query = (rotate_wide(products[0], sin_wide) * 0.125).astype(jnp.bfloat16)
+    keys_own = rotate_wide(products[1], sin_wide).astype(jnp.bfloat16)
+    values_own = products[2].astype(jnp.bfloat16)
+    keys_prev, values_prev = (lax.ppermute(a, "ctx", [(0, 1)]) for a in (keys_own, values_own))
+    mixed_low, totals = attend_forward(info, query, keys_own, values_own, keys_prev, values_prev)
     attn_part = jnp.dot(mixed_low, out_full, preferred_element_type=jnp.float32)
-    middle = stream + lax.psum(attn_part, "tp")
+    middle = stream + lax.psum(attn_part.astype(jnp.bfloat16), "tp").astype(jnp.float32)
     normed_two, scale_two = normalize(middle, gain_two)
     gate = jnp.dot(normed_two, gate_up_full[0], preferred_element_type=jnp.float32)
     upward = jnp.dot(normed_two, gate_up_full[1], preferred_element_type=jnp.float32)
@@ -214,32 +368,22 @@
         [outer_sum(normed_two, gate_grad), outer_sum(normed_two, upward_grad)]
     )
     mlp_back_part = back_dot(gate_grad, gate_up_use[0]) + back_dot(upward_grad, gate_up_use[1])
-    normed_two_grad = lax.psum(mlp_back_part, "tp")
+    normed_two_grad = lax.psum(mlp_back_part.astype(jnp.bfloat16), "tp").astype(jnp.float32)
     middle_norm_grad, gain_two_grad = normalize_back(middle, scale_two, gain_two, normed_two_grad)
     middle_grad = upstream + middle_norm_grad
     middle_low = middle_grad.astype(jnp.bfloat16)
     out_grad_local = outer_sum(mixed_low, middle_low)
-    mixed_grad = back_dot(middle_low, out_use).astype(jnp.bfloat16).reshape(shape3)
-    query_grad, key_grad, value_grad = attend_back(
-        query, keys_all, values_all, key_mask, totals, mixed_grad, block
-    )
-    key_own_grad, value_own_grad = (
-        lax.psum_scatter(
-            key_grad.reshape(group_rows, local_width), "ctx", scatter_dimension=0, tiled=True
-        ),
-        lax.psum_scatter(
-            value_grad.reshape(group_rows, local_width), "ctx", scatter_dimension=0, tiled=True
-        ),
-    )
-    query_low = (
-        rotate(query_grad, cosine, -sine).reshape(row_count, local_width).astype(jnp.bfloat16)
-    )
-    key_low = (
-        rotate(key_own_grad.reshape(shape3), cosine, -sine)
-        .reshape(row_count, local_width)
-        .astype(jnp.bfloat16)
-    )
-    value_low = value_own_grad.astype(jnp.bfloat16)
+    mixed_grad = back_dot(middle_low, out_use).astype(jnp.bfloat16)
+    query_low, key_grad, value_grad, key_prev_grad, value_prev_grad = attend_back(
+        info, query, keys_own, values_own, keys_prev, values_prev, mixed_low, mixed_grad,
+        totals, cosine, sine,
+    )
+    key_more, value_more = (
+        lax.ppermute(a, "ctx", [(1, 0)]).astype(jnp.float32)
+        for a in (key_prev_grad, value_prev_grad)
+    )
+    key_low = rotate_wide(key_grad + key_more, -sin_wide).astype(jnp.bfloat16)
+    value_low = (value_grad + value_more).astype(jnp.bfloat16)
     qkv_grad_local = jnp.stack(
         [
             outer_sum(normed_one, query_low),
@@ -252,15 +396,15 @@
         + back_dot(key_low, qkv_use[1])
         + back_dot(value_low, qkv_use[2])
     )
-    normed_one_grad = lax.psum(attn_back_part, "tp")
+    normed_one_grad = lax.psum(attn_back_part.astype(jnp.bfloat16), "tp").astype(jnp.float32)
     stream_grad, gain_one_grad = normalize_back(stream, scale_one, gain_one, normed_one_grad)
     input_grad = (middle_grad + stream_grad).astype(jnp.bfloat16)
     gains_local = jnp.stack([gain_one_grad, gain_two_grad])
     qkv_grad, out_grad, gate_up_grad, down_grad, gains_grad = (
-        lax.psum_scatter(qkv_grad_local, ("shard", "ctx"), scatter_dimension=1, tiled=True),
-        lax.psum_scatter(out_grad_local, ("shard", "ctx"), scatter_dimension=1, tiled=True),
-        lax.psum_scatter(gate_up_grad_local, ("shard", "ctx"), scatter_dimension=1, tiled=True),
-        lax.psum_scatter(down_grad_local, ("shard", "ctx"), scatter_dimension=1, tiled=True),
+        scatter_low(qkv_grad_local),
+        scatter_low(out_grad_local),
+        scatter_low(gate_up_grad_local),
+        scatter_low(down_grad_local),
         lax.psum_scatter(gains_local, ("shard", "ctx"), scatter_dimension=1, tiled=True),
     )
     qkv_step, qkv_first_new, qkv_second_new = adam_update(

time: 2250 us -> 1490 us (0.66)
  waiting for transfers between devices: 1580 us -> 1070 us
  matrix products: 388 us -> 188 us
  other arithmetic: 206 us -> 96.5 us
  Pallas kernels: 0 us -> 57.4 us
    psum x3 -> x2, waiting for transfers between devices: 812 us -> 320 us  [the longest x1 167 us: body(): lax.psum(attn_part.astype(jnp.bfloat16), 'tp').astype(jnp.float32)]
    reduce_scatter x6 -> x4, waiting for transfers between devices: 440 us -> 252 us  [scatter_low(): lax.psum_scatter(grad.astype(jnp.bfloat16), ('shard', 'ctx'), scatter_dim...]
    dot_general x15 -> x3, matrix products: 197 us -> 13.4 us  [body(): jnp.dot(normed_one, qkv_full[i], preferred_element_type=jnp.float32)]
    psum x1, waiting for transfers between devices: 149 us -> 251 us  [body(): lax.psum(mlp_part.astype(jnp.bfloat16), 'tp').astype(jnp.float32)]
    ppermute x0 -> x4, waiting for transfers between devices: none -> 99.1 us  [the longest x2 54.9 us: body(): lax.ppermute(a, 'ctx', [(1, 0)]).astype(jnp.float32)]
    pallas_call x0 -> x2, Pallas kernels: none -> 57.4 us  [the longest x1 35.4 us: attend_back(): pl.pallas_call(attend_back_kernel, out_shape=(jax.ShapeDtypeStruct((rows,...]
    convert_element_type x4 -> x3, other arithmetic: 55.9 us -> 5.55 us  [the longest x1 3.96 us: body(): keys_own = rotate_wide(products[1], sin_wide).astype(jnp.bfloat16)]
    reduce_sum x2 -> x0, other arithmetic: 27.4 us -> none  [attend_forward(): denom = jnp.sum(expo, axis=-1, keepdims=True)]
  transfers between devices with their start and end apart: 17 -> 16, of which waited for: 13 -> 15; matrix products, arithmetic and copies ran while one was open for 17% -> 14% of each run, Pallas kernels for 0% -> 1%
where the time goes in v1:
time: 1490 us; the launch traced here: 1480 us
  waiting for transfers between devices  1070 us (72%)
  matrix products  188 us (13%)
  other arithmetic  96.5 us (6%)
  Pallas kernels  57.4 us (4%)
  local copies, waits for them, and re-layouts  31 us (2%)
  between operations  16 us (1%)
    reduce_scatter x4, waiting for transfers between devices, scatter_low(): lax.psum_scatter(grad.astype(jnp.bfloat16), ('shard', 'ctx'), scatter_dim...  252 us
    psum x1, waiting for transfers between devices, body(): lax.psum(mlp_part.astype(jnp.bfloat16), 'tp').astype(jnp.float32)  251 us
    psum x1, waiting for transfers between devices, body(): lax.psum(attn_part.astype(jnp.bfloat16), 'tp').astype(jnp.float32)  167 us
    psum x1, waiting for transfers between devices, body(): lax.psum(mlp_back_part.astype(jnp.bfloat16), 'tp').astype(jnp.float32)  153 us
    all_gather x1, waiting for transfers between devices, body(): lax.all_gather(gate_up_low, ('shard', 'ctx'), axis=1, tiled=True)  81.5 us
    dot_general x7, matrix products, back_dot(): lax.dot_general(grad, weight, (((1,), (1,)), ((), ())), preferred_element...  71.2 us
    dot_general x7, matrix products, outer_sum(): lax.dot_general(left, right, (((0,), (0,)), ((), ())), preferred_element_...  58.8 us
    ppermute x2, waiting for transfers between devices, body(): lax.ppermute(a, 'ctx', [(1, 0)]).astype(jnp.float32)  54.9 us
  transfers between devices with their start and end apart: 16, of which 15 were waited for; matrix products, arithmetic and copies ran while one was open for 14% of the time, Pallas kernels for 1%

profile of v1, /device:TPU:0, one launch (start us, length us, event | category | flops | bytes accessed | tf_op | source)
XLA Modules:
  0.0 1484.6 jit_solution(7282717678466331716)
XLA Ops:
  11.7 14.5 all_gather.15
  44.4 14.4 all-gather.5.cloned.1.call-done
  86.0 22.0 %collective-permute-done.kp_ref = bf16[1024,512]{1,0:T(8,128)(2,1)S(1)} collective-permute-done((bf16[1024,512]{1,0:T(8,128)(2,1)S(1)}, bf16[1024,512]{1,0:T(8,128)(2,1)S(1)}, u32[]{:S(2)}, u32[]{:S(2)}) %collective-permute-start) | collective-permute-done | bytes 1048608 | tf_op jit(solution)/shard_map/ppermute | solution.py:346
  108.0 22.2 %collective-permute-done.1.vp_ref = bf16[1024,512]{1,0:T(8,128)(2,1)S(1)} collective-permute-done((bf16[1024,512]{1,0:T(8,128)(2,1)S(1)}, bf16[1024,512]{1,0:T(8,128)(2,1)S(1)}, u32[]{:S(2)}, u32[]{:S(2)}) %collective-permute-start.1) | collective-permute-done | bytes 1048608 | tf_op jit(solution)/shard_map/ppermute | solution.py:346
  131.2 22.0 %attend_forward.1 = (bf16[1024,512]{1,0:T(8,128)(2,1)S(1)}, f32[4,2,1024]{2,1,0:T(2,128)S(1)}) custom-call(s32[2]{0:T(128)S(1)} %pad_add_fusion.info, bf16[1024,512]{1,0:T(8,128)(2,1)S(1)} %get-tuple-element.65.q_ref, bf16[1024,512]{1,0:T(8,128)(2,1)S(1)} %get-tuple-element.64.k_ref, bf16[1024,512]{1,0:T(8,128)(2,1)S(1)} %fusion.49.v_ref, ...), custom_call_target="tpu_custom_call" | custom-call | flops 3221225472 | bytes 8388608 | tf_op jit(solution)/shard_map/attend_forward/pallas_call | solution.py:86
  166.8 166.9 %all-reduce.5.cloned.1.call-done = bf16[1024,2048]{1,0:T(8,128)(2,1)} async-done(((bf16[1024,2048]{1,0:T(8,128)(2,1)}), bf16[1024,2048]{1,0:T(8,128)(2,1)}) %all-reduce.5.cloned.1.call-update) | async-done | bytes 4194320 | tf_op jit(solution)/shard_map/psum | solution.py:349
  343.7 81.5 %all-gather.9.cloned.1.call-done = bf16[2,2048,2048]{2,1,0:T(8,128)(2,1)} async-done(((bf16[2,256,2048]{2,1,0:T(8,128)(2,1)}), bf16[2,2048,2048]{2,1,0:T(8,128)(2,1)}) %all-gather.9.cloned.1.call-update) | async-done | bytes 16777232 | tf_op jit(solution)/shard_map/all_gather | solution.py:319
  425.2 15.4 %fusion.18 = f32[1024,2048]{1,0:T(8,128)} fusion(bf16[1024,2048]{1,0:T(8,128)(2,1)} %multiply_convert_fusion.3, bf16[2,2048,2048]{2,1,0:T(8,128)(2,1)} %all-gather.9.cloned.1.call-done), kind=kOutput, calls=%fused_computation.44 | convolution fusion | flops 8589934592 | bytes 20971520 | tf_op jit(solution)/shard_map/dot_general | solution.py:351
  440.5 11.0 fusion.20
  451.5 32.1 %all-gather.11.cloned.1.call-done = bf16[2048,2048]{1,0:T(8,128)(2,1)} async-done(((bf16[2048,256]{1,0:T(8,128)(2,1)}), bf16[2048,2048]{1,0:T(8,128)(2,1)}) %all-gather.11.cloned.1.call-update) | async-done | bytes 8388624 | tf_op jit(solution)/shard_map/all_gather | solution.py:320
  483.6 22.0 %multiply_convert_fusion = (bf16[1024,2048]{1,0:T(8,128)(2,1)}, bf16[1024,2048]{1,0:T(8,128)(2,1)}, bf16[1024,2048]{1,0:T(8,128)(2,1)}) fusion(f32[1024,2048]{1,0:T(8,128)} %fusion.18, f32[1024,2048]{1,0:T(8,128)} %fusion.20, bf16[1024,2048]{1,0:T(8,128)(2,1)} %param.19, bf16[2048,2048]{1,0:T(8,128)(2,1)} %all-gather.11.cloned.1.call-done), kind=kOutput, calls=%fused_computation.34 | convolution fusion | flops 8621391872 | bytes 41943040 | tf_op jit(solution)/shard_map/dot_general | solution.py:251
  505.6 12.7 fusion.17
  518.4 12.8 add_convert_fusion.1
  533.3 153.1 %all-reduce.7.cloned.1.call-done = bf16[1024,2048]{1,0:T(8,128)(2,1)} async-done(((bf16[1024,2048]{1,0:T(8,128)(2,1)}), bf16[1024,2048]{1,0:T(8,128)(2,1)}) %all-reduce.7.cloned.1.call-update) | async-done | bytes 4194320 | tf_op jit(solution)/shard_map/psum | solution.py:371
  704.4 35.4 %attend_back.1 = (bf16[1024,512]{1,0:T(8,128)(2,1)S(1)}, f32[1024,512]{1,0:T(8,128)}, f32[1024,512]{1,0:T(8,128)}, bf16[1024,512]{1,0:T(8,128)(2,1)S(1)}, bf16[1024,512]{1,0:T(8,128)(2,1)S(1)}) custom-call(s32[2]{0:T(128)S(1)} %pad_add_fusion.info, bf16[1024,512]{1,0:T(8,128)(2,1)S(1)} %get-tuple-element.65.q_ref, bf16[1024,512]{1,0:T(8,128)(2,1)} %copy-done, ...), custom_call_target="tpu_custom_call" | custom-call | flops 8053063680 | bytes 16777216 | tf_op jit(solution)/shard_map/attend_back/pallas_call | solution.py:201
  741.2 11.9 convolution_convert_fusion.1
  758.5 45.2 %collective-permute-done.2 = bf16[1024,512]{1,0:T(8,128)(2,1)S(1)} collective-permute-done((bf16[1024,512]{1,0:T(8,128)(2,1)S(1)}, bf16[1024,512]{1,0:T(8,128)(2,1)S(1)}, u32[]{:S(2)}, u32[]{:S(2)}) %collective-permute-start.2) | collective-permute-done | bytes 1048608 | tf_op jit(solution)/shard_map/ppermute | solution.py:382
  842.9 14.0 convolution_convert_fusion
  872.4 251.3 %all-reduce.9.cloned.1.call-done = (bf16[1024,2048]{1,0:T(8,128)(2,1)}, bf16[1024,2048]{1,0:T(8,128)(2,1)}) async-done(((bf16[1024,2048]{1,0:T(8,128)(2,1)}, bf16[1024,2048]{1,0:T(8,128)(2,1)}), (bf16[1024,2048]{1,0:T(8,128)(2,1)}, bf16[1024,2048]{1,0:T(8,128)(2,1)})) %all-reduce.9.cloned.1.call-update) | async-done | bytes 8388624 | tf_op jit(solution)/shard_map/psum | solution.py:358
  1137.0 12.5 convert_bitcast_fusion
  1169.8 72.6 %reduce-scatter.14.cloned.1.call-done = bf16[2048,256]{1,0:T(8,128)(2,1)} async-done(((bf16[2048,2048]{1,0:T(8,128)(2,1)}), bf16[2048,256]{1,0:T(8,128)(2,1)}) %reduce-scatter.14.cloned.1.call-update) | async-done | bytes 1048592 | tf_op jit(solution)/shard_map/reduce_scatter | solution.py:271
  1260.9 21.2 %reduce-scatter.16.cloned.1.call-done = f32[256,2]{1,0:T(8,128)} async-done(((f32[2048,2]{1,0:T(8,128)}), f32[256,2]{1,0:T(8,128)}) %reduce-scatter.16.cloned.1.call-update) | async-done | bytes 2064
  1283.7 63.5 %reduce-scatter.8.cloned.1.call-done = bf16[3,256,512]{2,1,0:T(8,128)(2,1)} async-done(((bf16[3,2048,512]{2,1,0:T(8,128)(2,1)}), bf16[3,256,512]{2,1,0:T(8,128)(2,1)}) %reduce-scatter.8.cloned.1.call-update) | async-done | bytes 786448 | tf_op jit(solution)/shard_map/reduce_scatter | solution.py:271
  1352.1 115.0 %reduce-scatter.12.cloned.1.call-done = bf16[2,256,2048]{2,1,0:T(8,128)(2,1)} async-done(((bf16[2,2048,2048]{2,1,0:T(8,128)(2,1)}), bf16[2,256,2048]{2,1,0:T(8,128)(2,1)}) %reduce-scatter.12.cloned.1.call-update) | async-done | bytes 2097168 | tf_op jit(solution)/shard_map/reduce_scatter | solution.py:271
  (208 shorter events, 223.4 us)
Async XLA Ops:
  7.2 51.6 %all-gather.5.cloned.1.call-start = ((), (), s32[]{:S(2)}) async-start(), calls=%async_computation.5 | async-start | bytes 7077888 | tf_op jit(solution)/shard_map/all_gather | solution.py:317
  9.7 145.5 %all-gather.7.cloned.1.call-start = ((), (), s32[]{:S(2)}) async-start(), calls=%async_computation.6 | async-start | bytes 2359296 | tf_op jit(solution)/shard_map/all_gather | solution.py:318
  11.5 322.2 %all-reduce.5.cloned.1.call-start = ((), (), s32[]{:S(2)}) async-start(), calls=%async_computation.7 | async-start | bytes 8388608 | tf_op jit(solution)/shard_map/psum | solution.py:349
  11.6 60.7 %copy-start.42 = (s32[512]{0:T(512)}, s32[512]{0:T(512)S(1)}, u32[]{:S(2)}) copy-start(s32[512]{0:T(512)S(1)} %get-tuple-element.90) | copy-start | bytes 6148
  11.6 60.7 %copy-start.44 = (s32[512]{0:T(512)}, s32[512]{0:T(512)S(1)}, u32[]{:S(2)}) copy-start(s32[512]{0:T(512)S(1)} %get-tuple-element.91) | copy-start | bytes 6148
  11.6 60.6 %copy-start.50 = (pred[512]{0:T(512)(128)(4,1)}, pred[512]{0:T(512)(128)(4,1)S(1)}, u32[]{:S(2)}) copy-start(pred[512]{0:T(512)(128)(4,1)S(1)} %fusion.60) | copy-start | bytes 1540
  76.3 31.7 %collective-permute-start = (bf16[1024,512]{1,0:T(8,128)(2,1)S(1)}, bf16[1024,512]{1,0:T(8,128)(2,1)S(1)}, u32[]{:S(2)}, u32[]{:S(2)}) collective-permute-start(bf16[1024,512]{1,0:T(8,128)(2,1)S(1)} %get-tuple-element.64.k_ref), channel_id=1, source_target_pairs={{0,4},{1,5},{2,6},{3,7},{8,12},{9,13},{10,14},{11,15},{16,20},{17,... | collective-permute-start | bytes 3145736 | tf_op jit(solution)/shard_map/ppermute | solution.py:346
  83.9 46.4 %collective-permute-start.1 = (bf16[1024,512]{1,0:T(8,128)(2,1)S(1)}, bf16[1024,512]{1,0:T(8,128)(2,1)S(1)}, u32[]{:S(2)}, u32[]{:S(2)}) collective-permute-start(bf16[1024,512]{1,0:T(8,128)(2,1)S(1)} %fusion.49.v_ref), channel_id=1, source_target_pairs={{0,4},{1,5},{2,6},{3,7},{8,12},{9,13},{10,14},{11,15},{16,20},{17,... | collective-permute-start | bytes 3145736 | tf_op jit(solution)/shard_map/ppermute | solution.py:346
  161.5 263.6 %all-gather.9.cloned.1.call-start = ((), (), s32[]{:S(2)}) async-start(), calls=%async_computation.8 | async-start | bytes 18874368 | tf_op jit(solution)/shard_map/all_gather | solution.py:319
  165.6 318.0 %all-gather.11.cloned.1.call-start = ((), (), s32[]{:S(2)}) async-start(), calls=%async_computation.9 | async-start | bytes 9437184 | tf_op jit(solution)/shard_map/all_gather | solution.py:320
  166.7 519.6 %all-reduce.7.cloned.1.call-start = ((), (), s32[]{:S(2)}) async-start(), calls=%async_computation.10 | async-start | bytes 8388608 | tf_op jit(solution)/shard_map/psum | solution.py:371
  531.2 592.5 %all-reduce.9.cloned.1.call-start = ((), (), s32[]{:S(2)}) async-start(), calls=%async_computation.16 | async-start | bytes 16777216 | tf_op jit(solution)/shard_map/psum | solution.py:358
  739.9 63.9 %collective-permute-start.2 = (bf16[1024,512]{1,0:T(8,128)(2,1)S(1)}, bf16[1024,512]{1,0:T(8,128)(2,1)S(1)}, u32[]{:S(2)}, u32[]{:S(2)}) collective-permute-start(bf16[1024,512]{1,0:T(8,128)(2,1)S(1)} %get-tuple-element.33), channel_id=1, source_target_pairs={{4,0},{5,1},{6,2},{7,3},{12,8},{13,9},{14,10},{15,11},{20,16},{21,... | collective-permute-start | bytes 3145736 | tf_op jit(solution)/shard_map/ppermute | solution.py:382
  753.1 72.2 %collective-permute-start.3 = (bf16[1024,512]{1,0:T(8,128)(2,1)S(1)}, bf16[1024,512]{1,0:T(8,128)(2,1)S(1)}, u32[]{:S(2)}, u32[]{:S(2)}) collective-permute-start(bf16[1024,512]{1,0:T(8,128)(2,1)S(1)} %get-tuple-element.35), channel_id=1, source_target_pairs={{4,0},{5,1},{6,2},{7,3},{12,8},{13,9},{14,10},{15,11},{20,16},{21,... | collective-permute-start | bytes 3145736 | tf_op jit(solution)/shard_map/ppermute | solution.py:382
  833.8 333.4 %reduce-scatter.10.cloned.1.call-start = ((), (), s32[]{:S(2)}) async-start(), calls=%async_computation.12 | async-start | bytes 2359296 | tf_op jit(solution)/shard_map/reduce_scatter | solution.py:271
  842.9 399.6 %reduce-scatter.14.cloned.1.call-start = ((), (), s32[]{:S(2)}) async-start(), calls=%async_computation.14 | async-start | bytes 9437184 | tf_op jit(solution)/shard_map/reduce_scatter | solution.py:271
  857.0 425.1 %reduce-scatter.16.cloned.1.call-start = ((), (), s32[]{:S(2)}) async-start(), calls=%async_computation.15 | async-start | bytes 1179648
  1130.9 216.3 %reduce-scatter.8.cloned.1.call-start = ((), (), s32[]{:S(2)}) async-start(), calls=%async_computation.11 | async-start | bytes 7077888 | tf_op jit(solution)/shard_map/reduce_scatter | solution.py:271
  1136.7 330.4 %reduce-scatter.12.cloned.1.call-start = ((), (), s32[]{:S(2)}) async-start(), calls=%async_computation.13 | async-start | bytes 18874368 | tf_op jit(solution)/shard_map/reduce_scatter | solution.py:271
  1166.0 76.4 %copy-start.25 = (f32[2048,256]{1,0:T(8,128)S(1)}, f32[2048,256]{1,0:T(8,128)}, u32[]{:S(2)}) copy-start(f32[2048,256]{1,0:T(8,128)} %param.24) | copy-start | bytes 6291460
  1169.8 79.9 %copy-start.46 = (f32[1024]{0:T(1024)S(1)}, f32[1024]{0:T(1024)}, u32[]{:S(2)}) copy-start(f32[1024]{0:T(1024)} %get-tuple-element.84) | copy-start | bytes 12292
  1251.6 95.6 %copy-start.26 = (f32[3,256,512]{2,1,0:T(8,128)S(1)}, f32[3,256,512]{2,1,0:T(8,128)}, u32[]{:S(2)}) copy-start(f32[3,256,512]{2,1,0:T(8,128)} %param.21) | copy-start | bytes 4718596
  1251.6 95.6 %copy-start.34 = (f32[3,256,512]{2,1,0:T(8,128)S(1)}, f32[3,256,512]{2,1,0:T(8,128)}, u32[]{:S(2)}) copy-start(f32[3,256,512]{2,1,0:T(8,128)} %param.26) | copy-start | bytes 4718596
  1283.1 69.0 %copy-start.47 = (f32[2,256]{1,0:T(2,128)}, f32[2,256]{1,0:T(2,128)S(1)}, u32[]{:S(2)}) copy-start(f32[2,256]{1,0:T(2,128)S(1)} %copy.63) | copy-start | bytes 6148
  (53 other events, 656.6 us)
Sparse Core Ops, SparseCore 0:
  10.5 48.2 all-gather.4
  61.2 29.5 all-gather.6
  161.7 172.0 all-reduce.4
  336.2 88.8 all-gather.8
  427.6 55.9 all-gather.10
  531.3 154.9 all-reduce.6
  834.0 289.7 all-reduce.8
  1127.0 40.2 reduce-scatter.9
  1171.1 71.2 reduce-scatter.13
  1246.0 36.0 reduce-scatter.15
  1285.5 61.7 reduce-scatter.7
  1351.1 115.9 reduce-scatter.11

commit v2 on v0

v2 whole, which is shorter than its diff:
```python
import functools
import jax
import jax.numpy as jnp
from jax import lax
from jax.experimental import pallas as pl
from jax.experimental.pallas import tpu as pltpu
from jax.sharding import PartitionSpec as P

HEAD = 64
PAIR = 128
BLOCK = 256
CHUNK = 64
MASKED = -1e30
MESH = pl.DeviceIdType.MESH


norm_eps = 1e-05
rope_base = 130000.0
beta_one = 0.9
beta_two = 0.95
learn_rate = 0.02
decay_rate = 0.1
adam_eps = 1e-08
step_count = 4.0


def rotation(position, head_size):
    half = head_size // 2
    freqs = rope_base ** (-(jnp.arange(half, dtype=jnp.float32) * 2.0) / head_size)
    angle = position.astype(jnp.float32)[:, None] * freqs[None, :]
    return (jnp.cos(angle)[:, None, :], jnp.sin(angle)[:, None, :])


def outer_sum(left, right):
    return lax.dot_general(
        left, right, (((0,), (0,)), ((), ())), preferred_element_type=jnp.float32
    )


def back_dot(grad, weight):
    return lax.dot_general(
        grad, weight, (((1,), (1,)), ((), ())), preferred_element_type=jnp.float32
    )


def dot(left, right, contract):
    return lax.dot_general(
        left, right, ((contract[:1], contract[1:]), ((), ())), preferred_element_type=jnp.float32
    )


def one_head(values, head):
    lane = lax.broadcasted_iota(jnp.int32, values.shape, 1)
    return jnp.where((lane < HEAD) == (head == 0), values, jnp.zeros_like(values))


def causal(scores):
    key = lax.broadcasted_iota(jnp.int32, scores.shape, 0)
    query = lax.broadcasted_iota(jnp.int32, scores.shape, 1)
    return jnp.where(key <= query, scores, MASKED)


def rotate_lanes(values, cosine, sine):
    lane = lax.broadcasted_iota(jnp.int32, values.shape, 1) % HEAD
    width = values.shape[1]
    ahead = pltpu.roll(values, width - HEAD // 2, 1)
    behind = pltpu.roll(values, HEAD // 2, 1)
    return values * cosine + jnp.where(lane < HEAD // 2, -ahead, behind) * sine


def greet(me, count, more=0):
    barrier = pltpu.get_barrier_semaphore()

    @pl.when(me > 0)
    def _():
        pl.semaphore_signal(barrier, inc=1, device_id={"tp": me - 1}, device_id_type=MESH)

    @pl.when(me < count - 1)
    def _():
        pl.semaphore_signal(barrier, inc=1, device_id={"tp": me + 1}, device_id_type=MESH)

    @pl.when((me > 0) & (me < count - 1))
    def _():
        pl.semaphore_wait(barrier, 2 + more)

    @pl.when((me == 0) | (me == count - 1))
    def _():
        pl.semaphore_wait(barrier, 1 + more)


def chain_parts(count, part_ref, out_ref, slots, send, recv, finish, size):
    me = lax.axis_index("tp")
    half = out_ref.shape[0] // 2
    chunks = half // size

    def copy(stream, at, source, target, device):
        return pltpu.make_async_remote_copy(
            src_ref=source, dst_ref=target, send_sem=send.at[stream, at],
            recv_sem=recv.at[stream, at], device_id={"tp": device}, device_id_type=MESH,
        )

    def ends(way):
        place = me if way == 1 else count - 1 - me
        return place, me + way

    def reduce_copy(way, at, device):
        index = 0 if way == 1 else 1
        rows = pl.ds(pl.multiple_of(at * size, size), size)
        return copy(index, at, slots.at[index, rows], slots.at[index, rows], device)

    def spread_copy(way, at, device):
        base = 0 if way == 1 else half
        rows = pl.ds(pl.multiple_of(base + at * size, size), size)
        return copy(2 if way == 1 else 3, at, out_ref.at[rows], out_ref.at[rows], device)

    def reduce_step(way, tick):
        place, ahead = ends(way)
        index = 0 if way == 1 else 1
        base = half if way == 1 else 0
        at = tick - place

        @pl.when((at >= 0) & (at < chunks))
        def _():
            local = pl.ds(pl.multiple_of(at * size, size), size)
            rows = pl.ds(pl.multiple_of(base + at * size, size), size)

            @pl.when(place == 0)
            def _():
                slots[index, local] = part_ref[rows]

            @pl.when(place > 0)
            def _():
                reduce_copy(way, at, ahead).wait_recv()

            @pl.when((place > 0) & (place < count - 1))
            def _():
                slots[index, local] = (
                    slots[index, local].astype(jnp.float32) + part_ref[rows].astype(jnp.float32)
                ).astype(jnp.bfloat16)

            @pl.when(place < count - 1)
            def _():
                reduce_copy(way, at, ahead).start()

            @pl.when(place == count - 1)
            def _():
                total = slots[index, local].astype(jnp.float32) + part_ref[rows].astype(jnp.float32)
                out_ref[rows] = finish(rows, total)
                spread_copy(-way, at, me - way).start()

    def spread_step(way, tick):
        place, ahead = ends(way)
        at = tick - (count - 1) - place

        @pl.when((at >= 0) & (at < chunks) & (place > 0))
        def _():
            spread_copy(way, at, ahead).wait_recv()

            @pl.when(place < count - 1)
            def _():
                spread_copy(way, at, ahead).start()

    def step(tick):
        for way in (1, -1):
            reduce_step(way, tick)
        for way in (1, -1):
            spread_step(way, tick)

    def drain():
        @pl.loop(0, chunks)
        def _(at):
            for way in (1, -1):
                place, ahead = ends(way)

                @pl.when(place < count - 1)
                def _():
                    reduce_copy(way, at, ahead).wait_send()
                    spread_copy(way, at, ahead).wait_send()

    return step, drain, chunks + 2 * (count - 1)


def chain(count, part_ref, out_ref, slots, send, recv, finish):
    step, drain, ticks = chain_parts(count, part_ref, out_ref, slots, send, recv, finish, CHUNK)
    pl.loop(0, ticks)(step)
    drain()


def unit_scale(stream):
    return lax.rsqrt(jnp.mean(stream * stream, axis=-1, keepdims=True) + norm_eps)


def fold(values):
    return values.reshape(-1, 8, values.shape[1]).sum(0)


def norm_back(stream, gain, upstream):
    scale = unit_scale(stream)
    gain_grad = fold(upstream * stream * scale)
    inner = jnp.sum(upstream * gain * stream, axis=-1, keepdims=True)
    grad = scale * gain * upstream - stream * (scale * scale * scale / stream.shape[-1]) * inner
    return grad, gain_grad


def middle_kernel(count, part_ref, tokens_ref, gain_ref, out_ref, middle_ref, slots, send, recv):
    greet(lax.axis_index("tp"), count)
    middle_ref[...] = jnp.zeros_like(middle_ref)

    def finish(rows, total):
        middle = tokens_ref[rows].astype(jnp.float32) + total
        middle_ref[rows] = middle
        return (middle * unit_scale(middle) * gain_ref[...]).astype(jnp.bfloat16)

    chain(count, part_ref, out_ref, slots, send, recv, finish)


def middle_back_kernel(
    count, part_ref, middle_ref, cotangent_ref, gain_ref, out_ref, grad_ref, gain_grad_ref, slots, send, recv
):
    greet(lax.axis_index("tp"), count)
    grad_ref[...] = jnp.zeros_like(grad_ref)
    gain_grad_ref[...] = jnp.zeros_like(gain_grad_ref)

    def finish(rows, total):
        grad, gain_grad = norm_back(middle_ref[rows], gain_ref[...], total)
        gain_grad_ref[...] += gain_grad
        grad = cotangent_ref[rows].astype(jnp.float32) + grad
        grad_ref[rows] = grad
        return grad.astype(jnp.bfloat16)

    chain(count, part_ref, out_ref, slots, send, recv, finish)


def input_back_kernel(
    count, part_ref, tokens_ref, grad_ref, gain_ref, out_ref, gain_grad_ref, slots, send, recv
):
    greet(lax.axis_index("tp"), count)
    gain_grad_ref[...] = jnp.zeros_like(gain_grad_ref)

    def finish(rows, total):
        grad, gain_grad = norm_back(tokens_ref[rows].astype(jnp.float32), gain_ref[...], total)
        gain_grad_ref[...] += gain_grad
        return (grad_ref[rows] + grad).astype(jnp.bfloat16)

    chain(count, part_ref, out_ref, slots, send, recv, finish)


def run_chain(kernel, name, number, count, inputs, extra):
    rows, width = inputs[0].shape
    vmem = pl.BlockSpec(memory_space=pltpu.VMEM)
    chunks = rows // 2 // CHUNK
    outs = (jax.ShapeDtypeStruct((rows, width), jnp.bfloat16),) + tuple(extra)
    return pl.pallas_call(
        functools.partial(kernel, count),
        out_shape=outs,
        in_specs=[vmem] * len(inputs),
        out_specs=(vmem,) * len(outs),
        scratch_shapes=[
            pltpu.VMEM((2, rows // 2, width), jnp.bfloat16),
            pltpu.SemaphoreType.DMA((4, chunks)),
            pltpu.SemaphoreType.DMA((4, chunks)),
        ],
        compiler_params=pltpu.CompilerParams(
            collective_id=number, has_side_effects=True, vmem_limit_bytes=56 * 2**20
        ),
        cost_estimate=pl.CostEstimate(
            flops=100 * 10**9, bytes_accessed=12 * rows * width, transcendentals=0
        ),
        name=name,
    )(*inputs)


def rotate_pairs(values, cosine, sine):
    parts = [
        rotate_lanes(values[:, at : at + PAIR], cosine, sine)
        for at in range(0, values.shape[1], PAIR)
    ]
    return jnp.concatenate(parts, 1)


def greet_partner(late):
    barrier = pltpu.get_barrier_semaphore()
    pl.semaphore_signal(barrier, inc=1, device_id={"ctx": 1 - late}, device_id_type=MESH)
    pl.semaphore_wait(barrier, 1)


def front_kernel(
    live_ref, tokens_ref, weight_ref, gain_ref, cos_ref, sin_ref,
    h_ref, q_ref, k_ref, v_ref, kp_ref, vp_ref, o_ref, l_ref, send, recv,
):
    late = lax.axis_index("ctx")
    rows, width = q_ref.shape
    block = min(BLOCK, rows)
    blocks = rows // block
    pairs = width // PAIR
    greet_partner(late)

    def here(at):
        return pl.ds(pl.multiple_of(at * block, block), block)

    def lanes(pair):
        return pl.ds(pl.multiple_of(pair * PAIR, PAIR), PAIR)

    @pl.loop(0, blocks)
    def _(at):
        stream = tokens_ref[here(at)].astype(jnp.float32)
        normed = (stream * unit_scale(stream) * gain_ref[...]).astype(jnp.bfloat16)
        h_ref[here(at)] = normed
        keys = dot(normed, weight_ref[1], (1, 0))
        k_ref[here(at)] = rotate_pairs(keys, cos_ref[here(at)], sin_ref[here(at)]).astype(jnp.bfloat16)
        v_ref[here(at)] = dot(normed, weight_ref[2], (1, 0)).astype(jnp.bfloat16)

    def exchange(pair):
        return [
            pltpu.make_async_remote_copy(
                src_ref=own.at[:, lanes(pair)], dst_ref=prev.at[:, lanes(pair)],
                send_sem=send.at[which, pair], recv_sem=recv.at[which, pair],
                device_id={"ctx": 1 - late}, device_id_type=MESH,
            )
            for which, own, prev in ((0, k_ref, kp_ref), (1, v_ref, vp_ref))
        ]

    @pl.when(late == 0)
    def _():
        @pl.loop(0, pairs)
        def _(pair):
            for copy in exchange(pair):
                copy.start()

    @pl.loop(0, blocks)
    def _(at):
        query = dot(h_ref[here(at)], weight_ref[0], (1, 0))
        query = rotate_pairs(query, cos_ref[here(at)], sin_ref[here(at)]) * 0.125
        q_ref[here(at)] = query.astype(jnp.bfloat16)

    def attend(pair, own, with_prev):
        column = lanes(pair)
        mine = slice(own * block, (own + 1) * block)
        query = q_ref[mine, column]
        mixed = []
        for head in range(2):
            queries = one_head(query, head)
            parts = []
            if with_prev:
                parts.append((dot(kp_ref[:, column], queries, (1, 1)), vp_ref[:, column]))
            if own:
                before = slice(0, own * block)
                parts.append((dot(k_ref[before, column], queries, (1, 1)), v_ref[before, column]))
            parts.append((causal(dot(k_ref[mine, column], queries, (1, 1))), v_ref[mine, column]))
            peak = parts[0][0].max(0, keepdims=True)
            for scores, _ in parts[1:]:
                peak = jnp.maximum(peak, scores.max(0, keepdims=True))
            expo = [jnp.exp(scores - peak) for scores, _ in parts]
            denom = expo[0].sum(0, keepdims=True)
            for e in expo[1:]:
                denom = denom + e.sum(0, keepdims=True)
            inverse = 1.0 / denom
            total = None
            for e, (_, value) in zip(expo, parts):
                term = dot(value, (e * inverse).astype(jnp.bfloat16), (0, 0))
                total = term if total is None else total + term
            mixed.append(total[head * HEAD : (head + 1) * HEAD])
            index = late * rows + own * block + lax.broadcasted_iota(jnp.int32, peak.shape, 1)
            l_ref[pair, head : head + 1, mine] = jnp.where(
                index < live_ref[0], peak + jnp.log(denom), -MASKED
            )
        result = jnp.concatenate(mixed, 0).T
        index = late * rows + own * block + lax.broadcasted_iota(jnp.int32, result.shape, 0)
        own_value = v_ref[mine, column].astype(jnp.float32)
        o_ref[mine, column] = jnp.where(index < live_ref[0], result, own_value).astype(jnp.bfloat16)

    @pl.loop(0, pairs)
    def _(pair):
        @pl.when(late == 0)
        def _():
            for own in range(blocks):
                attend(pair, own, False)

        @pl.when(late == 1)
        def _():
            for copy in exchange(pair):
                copy.wait_recv()
            for own in range(blocks):
                attend(pair, own, True)

    @pl.when(late == 0)
    def _():
        @pl.loop(0, pairs)
        def _(pair):
            for copy in exchange(pair):
                copy.wait_send()


VMEM_SPEC = pl.BlockSpec(memory_space=pltpu.VMEM)
SMEM_SPEC = pl.BlockSpec(memory_space=pltpu.SMEM)


def layer_front(live, tokens, weight, gain, cosine, sine):
    rows, depth = tokens.shape
    width = weight.shape[2]
    pairs = width // PAIR
    part = jax.ShapeDtypeStruct((rows, width), jnp.bfloat16)
    outs = (
        jax.ShapeDtypeStruct((rows, depth), jnp.bfloat16), part, part, part, part, part, part,
        jax.ShapeDtypeStruct((pairs, 2, rows), jnp.float32),
    )
    return pl.pallas_call(
        front_kernel,
        out_shape=outs,
        in_specs=[SMEM_SPEC] + [VMEM_SPEC] * 5,
        out_specs=(VMEM_SPEC,) * len(outs),
        scratch_shapes=[pltpu.SemaphoreType.DMA((2, pairs))] * 2,
        compiler_params=pltpu.CompilerParams(
            collective_id=4, has_side_effects=True, vmem_limit_bytes=56 * 2**20
        ),
        cost_estimate=pl.CostEstimate(
            flops=80 * 10**9, bytes_accessed=40 * 2**20, transcendentals=0
        ),
        name="layer_front",
    )(live, tokens, weight, gain, cosine, sine)


def attend_back_kernel(
    count, live_ref, q_ref, k_ref, v_ref, kp_ref, vp_ref, o_ref, do_ref, l_ref, cos_ref, sin_ref,
    part_ref, dq_ref, dk_ref, dv_ref, out_ref,
    dq_acc, dk_acc, dv_acc, dkp_acc, dvp_acc, leave, arrive, slots, send, recv, chain_send, chain_recv,
):
    late = lax.axis_index("ctx")
    me = lax.axis_index("tp")
    rows, width = q_ref.shape
    block = min(BLOCK, rows)
    blocks = rows // block
    pairs = width // PAIR
    barrier = pltpu.get_barrier_semaphore()
    pl.semaphore_signal(barrier, inc=1, device_id={"ctx": 1 - late}, device_id_type=MESH)
    greet(me, count, 1)
    tick, drain, ticks = chain_parts(
        count, part_ref, out_ref, slots, chain_send, chain_recv,
        lambda at, total: total.astype(jnp.bfloat16), 32,
    )

    def here(at):
        return pl.ds(pl.multiple_of(at * block, block), block)

    def lanes(pair):
        return pl.ds(pl.multiple_of(pair * PAIR, PAIR), PAIR)

    def prepare(pair, step):
        column = lanes(pair)
        query = q_ref[here(step), column]
        upstream = do_ref[here(step), column]
        product = (upstream.astype(jnp.float32) * o_ref[here(step), column].astype(jnp.float32)).T
        queries = [one_head(query, head) for head in range(2)]
        upstreams = [one_head(upstream, head) for head in range(2)]
        inner = [
            product[head * HEAD : (head + 1) * HEAD].sum(0, keepdims=True) for head in range(2)
        ]
        totals = [l_ref[pair, head : head + 1, here(step)] for head in range(2)]
        query_both = jnp.concatenate(queries, 0)
        upstream_both = jnp.concatenate(upstreams, 0)

        def tile(keys, values, masked):
            grads, probs_all, out = [], [], []
            for head in range(2):
                scores = dot(keys, queries[head], (1, 1))
                if masked:
                    scores = causal(scores)
                probs = jnp.exp(scores - totals[head])
                prob_grad = dot(values, upstreams[head], (1, 1))
                score_grad = (probs * (prob_grad - inner[head])).astype(jnp.bfloat16)
                probs_all.append(probs.astype(jnp.bfloat16))
                grads.append(score_grad)
                out.append(dot(keys, score_grad, (0, 0))[head * HEAD : (head + 1) * HEAD])
            key_grad = dot(jnp.concatenate(grads, 1), query_both, (1, 0))
            value_grad = dot(jnp.concatenate(probs_all, 1), upstream_both, (1, 0))
            return jnp.concatenate(out, 0), key_grad, value_grad

        return tile, upstream

    def exchange(pair):
        return pltpu.make_async_remote_copy(
            src_ref=leave.at[pair], dst_ref=arrive.at[pair], send_sem=send.at[pair],
            recv_sem=recv.at[pair], device_id={"ctx": 1 - late}, device_id_type=MESH,
        )

    def prev_step(pair, step):
        column = lanes(pair)
        tile, _ = prepare(pair, step)

        @pl.when(step == 0)
        def _():
            dkp_acc[...] = jnp.zeros_like(dkp_acc)
            dvp_acc[...] = jnp.zeros_like(dvp_acc)

        query_grad = None
        for at in range(blocks):
            mine = slice(at * block, (at + 1) * block)
            more, key_grad, value_grad = tile(kp_ref[mine, column], vp_ref[mine, column], False)
            query_grad = more if query_grad is None else query_grad + more
            dkp_acc[mine] += key_grad
            dvp_acc[mine] += value_grad
        dq_acc[pair, :, here(step)] = query_grad

        @pl.when(step == blocks - 1)
        def _():
            leave[pair, 0] = dkp_acc[...].astype(jnp.bfloat16)
            leave[pair, 1] = dvp_acc[...].astype(jnp.bfloat16)
            exchange(pair).start()

    def own_step(pair, step):
        column = lanes(pair)
        tile, upstream = prepare(pair, step)
        query_grad, key_grad, value_grad = tile(k_ref[here(step), column], v_ref[here(step), column], True)
        index = late * rows + step * block + lax.broadcasted_iota(jnp.int32, upstream.shape, 0)
        dk_acc[here(step), column] = key_grad
        dv_acc[here(step), column] = value_grad + jnp.where(
            index < live_ref[0], 0.0, upstream.astype(jnp.float32)
        )
        dq_acc[pair, :, here(step)] += query_grad

        @pl.loop(0, step)
        def _(at):
            more, key_grad, value_grad = tile(k_ref[here(at), column], v_ref[here(at), column], False)
            dk_acc[here(at), column] += key_grad
            dv_acc[here(at), column] += value_grad
            dq_acc[pair, :, here(step)] += more

        grad = dq_acc[pair, :, here(step)].T * 0.125
        grad = rotate_lanes(grad, cos_ref[here(step)], -sin_ref[here(step)])
        dq_ref[here(step), column] = grad.astype(jnp.bfloat16)

    @pl.when(late == 0)
    def _():
        dq_acc[...] = jnp.zeros_like(dq_acc)

    steps = pairs * blocks

    @pl.loop(0, 2 * steps)
    def _(at):
        @pl.when(at < ticks)
        def _():
            tick(at)

        @pl.when((late == 1) & (at < steps))
        def _():
            prev_step(at // blocks, at % blocks)

        @pl.when(at >= steps)
        def _():
            own_step((at - steps) // blocks, at % blocks)

    if ticks > 2 * steps:
        pl.loop(2 * steps, ticks)(tick)

    @pl.loop(0, pairs)
    def _(pair):
        column = lanes(pair)

        @pl.when(late == 0)
        def _():
            exchange(pair).wait_recv()
            dk_acc[:, column] += arrive[pair, 0].astype(jnp.float32)
            dv_acc[:, column] += arrive[pair, 1].astype(jnp.float32)

        @pl.when(late == 1)
        def _():
            exchange(pair).wait_send()

        dk_ref[:, column] = rotate_lanes(dk_acc[:, column], cos_ref[...], -sin_ref[...]).astype(
            jnp.bfloat16
        )
        dv_ref[:, column] = dv_acc[:, column].astype(jnp.bfloat16)

    drain()


def attend_back(live, arrays, cosine, sine, out_part, count):
    rows, width = arrays[0].shape
    pairs = width // PAIR
    part = jax.ShapeDtypeStruct((rows, width), jnp.bfloat16)
    outs = (part, part, part, jax.ShapeDtypeStruct(out_part.shape, jnp.bfloat16))
    chunks = rows // 2 // 32
    return pl.pallas_call(
        functools.partial(attend_back_kernel, count),
        out_shape=outs,
        in_specs=[SMEM_SPEC] + [VMEM_SPEC] * 11,
        out_specs=(VMEM_SPEC,) * len(outs),
        scratch_shapes=[
            pltpu.VMEM((pairs, PAIR, rows), jnp.float32),
            pltpu.VMEM((rows, width), jnp.float32),
            pltpu.VMEM((rows, width), jnp.float32),
            pltpu.VMEM((rows, PAIR), jnp.float32),
            pltpu.VMEM((rows, PAIR), jnp.float32),
            pltpu.VMEM((pairs, 2, rows, PAIR), jnp.bfloat16),
            pltpu.VMEM((pairs, 2, rows, PAIR), jnp.bfloat16),
            pltpu.VMEM((2, rows // 2, out_part.shape[1]), jnp.bfloat16),
            pltpu.SemaphoreType.DMA((pairs,)),
            pltpu.SemaphoreType.DMA((pairs,)),
            pltpu.SemaphoreType.DMA((4, chunks)),
            pltpu.SemaphoreType.DMA((4, chunks)),
        ],
        compiler_params=pltpu.CompilerParams(
            collective_id=5, has_side_effects=True, vmem_limit_bytes=58 * 2**20
        ),
        cost_estimate=pl.CostEstimate(
            flops=100 * 10**9, bytes_accessed=40 * 2**20, transcendentals=0
        ),
        name="attend_back",
    )(live, *arrays, cosine, sine, out_part)


def scatter_low(grad):
    return lax.psum_scatter(
        grad.astype(jnp.bfloat16), ("shard", "ctx"), scatter_dimension=1, tiled=True
    ).astype(jnp.float32)


def after(array, *others):
    return lax.optimization_barrier((array, *others))[0]


def adam_update(weight, first, second, grad, decay):
    first_new = beta_one * first + (1.0 - beta_one) * grad
    second_new = beta_two * second + (1.0 - beta_two) * grad * grad
    first_hat = first_new / (1.0 - beta_one**step_count)
    second_hat = second_new / (1.0 - beta_two**step_count)
    update = learn_rate * (first_hat / (jnp.sqrt(second_hat) + adam_eps) + decay * weight)
    return (update, first_new, second_new)


def body(
    tokens,
    cotangent,
    lengths,
    qkv_weight,
    out_weight,
    gate_up_weight,
    down_weight,
    norm_gains,
    qkv_first,
    out_first,
    gate_up_first,
    down_first,
    gains_first,
    qkv_second,
    out_second,
    gate_up_second,
    down_second,
    gains_second,
):
    row_count = tokens.shape[0]
    count = lax.axis_size("tp")
    offset = lax.axis_index("ctx") * row_count
    query_index = offset + jnp.arange(row_count, dtype=jnp.int32)
    qkv_low = qkv_weight.astype(jnp.bfloat16)
    out_low = out_weight.astype(jnp.bfloat16)
    gate_up_low = gate_up_weight.astype(jnp.bfloat16)
    down_low = down_weight.astype(jnp.bfloat16)
    gains_low = norm_gains.astype(jnp.bfloat16)
    qkv_full, out_full, gate_up_full, down_full, gains_full = (
        lax.all_gather(qkv_low, ("shard", "ctx"), axis=1, tiled=True),
        lax.all_gather(out_low, ("shard", "ctx"), axis=1, tiled=True),
        lax.all_gather(gate_up_low, ("shard", "ctx"), axis=1, tiled=True),
        lax.all_gather(down_low, ("shard", "ctx"), axis=1, tiled=True),
        lax.all_gather(gains_low, ("shard", "ctx"), axis=1, tiled=True),
    )
    gain_one = gains_full[0:1].astype(jnp.float32)
    gain_two = gains_full[1:2].astype(jnp.float32)
    cosine, sine = rotation(query_index, HEAD)
    cosine, sine = (jnp.concatenate([c[:, 0]] * 4, 1) for c in (cosine, sine))
    normed_one, query, keys, values, keys_prev, values_prev, mixed_low, totals = layer_front(
        lengths, tokens, qkv_full, gain_one, cosine, sine
    )
    attn_part = jnp.dot(mixed_low, out_full, preferred_element_type=jnp.float32)
    whole = jax.ShapeDtypeStruct(attn_part.shape, jnp.float32)
    eight = jax.ShapeDtypeStruct((8, attn_part.shape[1]), jnp.float32)
    normed_two, middle = run_chain(
        middle_kernel, "sum_middle", 1, count,
        [attn_part.astype(jnp.bfloat16), tokens, gain_two], [whole],
    )
    gate = jnp.dot(normed_two, gate_up_full[0], preferred_element_type=jnp.float32)
    upward = jnp.dot(normed_two, gate_up_full[1], preferred_element_type=jnp.float32)
    sigma = jax.nn.sigmoid(gate)
    swish = gate * sigma
    hidden = (swish * upward).astype(jnp.bfloat16)
    mlp_part = jnp.dot(hidden, down_full, preferred_element_type=jnp.float32)
    out_part = (middle + mlp_part).astype(jnp.bfloat16)
    down_grad_local = outer_sum(hidden, cotangent).astype(jnp.bfloat16)
    hidden_grad = back_dot(cotangent, down_full)
    gate_grad = (hidden_grad * upward * sigma * (1.0 + gate * (1.0 - sigma))).astype(jnp.bfloat16)
    upward_grad = (hidden_grad * swish).astype(jnp.bfloat16)
    gate_up_grad_local = jnp.stack(
        [outer_sum(normed_two, gate_grad), outer_sum(normed_two, upward_grad)]
    ).astype(jnp.bfloat16)
    mlp_back_part = (
        back_dot(gate_grad, gate_up_full[0]) + back_dot(upward_grad, gate_up_full[1])
    ).astype(jnp.bfloat16)
    mlp_back_part, down_grad_local, gate_up_grad_local, out_part = lax.optimization_barrier(
        (mlp_back_part, down_grad_local, gate_up_grad_local, out_part)
    )
    down_grad = scatter_low(down_grad_local)
    middle_low, middle_grad, gain_two_grad = run_chain(
        middle_back_kernel, "sum_middle_back", 2, count,
        [mlp_back_part, middle, cotangent, gain_two], [whole, eight],
    )
    gate_up_grad = scatter_low(after(gate_up_grad_local, down_grad, middle_low))
    out_grad_local = outer_sum(mixed_low, middle_low).astype(jnp.bfloat16)
    mixed_grad = back_dot(middle_low, out_full).astype(jnp.bfloat16)
    query_low, key_low, value_low, out_tokens = attend_back(
        lengths,
        [query, keys, values, keys_prev, values_prev, mixed_low, mixed_grad, totals],
        cosine, sine, out_part, count,
    )
    qkv_grad_local = jnp.stack(
        [
            outer_sum(normed_one, query_low),
            outer_sum(normed_one, key_low),
            outer_sum(normed_one, value_low),
        ]
    ).astype(jnp.bfloat16)
    attn_back_part = (
        back_dot(query_low, qkv_full[0])
        + back_dot(key_low, qkv_full[1])
        + back_dot(value_low, qkv_full[2])
    ).astype(jnp.bfloat16)
    attn_back_part, qkv_grad_local, out_grad_local, _ = lax.optimization_barrier(
        (attn_back_part, qkv_grad_local, out_grad_local, gate_up_grad)
    )
    out_grad = scatter_low(out_grad_local)
    qkv_grad = scatter_low(after(qkv_grad_local, out_grad))
    input_grad, gain_one_grad = run_chain(
        input_back_kernel, "sum_input_back", 3, count,
        [attn_back_part, tokens, middle_grad, gain_one], [eight],
    )
    gains_local = lax.psum(
        jnp.stack([gain_one_grad.sum(0), gain_two_grad.sum(0)]), ("shard", "ctx", "tp")
    )
    gains_grad = lax.dynamic_slice_in_dim(
        gains_local, lax.axis_index(("shard", "ctx")) * norm_gains.shape[1], norm_gains.shape[1], 1
    )
    qkv_step, qkv_first_new, qkv_second_new = adam_update(
        qkv_weight, qkv_first, qkv_second, qkv_grad, decay_rate
    )
    out_step, out_first_new, out_second_new = adam_update(
        out_weight, out_first, out_second, out_grad, decay_rate
    )
    gate_up_step, gate_up_first_new, gate_up_second_new = adam_update(
        gate_up_weight, gate_up_first, gate_up_second, gate_up_grad, decay_rate
    )
    down_step, down_first_new, down_second_new = adam_update(
        down_weight, down_first, down_second, down_grad, decay_rate
    )
    gains_step, gains_first_new, gains_second_new = adam_update(
        norm_gains, gains_first, gains_second, gains_grad, 0.0
    )
    qkv_new = qkv_weight - qkv_step
    gate_up_new = gate_up_weight - gate_up_step
    down_new = down_weight - down_step
    return (
        out_tokens,
        input_grad,
        qkv_grad,
        out_grad,
        gate_up_grad,
        down_grad,
        gains_grad,
        qkv_new,
        out_step,
        gate_up_new,
        down_new,
        gains_step,
        qkv_first_new,
        out_first_new,
        gate_up_first_new,
        down_first_new,
        gains_first_new,
        qkv_second_new,
        out_second_new,
        gate_up_second_new,
        down_second_new,
        gains_second_new,
    )


def solution(mesh):
    return jax.shard_map(
        body,
        mesh=mesh,
        in_specs=(
            P(("shard", "ctx"), None),
            P(("shard", "ctx"), None),
            P("shard"),
            P(None, ("shard", "ctx"), "tp"),
            P("tp", ("shard", "ctx")),
            P(None, ("shard", "ctx"), "tp"),
            P("tp", ("shard", "ctx")),
            P(None, ("shard", "ctx")),
            P(None, ("shard", "ctx"), "tp"),
            P("tp", ("shard", "ctx")),
            P(None, ("shard", "ctx"), "tp"),
            P("tp", ("shard", "ctx")),
            P(None, ("shard", "ctx")),
            P(None, ("shard", "ctx"), "tp"),
            P("tp", ("shard", "ctx")),
            P(None, ("shard", "ctx"), "tp"),
            P("tp", ("shard", "ctx")),
            P(None, ("shard", "ctx")),
        ),
        out_specs=(
            P(("shard", "ctx"), None),
            P(("shard", "ctx"), None),
            P(None, ("shard", "ctx"), "tp"),
            P("tp", ("shard", "ctx")),
            P(None, ("shard", "ctx"), "tp"),
            P("tp", ("shard", "ctx")),
            P(None, ("shard", "ctx")),
            P(None, ("shard", "ctx"), "tp"),
            P("tp", ("shard", "ctx")),
            P(None, ("shard", "ctx"), "tp"),
            P("tp", ("shard", "ctx")),
            P(None, ("shard", "ctx")),
            P(None, ("shard", "ctx"), "tp"),
            P("tp", ("shard", "ctx")),
            P(None, ("shard", "ctx"), "tp"),
            P("tp", ("shard", "ctx")),
            P(None, ("shard", "ctx")),
            P(None, ("shard", "ctx"), "tp"),
            P("tp", ("shard", "ctx")),
            P(None, ("shard", "ctx"), "tp"),
            P("tp", ("shard", "ctx")),
            P(None, ("shard", "ctx")),
        ),
        check_vma=False,
    )
```

time: 2250 us -> 970 us (0.43)
  waiting for transfers between devices: 1580 us -> 64.7 us
  Pallas kernels: 0 us -> 597 us
  matrix products: 388 us -> 178 us
  other arithmetic: 206 us -> 49.1 us
  blocking collectives: 14.2 us -> 52.6 us
    psum x4 -> x0, waiting for transfers between devices: 961 us -> none  [the longest x1 286 us: body(): middle = stream + lax.psum(attn_part, 'tp')]
    pallas_call x0 -> x5, Pallas kernels: none -> 597 us  [the longest x3 366 us: run_chain(): pl.pallas_call(functools.partial(kernel, count), out_shape=outs, in_specs...]
    reduce_scatter x6 -> x4, waiting for transfers between devices: 440 us -> 42.8 us  [scatter_low(): lax.psum_scatter(grad.astype(jnp.bfloat16), ('shard', 'ctx'), scatter_dim...]
    dot_general x15 -> x0, matrix products: 197 us -> none  [the longest x2 44.5 us: attend_back(): jnp.einsum('qhd,khd->hqk', rows_grad, values, preferred_element_type=jnp....]
    all_gather x1, waiting for transfers between devices: 78.9 us -> 0.01 us  [body(): lax.all_gather(gate_up_low, ('shard', 'ctx'), axis=1, tiled=True)]
    convert_element_type x6 -> x2, other arithmetic: 68.5 us -> 0.62 us  [the longest x1 0.62 us: body(): gain_two = gains_full[1:2].astype(jnp.float32)]
    reduce_sum x6 -> x2, other arithmetic: 50.1 us -> 0.88 us  [the longest x1 0.86 us: body(): gain_one_grad.sum(0)]
    psum x0 -> x1, blocking collectives: none -> 37.4 us  [body(): lax.psum(jnp.stack([gain_one_grad.sum(0), gain_two_grad.sum(0)]), ('shard...]
  transfers between devices with their start and end apart: 17 -> 8, of which waited for: 13 -> 2; matrix products, arithmetic and copies ran while one was open for 17% -> 8% of each run, Pallas kernels for 0% -> 62%
where the time goes in v2:
time: 970 us; the launch traced here: 965 us
  Pallas kernels  597 us (62%)
  matrix products  178 us (18%)
  waiting for transfers between devices  64.7 us (7%)
  blocking collectives  52.6 us (5%)
  other arithmetic  49.1 us (5%)
  between operations  15.4 us (2%)
    pallas_call x3, Pallas kernels, run_chain(): pl.pallas_call(functools.partial(kernel, count), out_shape=outs, in_specs...  366 us
    pallas_call x1, Pallas kernels, attend_back(): pl.pallas_call(functools.partial(attend_back_kernel, count), out_shape=ou...  151 us
    pallas_call x1, Pallas kernels, layer_front(): pl.pallas_call(front_kernel, out_shape=outs, in_specs=[SMEM_SPEC] + [VMEM...  79.2 us
    dot_general x7, matrix products, back_dot(): lax.dot_general(grad, weight, (((1,), (1,)), ((), ())), preferred_element...  71.1 us
    dot_general x7, matrix products, outer_sum(): lax.dot_general(left, right, (((0,), (0,)), ((), ())), preferred_element_...  49.7 us
    reduce_scatter x4, waiting for transfers between devices, scatter_low(): lax.psum_scatter(grad.astype(jnp.bfloat16), ('shard', 'ctx'), scatter_dim...  42.8 us
    psum x1, blocking collectives, body(): lax.psum(jnp.stack([gain_one_grad.sum(0), gain_two_grad.sum(0)]), ('shard...  37.4 us
    dot_general x1, matrix products, body(): jnp.dot(normed_two, gate_up_full[1], preferred_element_type=jnp.float32)  21.9 us
  transfers between devices with their start and end apart: 8, of which 2 were waited for; matrix products, arithmetic and copies ran while one was open for 8% of the time, Pallas kernels for 62%

profile of v2, /device:TPU:0, one launch (start us, length us, event | category | flops | bytes accessed | tf_op | source)
XLA Modules:
  0.0 964.6 jit_solution(2561578750651079795)
XLA Ops:
  17.4 15.2 %all_gather.16 = bf16[2,2048]{1,0:T(2,128)(2,1)S(1)} all-gather(bf16[2,256]{1,0:T(2,128)(2,1)S(1)} %convert_element_type.73), channel_id=1, replica_groups=mesh['shard'=4,'ctx'=2,'tp'=4] {'shard','ctx'}, dimensions={1}, use_global_device_ids=true | all-gather | bytes 9216 | tf_op jit(solution)/shard_map/all_gather | solution.py:665
  37.0 21.8 %all-gather.5.cloned.1.call-done.weight_ref = bf16[3,2048,512]{2,1,0:T(8,128)(2,1)} async-done(((bf16[3,256,512]{2,1,0:T(8,128)(2,1)}), bf16[3,2048,512]{2,1,0:T(8,128)(2,1)}) %all-gather.5.cloned.1.call-update) | async-done | bytes 6291472 | tf_op jit(solution)/shard_map/all_gather | solution.py:661
  58.8 79.2 %layer_front.1 = (bf16[1024,2048]{1,0:T(8,128)(2,1)}, bf16[1024,512]{1,0:T(8,128)(2,1)}, bf16[1024,512]{1,0:T(8,128)(2,1)}, bf16[1024,512]{1,0:T(8,128)(2,1)}, b...) custom-call(s32[1]{0:T(128)S(6)} %copy.42.live_ref, ...), custom_call_target="tpu_custom_call" | custom-call | flops 80000000000 | bytes 41943040 | tf_op jit(solution)/shard_map/layer_front/pallas_call | solution.py:407
  138.0 6.6 convolution_convert_fusion.1.part_ref
  144.6 122.9 %sum_middle.1 = (bf16[1024,2048]{1,0:T(8,128)(2,1)}, f32[1024,2048]{1,0:T(8,128)}) custom-call(bf16[1024,2048]{1,0:T(8,128)(2,1)} %convolution_convert_fusion.1.part_ref, bf16[1024,2048]{1,0:T(8,128)(2,1)} %tokens_ref.5, f32[1,2048]{1,0:T(1,128)} %get-tuple-element.101.gain_ref), custom_call_target="tpu_custom_call" | custom-call | flops 99999997952 | bytes 25165824 | tf_op jit(solution)/shard_map/sum_middle/pallas_call | solution.py:253
  267.6 14.5 %fusion.20 = f32[1024,2048]{1,0:T(8,128)} fusion(bf16[1024,2048]{1,0:T(8,128)(2,1)} %cotangent_ref.1, bf16[2048,2048]{1,0:T(8,128)(2,1)} %all-gather.7.cloned.1.call-done), kind=kOutput, calls=%fused_computation.63 | convolution fusion | flops 8589934592 | bytes 20971520 | tf_op jit(solution)/shard_map/dot_general | solution.py:41
  282.1 14.5 %fusion.4 = f32[1024,2048]{1,0:T(8,128)} fusion(bf16[1024,2048]{1,0:T(8,128)(2,1)} %get-tuple-element.56, bf16[2,2048,2048]{2,1,0:T(8,128)(2,1)} %all-gather.11.cloned.1.call-done), kind=kOutput, calls=%fused_computation.17 | convolution fusion | flops 8589934592 | bytes 20971520 | tf_op jit(solution)/shard_map/dot_general | solution.py:681
  296.6 21.9 %multiply_convert_fusion = (bf16[1024,2048]{1,0:T(8,128)(2,1)}, bf16[1024,2048]{1,0:T(8,128)(2,1)}, bf16[1024,2048]{1,0:T(8,128)(2,1)}) fusion(f32[1024,2048]{1,0:T(8,128)} %fusion.4, f32[1024,2048]{1,0:T(8,128)} %fusion.20, bf16[1024,2048]{1,0:T(8,128)(2,1)} %get-tuple-element.56, bf16[2,2048,2048]{2,1,0:T(8,128)(2,1)} %all-gather.11.cloned.1.call-done), kind=kOutput, calls=%fused_computation.7 | convolution fusion | flops 8621391872 | bytes 41943040 | tf_op jit(solution)/shard_map/dot_general | solution.py:682
  318.5 13.9 %convolution_convert_fusion = bf16[2048,2048]{1,0:T(8,128)(2,1)} fusion(bf16[1024,2048]{1,0:T(8,128)(2,1)} %get-tuple-element.98, bf16[1024,2048]{1,0:T(8,128)(2,1)S(1)} %copy-done.15), kind=kOutput, calls=%fused_computation.13 | convolution fusion | flops 8594128896 | bytes 16777216 | tf_op jit(solution)/shard_map/dot_general | solution.py:35
  332.4 12.4 %convert_bitcast_fusion = bf16[1,2048,2048]{2,1,0:T(8,128)(2,1)S(1)} fusion(bf16[1024,2048]{1,0:T(8,128)(2,1)} %get-tuple-element.56, bf16[1024,2048]{1,0:T(8,128)(2,1)} %get-tuple-element.100), kind=kOutput, calls=%fused_computation.5 | convolution fusion | flops 8594128896 | bytes 16777216 | tf_op jit(solution)/shard_map/dot_general | solution.py:35
  344.9 9.8 %convert_bitcast_fusion.1 = bf16[1,2048,2048]{2,1,0:T(8,128)(2,1)S(1)} fusion(bf16[1024,2048]{1,0:T(8,128)(2,1)S(1)} %copy-done.23, bf16[1024,2048]{1,0:T(8,128)(2,1)S(1)} %copy-done.24), kind=kOutput, calls=%fused_computation.6 | convolution fusion | flops 8594128896 | bytes 16777216 | tf_op jit(solution)/shard_map/dot_general | solution.py:35
  354.7 6.8 pad_maximum_fusion
  361.4 12.8 %fusion.1 = f32[1024,2048]{1,0:T(8,128)S(1)} fusion(bf16[1024,2048]{1,0:T(8,128)(2,1)} %get-tuple-element.100, bf16[2,2048,2048]{2,1,0:T(8,128)(2,1)} %all-gather.11.cloned.1.call-done), kind=kOutput, calls=%fused_computation.14 | convolution fusion | flops 8589934592 | bytes 20971520 | tf_op jit(solution)/shard_map/dot_general | solution.py:41
  374.3 13.0 %add_convert_fusion.2.part_ref = bf16[1024,2048]{1,0:T(8,128)(2,1)} fusion(f32[1024,2048]{1,0:T(8,128)S(1)} %fusion.1, bf16[1024,2048]{1,0:T(8,128)(2,1)S(1)} %copy-done.25, bf16[2,2048,2048]{2,1,0:T(8,128)(2,1)} %all-gather.11.cloned.1.call-done), kind=kOutput, calls=%fused_computation.8 | convolution fusion | flops 8594128896 | bytes 25165824 | tf_op jit(solution)/shard_map/dot_general | solution.py:41
  387.3 14.5 %add_convert_fusion.1.part_ref = bf16[1024,2048]{1,0:T(8,128)(2,1)} fusion(f32[1024,2048]{1,0:T(8,128)} %get-tuple-element.57.middle_ref, bf16[1024,2048]{1,0:T(8,128)(2,1)S(1)} %copy-done.22, bf16[2048,2048]{1,0:T(8,128)(2,1)} %all-gather.7.cloned.1.call-done), kind=kOutput, calls=%fused_computation.4 | convolution fusion | flops 8594128896 | bytes 25165824 | tf_op jit(solution)/shard_map/dot_general | solution.py:686
  401.9 121.3 %sum_middle_back.1 = (bf16[1024,2048]{1,0:T(8,128)(2,1)}, f32[1024,2048]{1,0:T(8,128)}, f32[8,2048]{1,0:T(8,128)}) custom-call(bf16[1024,2048]{1,0:T(8,128)(2,1)} %add_convert_fusion.2.part_ref, f32[1024,2048]{1,0:T(8,128)} %get-tuple-element.57.middle_ref, bf16[1024,2048]{1,0:T(8,128)(2,1)} %cotangent_ref.1, f32[1,2048]{1,0:T(1,128)} %get-tuple-element.101.gain_ref), custom_call_target="tpu_custom_call" | custom-call | flops 99999997952 | bytes 25165824 | tf_op jit(solution)/shard_map/sum_middle_back/pallas_call | solution.py:253
  536.6 151.3 %attend_back.1 = (bf16[1024,512]{1,0:T(8,128)(2,1)}, bf16[1024,512]{1,0:T(8,128)(2,1)}, bf16[1024,512]{1,0:T(8,128)(2,1)}, bf16[1024,2048]{1,0:T(8,128)(2,1)}) custom-call(s32[1]{0:T(128)S(6)} %copy.42.live_ref, bf16[1024,512]{1,0:T(8,128)(2,1)} %get-tuple-element.50.q_ref, bf16[1024,512]{1,0:T(8,128)(2,1)} %get-tuple-element.51.k_ref, ...), custom_call_target="tpu_custom_call" | custom-call | flops 99999997952 | bytes 41943040 | tf_op jit(solution)/shard_map/attend_back/pallas_call | solution.py:583
  701.2 7.2 fusion.11
  708.4 7.3 fusion.10
  719.4 10.8 %add_convert_fusion.part_ref = bf16[1024,2048]{1,0:T(8,128)(2,1)} fusion(f32[1024,2048]{1,0:T(8,128)} %fusion.11, f32[1024,2048]{1,0:T(8,128)} %fusion.10, bf16[1024,512]{1,0:T(8,128)(2,1)S(1)} %copy-done.7, bf16[3,2048,512]{2,1,0:T(8,128)(2,1)} %all-gather.5.cloned.1.call-done.weight_ref), kind=kOutput, calls=%fused_computation.3 | convolution fusion | flops 2153775104 | bytes 24117248 | tf_op jit(solution)/shard_map/dot_general | solution.py:41
  730.2 10.3 %multiply_subtract_fusion = (f32[2,256,2048]{2,1,0:T(8,128)}, f32[2,256,2048]{2,1,0:T(8,128)}, f32[2,256,2048]{2,1,0:T(8,128)}, f32[2,256,2048]{2,1,0:T(8,128)}) fusion(f32[2,256,2048]{2,1,0:T(8,128)} %param.23, f32[2,256,2048]{2,1,0:T(8,128)} %param.28, f32[2,256,2048]{2,1,0:T(8,128)} %param.33, bf16[2,256,2048]{2,1,0:T(8,128)(2,1)} %reduce-scatter.7.cloned.1.call-done), kind=kLoop, calls=%fused_computation.21 | loop fusion | flops 16777216 | bytes 31457280 | tf_op jit(solution)/shard_map/sub | solution.py:757
  740.6 42.7 %reduce-scatter.9.cloned.1.call-done = bf16[512,256]{1,0:T(8,128)(2,1)} async-done(((bf16[512,2048]{1,0:T(8,128)(2,1)}), bf16[512,256]{1,0:T(8,128)(2,1)}) %reduce-scatter.9.cloned.1.call-update) | async-done | bytes 262160 | tf_op jit(solution)/shard_map/reduce_scatter | solution.py:613
  785.8 122.0 %sum_input_back.1 = (bf16[1024,2048]{1,0:T(8,128)(2,1)}, f32[8,2048]{1,0:T(8,128)}) custom-call(bf16[1024,2048]{1,0:T(8,128)(2,1)} %add_convert_fusion.part_ref, bf16[1024,2048]{1,0:T(8,128)(2,1)} %tokens_ref.5, f32[1024,2048]{1,0:T(8,128)} %get-tuple-element.71.grad_ref, f32[1,2048]{1,0:T(1,128)} %get-tuple-element.102.gain_ref), custom_call_target="tpu_custom_call" | custom-call | flops 99999997952 | bytes 25165824 | tf_op jit(solution)/shard_map/sum_input_back/pallas_call | solution.py:253
  908.8 37.4 %psum.7 = f32[2,2048]{1,0:T(2,128)S(1)} all-reduce(f32[2,2048]{1,0:T(2,128)S(1)} %pad_maximum_fusion.4), channel_id=1, replica_groups=mesh['shard'=4,'ctx'=2,'tp'=4] {'shard','ctx','tp'}, use_global_device_ids=true, to_apply=%region_6.0 | all-reduce | flops 4096 | bytes 32768 | tf_op jit(solution)/shard_map/psum | solution.py:735
  (99 shorter events, 59.0 us)
Async XLA Ops:
  7.2 51.6 %all-gather.5.cloned.1.call-start = ((), (), s32[]{:S(2)}) async-start(), calls=%async_computation.4 | async-start | bytes 7077888 | tf_op jit(solution)/shard_map/all_gather | solution.py:661
  9.8 128.2 %all-gather.9.cloned.1.call-start = ((), (), s32[]{:S(2)}) async-start(), calls=%async_computation.6 | async-start | bytes 2359296 | tf_op jit(solution)/shard_map/all_gather | solution.py:662
  11.6 256.0 %all-gather.7.cloned.1.call-start = ((), (), s32[]{:S(2)}) async-start(), calls=%async_computation.5 | async-start | bytes 9437184 | tf_op jit(solution)/shard_map/all_gather | solution.py:664
  12.8 269.3 %all-gather.11.cloned.1.call-start = ((), (), s32[]{:S(2)}) async-start(), calls=%async_computation.7 | async-start | bytes 18874368 | tf_op jit(solution)/shard_map/all_gather | solution.py:663
  16.7 506.5 %reduce-scatter.5.cloned.1.call-start = ((), (), s32[]{:S(2)}) async-start(), calls=%async_computation.8 | async-start | bytes 9437184 | tf_op jit(solution)/shard_map/reduce_scatter | solution.py:613
  296.6 21.9 %copy-start.15 = (bf16[1024,2048]{1,0:T(8,128)(2,1)S(1)}, bf16[1024,2048]{1,0:T(8,128)(2,1)}, u32[]{:S(2)}) copy-start(bf16[1024,2048]{1,0:T(8,128)(2,1)} %cotangent_ref.1) | copy-start | bytes 12582916
  332.4 12.5 %copy-start.23 = (bf16[1024,2048]{1,0:T(8,128)(2,1)S(1)}, bf16[1024,2048]{1,0:T(8,128)(2,1)}, u32[]{:S(2)}) copy-start(bf16[1024,2048]{1,0:T(8,128)(2,1)} %get-tuple-element.56) | copy-start | bytes 12582916
  332.4 12.5 %copy-start.24 = (bf16[1024,2048]{1,0:T(8,128)(2,1)S(1)}, bf16[1024,2048]{1,0:T(8,128)(2,1)}, u32[]{:S(2)}) copy-start(bf16[1024,2048]{1,0:T(8,128)(2,1)} %get-tuple-element.99) | copy-start | bytes 12582916
  361.4 12.9 %copy-start.25 = (bf16[1024,2048]{1,0:T(8,128)(2,1)S(1)}, bf16[1024,2048]{1,0:T(8,128)(2,1)}, u32[]{:S(2)}) copy-start(bf16[1024,2048]{1,0:T(8,128)(2,1)} %get-tuple-element.99) | copy-start | bytes 12582916
  374.3 13.0 %copy-start.22 = (bf16[1024,2048]{1,0:T(8,128)(2,1)S(1)}, bf16[1024,2048]{1,0:T(8,128)(2,1)}, u32[]{:S(2)}) copy-start(bf16[1024,2048]{1,0:T(8,128)(2,1)} %get-tuple-element.98) | copy-start | bytes 12582916
  401.8 121.4 %copy-start.1 = (f32[2048,256]{1,0:T(8,128)S(1)}, f32[2048,256]{1,0:T(8,128)}, u32[]{:S(2)}) copy-start(f32[2048,256]{1,0:T(8,128)} %param.24) | copy-start | bytes 6291460
  401.8 328.3 %reduce-scatter.7.cloned.1.call-start = ((), (), s32[]{:S(2)}) async-start(), calls=%async_computation.9 | async-start | bytes 18874368 | tf_op jit(solution)/shard_map/reduce_scatter | solution.py:613
  529.5 253.8 %reduce-scatter.9.cloned.1.call-start = ((), (), s32[]{:S(2)}) async-start(), calls=%async_computation.10 | async-start | bytes 2359296 | tf_op jit(solution)/shard_map/reduce_scatter | solution.py:613
  708.4 7.3 copy-start.20
  730.1 10.4 %copy-start.10 = (f32[8,2048]{1,0:T(8,128)S(1)}, f32[8,2048]{1,0:T(8,128)}, u32[]{:S(2)}) copy-start(f32[8,2048]{1,0:T(8,128)} %get-tuple-element.77) | copy-start | bytes 196612
  730.1 53.2 %copy-start.5 = (f32[512,256]{1,0:T(8,128)S(1)}, f32[512,256]{1,0:T(8,128)}, u32[]{:S(2)}) copy-start(f32[512,256]{1,0:T(8,128)} %param.22) | copy-start | bytes 1572868
  730.1 53.2 %copy-start.8 = (f32[512,256]{1,0:T(8,128)S(1)}, f32[512,256]{1,0:T(8,128)}, u32[]{:S(2)}) copy-start(f32[512,256]{1,0:T(8,128)} %param.27) | copy-start | bytes 1572868
  730.1 53.2 %copy-start.9 = (f32[512,256]{1,0:T(8,128)S(1)}, f32[512,256]{1,0:T(8,128)}, u32[]{:S(2)}) copy-start(f32[512,256]{1,0:T(8,128)} %param.32) | copy-start | bytes 1572868
  740.5 206.3 %reduce-scatter.11.cloned.1.call-start = ((), (), s32[]{:S(2)}) async-start(), calls=%async_computation.11 | async-start | bytes 7077888 | tf_op jit(solution)/shard_map/reduce_scatter | solution.py:613
  785.8 160.4 %copy-start.12 = (f32[2,256]{1,0:T(2,128)S(1)}, f32[2,256]{1,0:T(2,128)}, u32[]{:S(2)}) copy-start(f32[2,256]{1,0:T(2,128)} %param.25) | copy-start | bytes 6148
  785.8 160.4 %copy-start.13 = (f32[2,256]{1,0:T(2,128)S(1)}, f32[2,256]{1,0:T(2,128)}, u32[]{:S(2)}) copy-start(f32[2,256]{1,0:T(2,128)} %param.30) | copy-start | bytes 6148
  785.8 160.4 %copy-start.14 = (f32[2,256]{1,0:T(2,128)S(1)}, f32[2,256]{1,0:T(2,128)}, u32[]{:S(2)}) copy-start(f32[2,256]{1,0:T(2,128)} %param.35) | copy-start | bytes 6148
  785.8 161.0 %copy-start.2 = (f32[3,256,512]{2,1,0:T(8,128)S(1)}, f32[3,256,512]{2,1,0:T(8,128)}, u32[]{:S(2)}) copy-start(f32[3,256,512]{2,1,0:T(8,128)} %param.21) | copy-start | bytes 4718596
  785.8 161.0 %copy-start.6 = (f32[3,256,512]{2,1,0:T(8,128)S(1)}, f32[3,256,512]{2,1,0:T(8,128)}, u32[]{:S(2)}) copy-start(f32[3,256,512]{2,1,0:T(8,128)} %param.26) | copy-start | bytes 4718596
  (10 other events, 43.0 us)
Sparse Core Ops, SparseCore 0:
  10.5 48.2 all-gather.4
  61.2 32.5 all-gather.8
  96.3 71.2 all-gather.6
  169.9 89.8 all-gather.10
  402.0 78.6 reduce-scatter.4
  529.6 154.5 reduce-scatter.6
  740.6 42.6 reduce-scatter.8
  786.7 61.7 reduce-scatter.10

commit v3 on v2

--- a/solution.py
+++ b/solution.py
@@ -9,9 +9,17 @@
 HEAD = 64
 PAIR = 128
 BLOCK = 256
-CHUNK = 64
+CHUNK = 16
+LAG = 2
+BACK_CHUNK = 16
+BACK_LAG = 4
+WIDE = 256
+BACK_TICKS = 2
+SPACING = 5
 MASKED = -1e30
 MESH = pl.DeviceIdType.MESH
+VMEM_SPEC = pl.BlockSpec(memory_space=pltpu.VMEM)
+SMEM_SPEC = pl.BlockSpec(memory_space=pltpu.SMEM)
 
 
 norm_eps = 1e-05
@@ -31,12 +39,6 @@
     return (jnp.cos(angle)[:, None, :], jnp.sin(angle)[:, None, :])
 
 
-def outer_sum(left, right):
-    return lax.dot_general(
-        left, right, (((0,), (0,)), ((), ())), preferred_element_type=jnp.float32
-    )
-
-
 def back_dot(grad, weight):
     return lax.dot_general(
         grad, weight, (((1,), (1,)), ((), ())), preferred_element_type=jnp.float32
@@ -68,7 +70,7 @@
     return values * cosine + jnp.where(lane < HEAD // 2, -ahead, behind) * sine
 
 
-def greet(me, count, more=0):
+def greet(me, count, more=0, more_ends=0):
     barrier = pltpu.get_barrier_semaphore()
 
     @pl.when(me > 0)
@@ -85,11 +87,13 @@
 
     @pl.when((me == 0) | (me == count - 1))
     def _():
-        pl.semaphore_wait(barrier, 1 + more)
-
-
-def chain_parts(count, part_ref, out_ref, slots, send, recv, finish, size):
+        pl.semaphore_wait(barrier, 1 + more + more_ends)
+
+
+def chain_parts(count, part_ref, out_ref, slots, send, recv, finish, size, lag=1, land=None):
     me = lax.axis_index("tp")
+    apart = land is not None
+    land = land if apart else out_ref
     half = out_ref.shape[0] // 2
     chunks = half // size
 
@@ -111,13 +115,13 @@
     def spread_copy(way, at, device):
         base = 0 if way == 1 else half
         rows = pl.ds(pl.multiple_of(base + at * size, size), size)
-        return copy(2 if way == 1 else 3, at, out_ref.at[rows], out_ref.at[rows], device)
+        return copy(2 if way == 1 else 3, at, land.at[rows], land.at[rows], device)
 
     def reduce_step(way, tick):
         place, ahead = ends(way)
         index = 0 if way == 1 else 1
         base = half if way == 1 else 0
-        at = tick - place
+        at = tick - lag * place
 
         @pl.when((at >= 0) & (at < chunks))
         def _():
@@ -145,12 +149,14 @@
             @pl.when(place == count - 1)
             def _():
                 total = slots[index, local].astype(jnp.float32) + part_ref[rows].astype(jnp.float32)
-                out_ref[rows] = finish(rows, total)
+                land[rows] = finish(rows, local, total)
+                if apart:
+                    out_ref[rows] = land[rows]
                 spread_copy(-way, at, me - way).start()
 
     def spread_step(way, tick):
         place, ahead = ends(way)
-        at = tick - (count - 1) - place
+        at = tick - lag * (count - 1) - lag * place
 
         @pl.when((at >= 0) & (at < chunks) & (place > 0))
         def _():
@@ -159,6 +165,11 @@
             @pl.when(place < count - 1)
             def _():
                 spread_copy(way, at, ahead).start()
+
+            if apart:
+                base = 0 if way == 1 else half
+                rows = pl.ds(pl.multiple_of(base + at * size, size), size)
+                out_ref[rows] = land[rows]
 
     def step(tick):
         for way in (1, -1):
@@ -177,13 +188,20 @@
                     reduce_copy(way, at, ahead).wait_send()
                     spread_copy(way, at, ahead).wait_send()
 
-    return step, drain, chunks + 2 * (count - 1)
-
-
-def chain(count, part_ref, out_ref, slots, send, recv, finish):
-    step, drain, ticks = chain_parts(count, part_ref, out_ref, slots, send, recv, finish, CHUNK)
-    pl.loop(0, ticks)(step)
-    drain()
+    return step, drain, chunks + 2 * lag * (count - 1)
+
+
+def run_ticks(parts, start):
+    step, drain, ticks = parts
+    tick = pl.program_id(0)
+    pl.when(tick == 0)(start)
+    step(tick)
+    pl.when(tick == ticks - 1)(drain)
+    return tick
+
+
+def tick_count(rows, count):
+    return rows // 2 // CHUNK + 2 * LAG * (count - 1)
 
 
 def unit_scale(stream):
@@ -202,72 +220,254 @@
     return grad, gain_grad
 
 
-def middle_kernel(count, part_ref, tokens_ref, gain_ref, out_ref, middle_ref, slots, send, recv):
-    greet(lax.axis_index("tp"), count)
-    middle_ref[...] = jnp.zeros_like(middle_ref)
-
-    def finish(rows, total):
+def middle_kernel(
+    count, blocks, mixed_ref, weight_ref, tokens_ref, gain_ref, cotangent_ref, down_ref,
+    out_ref, middle_ref, hidden_grad_ref, slots, land, part_ref, send, recv,
+):
+    def start():
+        greet(lax.axis_index("tp"), count)
+
+        @pl.loop(0, part_ref.shape[0] // BLOCK)
+        def _(at):
+            here = pl.ds(pl.multiple_of(at * BLOCK, BLOCK), BLOCK)
+            part_ref[here] = dot(mixed_ref[here], weight_ref[...], (1, 0)).astype(jnp.bfloat16)
+
+    def finish(rows, local, total):
         middle = tokens_ref[rows].astype(jnp.float32) + total
-        middle_ref[rows] = middle
+        middle_ref[local] = middle
         return (middle * unit_scale(middle) * gain_ref[...]).astype(jnp.bfloat16)
 
-    chain(count, part_ref, out_ref, slots, send, recv, finish)
+    parts = chain_parts(count, part_ref, out_ref, slots, send, recv, finish, CHUNK, LAG, land)
+    tick = run_ticks(parts, start)
+
+    @pl.when((tick % SPACING == 1) & (tick < blocks * SPACING))
+    def _():
+        hidden_grad_ref[...] = dot(cotangent_ref[...], down_ref[...], (1, 1))
 
 
 def middle_back_kernel(
-    count, part_ref, middle_ref, cotangent_ref, gain_ref, out_ref, grad_ref, gain_grad_ref, slots, send, recv
+    count, part_ref, middle_ref, cotangent_ref, gain_ref, hidden_ref, down_ref,
+    out_ref, grad_ref, gain_grad_ref, layer_ref, slots, land, send, recv,
 ):
-    greet(lax.axis_index("tp"), count)
-    grad_ref[...] = jnp.zeros_like(grad_ref)
-    gain_grad_ref[...] = jnp.zeros_like(gain_grad_ref)
-
-    def finish(rows, total):
-        grad, gain_grad = norm_back(middle_ref[rows], gain_ref[...], total)
+    def start():
+        greet(lax.axis_index("tp"), count)
+        gain_grad_ref[...] = jnp.zeros_like(gain_grad_ref)
+
+    def finish(rows, local, total):
+        grad, gain_grad = norm_back(middle_ref[local], gain_ref[...], total)
         gain_grad_ref[...] += gain_grad
         grad = cotangent_ref[rows].astype(jnp.float32) + grad
-        grad_ref[rows] = grad
+        grad_ref[local] = grad
         return grad.astype(jnp.bfloat16)
 
-    chain(count, part_ref, out_ref, slots, send, recv, finish)
+    parts = chain_parts(count, part_ref, out_ref, slots, send, recv, finish, CHUNK, LAG, land)
+    tick = run_ticks(parts, start)
+
+    @pl.when((tick % SPACING == 1) & (tick < part_ref.shape[1] // WIDE * SPACING))
+    def _():
+        skip = down_ref.shape[0] - hidden_ref.shape[1]
+        layer_ref[...] = dot(hidden_ref[...], down_ref[skip:], (1, 0)).astype(jnp.bfloat16)
 
 
 def input_back_kernel(
-    count, part_ref, tokens_ref, grad_ref, gain_ref, out_ref, gain_grad_ref, slots, send, recv
+    count, part_ref, tokens_ref, grad_ref, gain_ref, other_ref,
+    out_ref, gains_ref, slots, land, local, landed, along, send, recv, plane_send, plane_recv, line_send, line_recv,
 ):
-    greet(lax.axis_index("tp"), count)
-    gain_grad_ref[...] = jnp.zeros_like(gain_grad_ref)
-
-    def finish(rows, total):
+    me = lax.axis_index("tp")
+    size, index, peer = plane_peers()
+    width = gains_ref.shape[1]
+    last = (me == 0) | (me == count - 1)
+
+    def start():
+        @pl.when(last)
+        def _():
+            greet_plane(size, peer)
+
+        greet(me, count, 0, size - 1)
+        local[0:8] = jnp.zeros((8, local.shape[1]), jnp.float32)
+        local[8:16] = other_ref[...]
+
+    def finish(rows, part, total):
         grad, gain_grad = norm_back(tokens_ref[rows].astype(jnp.float32), gain_ref[...], total)
-        gain_grad_ref[...] += gain_grad
-        return (grad_ref[rows] + grad).astype(jnp.bfloat16)
-
-    chain(count, part_ref, out_ref, slots, send, recv, finish)
-
-
-def run_chain(kernel, name, number, count, inputs, extra):
-    rows, width = inputs[0].shape
-    vmem = pl.BlockSpec(memory_space=pltpu.VMEM)
+        local[0:8] += gain_grad
+        return (grad_ref[part] + grad).astype(jnp.bfloat16)
+
+    step, drain, ticks = chain_parts(
+        count, part_ref, out_ref, slots, send, recv, finish, CHUNK, LAG, land
+    )
+
+    def columns(at):
+        return pl.ds(pl.multiple_of(at * width, width), width)
+
+    def plane_copy(distance):
+        at, device = peer(distance)
+        return pltpu.make_async_remote_copy(
+            src_ref=local.at[:, columns(at)], dst_ref=landed.at[distance],
+            send_sem=plane_send.at[distance], recv_sem=plane_recv.at[distance],
+            device_id=device, device_id_type=MESH,
+        )
+
+    def line_copy(way):
+        which = 0 if way == 1 else 1
+        return pltpu.make_async_remote_copy(
+            src_ref=along.at[which], dst_ref=along.at[which],
+            send_sem=line_send.at[which], recv_sem=line_recv.at[which],
+            device_id={"tp": me + way}, device_id_type=MESH,
+        )
+
+    done = out_ref.shape[0] // 2 // CHUNK + LAG * (count - 1)
+
+    tick = pl.program_id(0)
+    pl.when(tick == 0)(start)
+    step(tick)
+
+    @pl.when(last & (tick == done - 1))
+    def _():
+        for distance in range(1, size):
+            plane_copy(distance).start()
+
+    @pl.when(last & (tick == done + LAG))
+    def _():
+        total = local[:, columns(index)]
+        for distance in range(1, size):
+            plane_copy(distance).wait()
+            total = total + landed[distance]
+
+        @pl.when(me == 0)
+        def _():
+            along[0] = total
+            line_copy(1).start()
+
+        @pl.when(me == count - 1)
+        def _():
+            along[1] = total
+            line_copy(-1).start()
+
+    @pl.when(tick == ticks - 1)
+    def _():
+        for way in (1, -1):
+            place = me if way == 1 else count - 1 - me
+
+            @pl.when(place > 0)
+            def _():
+                line_copy(way).wait_recv()
+
+            @pl.when((place > 0) & (place < count - 1))
+            def _():
+                line_copy(way).start()
+
+        for way in (1, -1):
+            place = me if way == 1 else count - 1 - me
+
+            @pl.when(place < count - 1)
+            def _():
+                line_copy(way).wait_send()
+
+        sums = along[0] + along[1]
+        gains_ref[0:1] = sums[0:8].sum(0, keepdims=True)
+        gains_ref[1:2] = sums[8:16].sum(0, keepdims=True)
+        drain()
+
+
+def chain_call(kernel, name, number, count, shape, inputs, outs, scratch):
+    rows, width = shape
     chunks = rows // 2 // CHUNK
-    outs = (jax.ShapeDtypeStruct((rows, width), jnp.bfloat16),) + tuple(extra)
+    arrays, in_specs = zip(*inputs)
+    out_shape, out_specs = zip(*outs)
     return pl.pallas_call(
-        functools.partial(kernel, count),
-        out_shape=outs,
-        in_specs=[vmem] * len(inputs),
-        out_specs=(vmem,) * len(outs),
+        kernel,
+        out_shape=out_shape,
+        grid=(tick_count(rows, count),),
+        in_specs=in_specs,
+        out_specs=out_specs,
         scratch_shapes=[
             pltpu.VMEM((2, rows // 2, width), jnp.bfloat16),
+            pltpu.VMEM((rows, width), jnp.bfloat16),
+            *scratch[:3],
             pltpu.SemaphoreType.DMA((4, chunks)),
             pltpu.SemaphoreType.DMA((4, chunks)),
+            *scratch[3:],
         ],
         compiler_params=pltpu.CompilerParams(
-            collective_id=number, has_side_effects=True, vmem_limit_bytes=56 * 2**20
+            collective_id=number, has_side_effects=True, vmem_limit_bytes=60 * 2**20
         ),
         cost_estimate=pl.CostEstimate(
             flops=100 * 10**9, bytes_accessed=12 * rows * width, transcendentals=0
         ),
         name=name,
-    )(*inputs)
+    )(*arrays)
+
+
+def kept(shape, dtype):
+    return jax.ShapeDtypeStruct(shape, dtype), VMEM_SPEC
+
+
+def sum_middle(mixed, both, tokens, gain, cotangent, count):
+    rows, width = tokens.shape
+    inner = mixed.shape[1]
+    hidden = both.shape[0] - inner
+    last = hidden // WIDE - 1
+    at = lambda i: jnp.minimum(i // SPACING, last)
+    return chain_call(
+        functools.partial(middle_kernel, count, last + 1), "sum_middle", 1, count, tokens.shape,
+        [
+            (mixed, VMEM_SPEC),
+            (both, pl.BlockSpec((inner, width), lambda i: (0, 0), pipeline_mode=pl.Buffered(1))),
+            (tokens, VMEM_SPEC), (gain, VMEM_SPEC), (cotangent, VMEM_SPEC),
+            (both, pl.BlockSpec((WIDE, width), lambda i: (inner // WIDE + at(i), 0))),
+        ],
+        [
+            kept(tokens.shape, jnp.bfloat16),
+            kept((rows // 2, width), jnp.float32),
+            (
+                jax.ShapeDtypeStruct((rows, hidden), jnp.float32),
+                pl.BlockSpec((rows, WIDE), lambda i: (0, at(i))),
+            ),
+        ],
+        [pltpu.VMEM(tokens.shape, jnp.bfloat16)],
+    )
+
+
+def sum_middle_back(part, middle, cotangent, gain, hidden, both, count):
+    rows, width = part.shape
+    last = width // WIDE - 1
+    at = lambda i: jnp.minimum(i // SPACING, last)
+    return chain_call(
+        functools.partial(middle_back_kernel, count), "sum_middle_back", 2, count, part.shape,
+        [
+            (part, VMEM_SPEC), (middle, VMEM_SPEC), (cotangent, VMEM_SPEC), (gain, VMEM_SPEC),
+            (hidden, VMEM_SPEC), (both, pl.BlockSpec((both.shape[0], WIDE), lambda i: (0, at(i)))),
+        ],
+        [
+            kept(part.shape, jnp.bfloat16),
+            kept((rows // 2, width), jnp.float32),
+            kept((8, width), jnp.float32),
+            (
+                jax.ShapeDtypeStruct(part.shape, jnp.bfloat16),
+                pl.BlockSpec((rows, WIDE), lambda i: (0, at(i))),
+            ),
+        ],
+        [],
+    )
+
+
+def sum_input_back(part, tokens, grad, gain, other, size, count):
+    width = part.shape[1]
+    plane = width // size
+    return chain_call(
+        functools.partial(input_back_kernel, count), "sum_input_back", 3, count, part.shape,
+        [(a, VMEM_SPEC) for a in (part, tokens, grad, gain, other)],
+        [kept(part.shape, jnp.bfloat16), kept((2, size), jnp.float32)],
+        [
+            pltpu.VMEM((16, width), jnp.float32),
+            pltpu.VMEM((plane, 16, size), jnp.float32),
+            pltpu.VMEM((2, 16, size), jnp.float32),
+            pltpu.SemaphoreType.DMA((plane,)),
+            pltpu.SemaphoreType.DMA((plane,)),
+            pltpu.SemaphoreType.DMA((2,)),
+            pltpu.SemaphoreType.DMA((2,)),
+        ],
+    )
 
 
 def rotate_pairs(values, cosine, sine):
@@ -278,22 +478,52 @@
     return jnp.concatenate(parts, 1)
 
 
-def greet_partner(late):
+def plane_peers():
+    ctx = lax.axis_size("ctx")
+    size = lax.axis_size("shard") * ctx
+    mine = lax.axis_index("shard") * ctx + lax.axis_index("ctx")
+
+    def peer(distance):
+        index = lax.rem(mine + distance, size)
+        return index, {"shard": index // ctx, "ctx": lax.rem(index, ctx)}
+
+    return size, mine, peer
+
+
+def greet_plane(size, peer):
     barrier = pltpu.get_barrier_semaphore()
-    pl.semaphore_signal(barrier, inc=1, device_id={"ctx": 1 - late}, device_id_type=MESH)
-    pl.semaphore_wait(barrier, 1)
+    for distance in range(1, size):
+        pl.semaphore_signal(barrier, inc=1, device_id=peer(distance)[1], device_id_type=MESH)
 
 
 def front_kernel(
-    live_ref, tokens_ref, weight_ref, gain_ref, cos_ref, sin_ref,
-    h_ref, q_ref, k_ref, v_ref, kp_ref, vp_ref, o_ref, l_ref, send, recv,
+    live_ref, tokens_ref, weight_ref, own_gain_ref, cos_ref, sin_ref,
+    h_ref, q_ref, k_ref, v_ref, kp_ref, vp_ref, o_ref, l_ref, gain_ref,
+    send, recv, gain_send, gain_recv,
 ):
     late = lax.axis_index("ctx")
     rows, width = q_ref.shape
     block = min(BLOCK, rows)
     blocks = rows // block
     pairs = width // PAIR
-    greet_partner(late)
+    size, index, peer = plane_peers()
+    part = own_gain_ref.shape[1]
+    greet_plane(size, peer)
+    pl.semaphore_wait(pltpu.get_barrier_semaphore(), size - 1)
+    mine = pl.ds(pl.multiple_of(index * part, part), part)
+    gain_ref[:, mine] = own_gain_ref[...]
+
+    def gain_copy(distance):
+        return pltpu.make_async_remote_copy(
+            src_ref=own_gain_ref, dst_ref=gain_ref.at[:, mine],
+            send_sem=gain_send.at[distance], recv_sem=gain_recv.at[distance],
+            device_id=peer(distance)[1], device_id_type=MESH,
+        )
+
+    for distance in range(1, size):
+        gain_copy(distance).start()
+    for distance in range(1, size):
+        gain_copy(distance).wait()
 
     def here(at):
         return pl.ds(pl.multiple_of(at * block, block), block)
@@ -304,7 +534,7 @@
     @pl.loop(0, blocks)
     def _(at):
         stream = tokens_ref[here(at)].astype(jnp.float32)
-        normed = (stream * unit_scale(stream) * gain_ref[...]).astype(jnp.bfloat16)
+        normed = (stream * unit_scale(stream) * gain_ref[0:1]).astype(jnp.bfloat16)
         h_ref[here(at)] = normed
         keys = dot(normed, weight_ref[1], (1, 0))
         k_ref[here(at)] = rotate_pairs(keys, cos_ref[here(at)], sin_ref[here(at)]).astype(jnp.bfloat16)
@@ -391,10 +621,6 @@
                 copy.wait_send()
 
 
-VMEM_SPEC = pl.BlockSpec(memory_space=pltpu.VMEM)
-SMEM_SPEC = pl.BlockSpec(memory_space=pltpu.SMEM)
-
-
 def layer_front(live, tokens, weight, gain, cosine, sine):
     rows, depth = tokens.shape
     width = weight.shape[2]
@@ -403,13 +629,16 @@
     outs = (
         jax.ShapeDtypeStruct((rows, depth), jnp.bfloat16), part, part, part, part, part, part,
         jax.ShapeDtypeStruct((pairs, 2, rows), jnp.float32),
-    )
+        jax.ShapeDtypeStruct((8, depth), jnp.float32),
+    )
+    size = lax.axis_size("shard") * lax.axis_size("ctx")
     return pl.pallas_call(
         front_kernel,
         out_shape=outs,
         in_specs=[SMEM_SPEC] + [VMEM_SPEC] * 5,
         out_specs=(VMEM_SPEC,) * len(outs),
-        scratch_shapes=[pltpu.SemaphoreType.DMA((2, pairs))] * 2,
+        scratch_shapes=[pltpu.SemaphoreType.DMA((2, pairs))] * 2
+        + [pltpu.SemaphoreType.DMA((size,))] * 2,
         compiler_params=pltpu.CompilerParams(
             collective_id=4, has_side_effects=True, vmem_limit_bytes=56 * 2**20
         ),
@@ -422,7 +651,7 @@
 
 def attend_back_kernel(
     count, live_ref, q_ref, k_ref, v_ref, kp_ref, vp_ref, o_ref, do_ref, l_ref, cos_ref, sin_ref,
-    part_ref, dq_ref, dk_ref, dv_ref, out_ref,
+    part_ref, middle_ref, dq_ref, dk_ref, dv_ref, out_ref,
     dq_acc, dk_acc, dv_acc, dkp_acc, dvp_acc, leave, arrive, slots, send, recv, chain_send, chain_recv,
 ):
     late = lax.axis_index("ctx")
@@ -436,7 +665,7 @@
     greet(me, count, 1)
     tick, drain, ticks = chain_parts(
         count, part_ref, out_ref, slots, chain_send, chain_recv,
-        lambda at, total: total.astype(jnp.bfloat16), 32,
+        lambda rows, part, total: (middle_ref[part] + total).astype(jnp.bfloat16), BACK_CHUNK, BACK_LAG,
     )
 
     def here(at):
@@ -537,9 +766,11 @@
 
     @pl.loop(0, 2 * steps)
     def _(at):
-        @pl.when(at < ticks)
-        def _():
-            tick(at)
+        for more in range(BACK_TICKS):
+
+            @pl.when(at * BACK_TICKS + more < ticks)
+            def _():
+                tick(at * BACK_TICKS + more)
 
         @pl.when((late == 1) & (at < steps))
         def _():
@@ -549,8 +780,8 @@
         def _():
             own_step((at - steps) // blocks, at % blocks)
 
-    if ticks > 2 * steps:
-        pl.loop(2 * steps, ticks)(tick)
+    if ticks > 2 * steps * BACK_TICKS:
+        pl.loop(2 * steps * BACK_TICKS, ticks)(tick)
 
     @pl.loop(0, pairs)
     def _(pair):
@@ -574,16 +805,16 @@
     drain()
 
 
-def attend_back(live, arrays, cosine, sine, out_part, count):
+def attend_back(live, arrays, cosine, sine, out_part, middle, count):
     rows, width = arrays[0].shape
     pairs = width // PAIR
     part = jax.ShapeDtypeStruct((rows, width), jnp.bfloat16)
     outs = (part, part, part, jax.ShapeDtypeStruct(out_part.shape, jnp.bfloat16))
-    chunks = rows // 2 // 32
+    chunks = rows // 2 // BACK_CHUNK
     return pl.pallas_call(
         functools.partial(attend_back_kernel, count),
         out_shape=outs,
-        in_specs=[SMEM_SPEC] + [VMEM_SPEC] * 11,
+        in_specs=[SMEM_SPEC] + [VMEM_SPEC] * 12,
         out_specs=(VMEM_SPEC,) * len(outs),
         scratch_shapes=[
             pltpu.VMEM((pairs, PAIR, rows), jnp.float32),
@@ -606,12 +837,140 @@
             flops=100 * 10**9, bytes_accessed=40 * 2**20, transcendentals=0
         ),
         name="attend_back",
-    )(live, *arrays, cosine, sine, out_part)
-
-
-def scatter_low(grad):
+    )(live, *arrays, cosine, sine, out_part, middle)
+
+
+def mlp_kernel(
+    normed_ref, weight_ref, hidden_grad_ref, cotangent_ref,
+    hidden_ref, down_grad_ref, gate_up_grad_ref, back_ref, turned, total,
+):
+    step = pl.program_id(0)
+
+    @pl.when(step == 0)
+    def _():
+        turned[...] = normed_ref[...].T
+        total[...] = jnp.zeros_like(total)
+
+    gate = dot(normed_ref[...], weight_ref[0], (1, 0))
+    upward = dot(normed_ref[...], weight_ref[1], (1, 0))
+    hidden_grad = hidden_grad_ref[...]
+    sigma = jax.nn.sigmoid(gate)
+    swish = gate * sigma
+    hidden = (swish * upward).astype(jnp.bfloat16)
+    hidden_ref[...] = hidden
+    gate_grad = (hidden_grad * upward * sigma * (1.0 + gate * (1.0 - sigma))).astype(jnp.bfloat16)
+    upward_grad = (hidden_grad * swish).astype(jnp.bfloat16)
+    both = jnp.concatenate([gate_grad, upward_grad], 1)
+    weights = jnp.concatenate([weight_ref[0], weight_ref[1]], 1)
+    total[...] += dot(both, weights, (1, 1))
+    gate_up_grad_ref[0] = dot(turned[...], gate_grad, (1, 0)).astype(jnp.bfloat16)
+    gate_up_grad_ref[1] = dot(turned[...], upward_grad, (1, 0)).astype(jnp.bfloat16)
+    down_grad_ref[...] = dot(hidden.T, cotangent_ref[...], (1, 0)).astype(jnp.bfloat16)
+
+    @pl.when(step == pl.num_programs(0) - 1)
+    def _():
+        back_ref[...] = total[...].astype(jnp.bfloat16)
+
+
+def mlp(normed, weight, hidden_grad, cotangent):
+    rows, depth = normed.shape
+    width = weight.shape[2]
+    whole = pl.BlockSpec((rows, depth), lambda j: (0, 0), pipeline_mode=pl.Buffered(1))
+    return pl.pallas_call(
+        mlp_kernel,
+        out_shape=(
+            jax.ShapeDtypeStruct((rows, width), jnp.bfloat16),
+            jax.ShapeDtypeStruct((width, depth), jnp.bfloat16),
+            jax.ShapeDtypeStruct((2, depth, width), jnp.bfloat16),
+            jax.ShapeDtypeStruct((rows, depth), jnp.bfloat16),
+        ),
+        grid=(width // WIDE,),
+        in_specs=[
+            whole,
+            pl.BlockSpec((2, depth, WIDE), lambda j: (0, 0, j)),
+            pl.BlockSpec((rows, WIDE), lambda j: (0, j)),
+            whole,
+        ],
+        out_specs=(
+            pl.BlockSpec((rows, WIDE), lambda j: (0, j)),
+            pl.BlockSpec((WIDE, depth), lambda j: (j, 0)),
+            pl.BlockSpec((2, depth, WIDE), lambda j: (0, 0, j)),
+            pl.BlockSpec((rows, depth), lambda j: (0, 0)),
+        ),
+        scratch_shapes=[
+            pltpu.VMEM((depth, rows), jnp.bfloat16), pltpu.VMEM((rows, depth), jnp.float32),
+        ],
+        compiler_params=pltpu.CompilerParams(vmem_limit_bytes=60 * 2**20),
+        cost_estimate=pl.CostEstimate(
+            flops=14 * rows * depth * width, bytes_accessed=80 * 2**20, transcendentals=rows * width
+        ),
+        name="mlp",
+    )(normed, weight, hidden_grad, cotangent)
+
+
+def projection_back_kernel(
+    normed_ref, weight_ref, dq_ref, dk_ref, dv_ref, mixed_ref, middle_ref, grad_ref, back_ref,
+    turned, total,
+):
+    step = pl.program_id(0)
+
+    @pl.when(step == 0)
+    def _():
+        turned[...] = normed_ref[...].T
+
+    for at, ref in enumerate((dq_ref, dk_ref, dv_ref)):
+
+        @pl.when(step == at)
+        def _():
+            term = dot(ref[...], weight_ref[0], (1, 1))
+            if at == 0:
+                total[...] = term
+            elif at == 1:
+                total[...] += term
+            else:
+                back_ref[...] = (total[...] + term).astype(jnp.bfloat16)
+            grad_ref[0] = dot(turned[...], ref[...], (1, 0)).astype(jnp.bfloat16)
+
+    @pl.when(step == 3)
+    def _():
+        turned[...] = middle_ref[...].T
+        grad_ref[0] = dot(turned[...], mixed_ref[...], (1, 0)).astype(jnp.bfloat16)
+
+
+def projection_back(normed, weight, dq, dk, dv, mixed, middle):
+    rows, depth = normed.shape
+    width = dq.shape[1]
+    whole = lambda w: pl.BlockSpec((rows, w), lambda j: (0, 0), pipeline_mode=pl.Buffered(1))
+    return pl.pallas_call(
+        projection_back_kernel,
+        out_shape=(
+            jax.ShapeDtypeStruct((4, depth, width), jnp.bfloat16),
+            jax.ShapeDtypeStruct((rows, depth), jnp.bfloat16),
+        ),
+        grid=(4,),
+        in_specs=[
+            whole(depth),
+            pl.BlockSpec((1, depth, width), lambda j: (jnp.minimum(j, 2), 0, 0)),
+            whole(width), whole(width), whole(width), whole(width), whole(depth),
+        ],
+        out_specs=(
+            pl.BlockSpec((1, depth, width), lambda j: (j, 0, 0)),
+            pl.BlockSpec((rows, depth), lambda j: (0, 0)),
+        ),
+        scratch_shapes=[
+            pltpu.VMEM((depth, rows), jnp.bfloat16), pltpu.VMEM((rows, depth), jnp.float32),
+        ],
+        compiler_params=pltpu.CompilerParams(vmem_limit_bytes=60 * 2**20),
+        cost_estimate=pl.CostEstimate(
+            flops=14 * rows * depth * width, bytes_accessed=40 * 2**20, transcendentals=0
+        ),
+        name="projection_back",
+    )(normed, weight, dq, dk, dv, mixed, middle)
+
+
+def scatter_low(grad, axis=1):
     return lax.psum_scatter(
-        grad.astype(jnp.bfloat16), ("shard", "ctx"), scatter_dimension=1, tiled=True
+        grad.astype(jnp.bfloat16), ("shard", "ctx"), scatter_dimension=axis, tiled=True
     ).astype(jnp.float32)
 
 
@@ -656,87 +1015,46 @@
     out_low = out_weight.astype(jnp.bfloat16)
     gate_up_low = gate_up_weight.astype(jnp.bfloat16)
     down_low = down_weight.astype(jnp.bfloat16)
-    gains_low = norm_gains.astype(jnp.bfloat16)
-    qkv_full, out_full, gate_up_full, down_full, gains_full = (
-        lax.all_gather(qkv_low, ("shard", "ctx"), axis=1, tiled=True),
-        lax.all_gather(out_low, ("shard", "ctx"), axis=1, tiled=True),
-        lax.all_gather(gate_up_low, ("shard", "ctx"), axis=1, tiled=True),
-        lax.all_gather(down_low, ("shard", "ctx"), axis=1, tiled=True),
-        lax.all_gather(gains_low, ("shard", "ctx"), axis=1, tiled=True),
-    )
-    gain_one = gains_full[0:1].astype(jnp.float32)
-    gain_two = gains_full[1:2].astype(jnp.float32)
+    gains_low = norm_gains.astype(jnp.bfloat16).astype(jnp.float32)
+    gains_low = jnp.concatenate([gains_low] * 4, 0)
+    gather = lambda a: lax.all_gather(a, ("shard", "ctx"), axis=1, tiled=True)
+    qkv_full = gather(qkv_low)
+    both_full = gather(after(jnp.concatenate([out_low, down_low], 0), qkv_full))
     cosine, sine = rotation(query_index, HEAD)
     cosine, sine = (jnp.concatenate([c[:, 0]] * 4, 1) for c in (cosine, sine))
-    normed_one, query, keys, values, keys_prev, values_prev, mixed_low, totals = layer_front(
-        lengths, tokens, qkv_full, gain_one, cosine, sine
-    )
-    attn_part = jnp.dot(mixed_low, out_full, preferred_element_type=jnp.float32)
-    whole = jax.ShapeDtypeStruct(attn_part.shape, jnp.float32)
-    eight = jax.ShapeDtypeStruct((8, attn_part.shape[1]), jnp.float32)
-    normed_two, middle = run_chain(
-        middle_kernel, "sum_middle", 1, count,
-        [attn_part.astype(jnp.bfloat16), tokens, gain_two], [whole],
-    )
-    gate = jnp.dot(normed_two, gate_up_full[0], preferred_element_type=jnp.float32)
-    upward = jnp.dot(normed_two, gate_up_full[1], preferred_element_type=jnp.float32)
-    sigma = jax.nn.sigmoid(gate)
-    swish = gate * sigma
-    hidden = (swish * upward).astype(jnp.bfloat16)
-    mlp_part = jnp.dot(hidden, down_full, preferred_element_type=jnp.float32)
-    out_part = (middle + mlp_part).astype(jnp.bfloat16)
-    down_grad_local = outer_sum(hidden, cotangent).astype(jnp.bfloat16)
-    hidden_grad = back_dot(cotangent, down_full)
-    gate_grad = (hidden_grad * upward * sigma * (1.0 + gate * (1.0 - sigma))).astype(jnp.bfloat16)
-    upward_grad = (hidden_grad * swish).astype(jnp.bfloat16)
-    gate_up_grad_local = jnp.stack(
-        [outer_sum(normed_two, gate_grad), outer_sum(normed_two, upward_grad)]
-    ).astype(jnp.bfloat16)
-    mlp_back_part = (
-        back_dot(gate_grad, gate_up_full[0]) + back_dot(upward_grad, gate_up_full[1])
-    ).astype(jnp.bfloat16)
-    mlp_back_part, down_grad_local, gate_up_grad_local, out_part = lax.optimization_barrier(
-        (mlp_back_part, down_grad_local, gate_up_grad_local, out_part)
-    )
-    down_grad = scatter_low(down_grad_local)
-    middle_low, middle_grad, gain_two_grad = run_chain(
-        middle_back_kernel, "sum_middle_back", 2, count,
-        [mlp_back_part, middle, cotangent, gain_two], [whole, eight],
-    )
-    gate_up_grad = scatter_low(after(gate_up_grad_local, down_grad, middle_low))
-    out_grad_local = outer_sum(mixed_low, middle_low).astype(jnp.bfloat16)
-    mixed_grad = back_dot(middle_low, out_full).astype(jnp.bfloat16)
+    normed_one, query, keys, values, keys_prev, values_prev, mixed_low, totals, gains_full = layer_front(
+        lengths, tokens, qkv_full, gains_low, cosine, sine
+    )
+    gain_one, gain_two = gains_full[0:1], gains_full[1:2]
+    gate_up_full = gather(after(gate_up_low, both_full, totals))
+    normed_two, middle, hidden_grad = sum_middle(
+        mixed_low, both_full, tokens, gain_two, cotangent, count
+    )
+    hidden, down_grad_local, gate_up_grad_local, mlp_back_part = mlp(
+        normed_two, gate_up_full, hidden_grad, cotangent
+    )
+    gate_up_grad = scatter_low(gate_up_grad_local)
+    middle_low, middle_grad, gain_two_grad, out_part = sum_middle_back(
+        mlp_back_part, middle, cotangent, gain_two, hidden, both_full, count
+    )
+    down_grad = scatter_low(after(down_grad_local, gate_up_grad, middle_low))
+    mixed_grad = back_dot(middle_low, both_full[: mixed_low.shape[1]]).astype(jnp.bfloat16)
     query_low, key_low, value_low, out_tokens = attend_back(
         lengths,
         [query, keys, values, keys_prev, values_prev, mixed_low, mixed_grad, totals],
-        cosine, sine, out_part, count,
-    )
-    qkv_grad_local = jnp.stack(
-        [
-            outer_sum(normed_one, query_low),
-            outer_sum(normed_one, key_low),
-            outer_sum(normed_one, value_low),
-        ]
-    ).astype(jnp.bfloat16)
-    attn_back_part = (
-        back_dot(query_low, qkv_full[0])
-        + back_dot(key_low, qkv_full[1])
-        + back_dot(value_low, qkv_full[2])
-    ).astype(jnp.bfloat16)
-    attn_back_part, qkv_grad_local, out_grad_local, _ = lax.optimization_barrier(
-        (attn_back_part, qkv_grad_local, out_grad_local, gate_up_grad)
-    )
-    out_grad = scatter_low(out_grad_local)
-    qkv_grad = scatter_low(after(qkv_grad_local, out_grad))
-    input_grad, gain_one_grad = run_chain(
-        input_back_kernel, "sum_input_back", 3, count,
-        [attn_back_part, tokens, middle_grad, gain_one], [eight],
-    )
-    gains_local = lax.psum(
-        jnp.stack([gain_one_grad.sum(0), gain_two_grad.sum(0)]), ("shard", "ctx", "tp")
-    )
-    gains_grad = lax.dynamic_slice_in_dim(
-        gains_local, lax.axis_index(("shard", "ctx")) * norm_gains.shape[1], norm_gains.shape[1], 1
+        cosine, sine, out_part, middle, count,
+    )
+    qkv_grad_local, attn_back_part = projection_back(
+        normed_one, qkv_full, query_low, key_low, value_low, mixed_low, middle_low
+    )
+    attn_back_part, qkv_grad_local, _ = lax.optimization_barrier(
+        (attn_back_part, qkv_grad_local, down_grad)
+    )
+    qkv_grad = scatter_low(qkv_grad_local)
+    out_grad = qkv_grad[3].T
+    qkv_grad = qkv_grad[:3]
+    input_grad, gains_grad = sum_input_back(
+        attn_back_part, tokens, middle_grad, gain_one, gain_two_grad, norm_gains.shape[1], count
     )
     qkv_step, qkv_first_new, qkv_second_new = adam_update(
         qkv_weight, qkv_first, qkv_second, qkv_grad, decay_rate

time: 970 us -> 829 us (0.85)
  matrix products: 178 us -> 6.2 us
  Pallas kernels: 597 us -> 689 us
  blocking collectives: 52.6 us -> 0 us
  local copies, waits for them, and re-layouts: 7.34 us -> 19.1 us
  other arithmetic: 49.1 us -> 37.8 us
    dot_general x11 -> x0, matrix products: 107 us -> none  [the longest x7 49.7 us: outer_sum(): lax.dot_general(left, right, (((0,), (0,)), ((), ())), preferred_element_...]
    pallas_call x3 -> x5, Pallas kernels: 366 us -> 457 us  [the longest x3 358 us: chain_call(): pl.pallas_call(kernel, out_shape=out_shape, grid=(tick_count(rows, count)...]
    dot_general x7 -> x1, matrix products: 71.1 us -> 6.2 us  [back_dot(): lax.dot_general(grad, weight, (((1,), (1,)), ((), ())), preferred_element...]
    psum x1 -> x0, blocking collectives: 37.4 us -> none  [body(): lax.psum(jnp.stack([gain_one_grad.sum(0), gain_two_grad.sum(0)]), ('shard...]
    reduce_scatter x4 -> x3, waiting for transfers between devices: 42.8 us -> 9.07 us  [scatter_low(): lax.psum_scatter(grad.astype(jnp.bfloat16), ('shard', 'ctx'), scatter_dim...]
    all_gather x4 -> x3, waiting for transfers between devices: 21.8 us -> 46.8 us  [body(): gather = lambda a: lax.all_gather(a, ('shard', 'ctx'), axis=1, tiled=True)]
    pallas_call x1, Pallas kernels: 79.2 us -> 94.7 us  [layer_front(): pl.pallas_call(front_kernel, out_shape=outs, in_specs=[SMEM_SPEC] + [VMEM...]
    all_gather x1 -> x0, blocking collectives: 15.2 us -> none  [body(): lax.all_gather(gains_low, ('shard', 'ctx'), axis=1, tiled=True)]
  transfers between devices with their start and end apart: 8 -> 6, of which waited for: 2 -> 2; matrix products, arithmetic and copies ran while one was open for 8% -> 2% of each run, Pallas kernels for 62% -> 75%
where the time goes in v3:
time: 829 us; the launch traced here: 824 us
  Pallas kernels  689 us (83%)
  waiting for transfers between devices  56 us (7%)
  other arithmetic  37.8 us (5%)
  local copies, waits for them, and re-layouts  19.1 us (2%)
  between operations  15.5 us (2%)
    pallas_call x3, Pallas kernels, chain_call(): pl.pallas_call(kernel, out_shape=out_shape, grid=(tick_count(rows, count)...  358 us
    pallas_call x1, Pallas kernels, attend_back(): pl.pallas_call(functools.partial(attend_back_kernel, count), out_shape=ou...  137 us
    pallas_call x1, Pallas kernels, layer_front(): pl.pallas_call(front_kernel, out_shape=outs, in_specs=[SMEM_SPEC] + [VMEM...  94.7 us
    pallas_call x1, Pallas kernels, mlp(): pl.pallas_call(mlp_kernel, out_shape=(jax.ShapeDtypeStruct((rows, width),...  73.8 us
    all_gather x3, waiting for transfers between devices, body(): gather = lambda a: lax.all_gather(a, ('shard', 'ctx'), axis=1, tiled=True)  46.8 us
    pallas_call x1, Pallas kernels, projection_back(): pl.pallas_call(projection_back_kernel, out_shape=(jax.ShapeDtypeStruct((4...  24.8 us
    unnamed x40, local copies, waits for them, and re-layouts  16.7 us
  transfers between devices with their start and end apart: 6, of which 2 were waited for; matrix products, arithmetic and copies ran while one was open for 2% of the time, Pallas kernels for 75%

profile of v3, /device:TPU:0, one launch (start us, length us, event | category | flops | bytes accessed | tf_op | source)
XLA Modules:
  0.0 824.2 jit_solution(1147922063146503318)
XLA Ops:
  7.2 2.5 convert_element_type.35
  12.0 46.8 %all-gather.4.cloned.1.call-done.weight_ref = bf16[3,2048,512]{2,1,0:T(8,128)(2,1)} async-done(((bf16[3,256,512]{2,1,0:T(8,128)(2,1)}), bf16[3,2048,512]{2,1,0:T(8,128)(2,1)}) %all-gather.4.cloned.1.call-update) | async-done | bytes 6291472 | tf_op jit(solution)/shard_map/all_gather | solution.py:1020
  59.5 3.8 convert_element_type.40
  64.0 1.9 multiply_sine_fusion
  65.9 1.8 pad_maximum_fusion.1
  67.7 94.7 %layer_front.1 = (bf16[1024,2048]{1,0:T(8,128)(2,1)}, bf16[1024,512]{1,0:T(8,128)(2,1)}, bf16[1024,512]{1,0:T(8,128)(2,1)}, bf16[1024,512]{1,0:T(8,128)(2,1)}, b...) custom-call(s32[1]{0:T(128)S(6)} %copy.50.live_ref, ...), custom_call_target="tpu_custom_call" | custom-call | flops 80000000000 | bytes 41943040 | tf_op jit(solution)/shard_map/layer_front/pallas_call | solution.py:635
  162.9 1.5 fusion.15
  164.5 120.8 %sum_middle.1 = (bf16[1024,2048]{1,0:T(8,128)(2,1)}, f32[512,2048]{1,0:T(8,128)}, f32[1024,2048]{1,0:T(8,128)}) custom-call(bf16[1024,512]{1,0:T(8,128)(2,1)} %get-tuple-element.60.mixed_ref.o_ref, bf16[2560,2048]{1,0:T(8,128)(2,1)} %all-gather.6.cloned.1.call-done.weight_ref.down_ref, bf16[1024,2048]{1,0:T(8,128)(2,1)} %tokens_ref.5, ...), custom_call_target="tpu_custom_call" | custom-call | flops 99999997952 | bytes 25165824 | tf_op jit(solution)/shard_map/sum_middle/pallas_call | solution.py:377
  285.3 73.8 %mlp.1 = (bf16[1024,2048]{1,0:T(8,128)(2,1)}, bf16[2048,2048]{1,0:T(8,128)(2,1)}, bf16[2,2048,2048]{2,1,0:T(8,128)(2,1)}, bf16[1024,2048]{1,0:T(8,128)(2,1)}) custom-call(bf16[1024,2048]{1,0:T(8,128)(2,1)} %get-tuple-element.63.normed_ref, bf16[2,2048,2048]{2,1,0:T(8,128)(2,1)} %all-gather.8.cloned.1.call-done.weight_ref, ...), custom_call_target="tpu_custom_call" | custom-call | flops 60129542144 | bytes 83886080 | tf_op jit(solution)/shard_map/mlp/pallas_call | solution.py:879
  359.3 114.5 %sum_middle_back.1 = (bf16[1024,2048]{1,0:T(8,128)(2,1)}, f32[512,2048]{1,0:T(8,128)}, f32[8,2048]{1,0:T(8,128)}, bf16[1024,2048]{1,0:T(8,128)(2,1)}) custom-call(bf16[1024,2048]{1,0:T(8,128)(2,1)} %get-tuple-element.67.part_ref, f32[512,2048]{1,0:T(8,128)} %get-tuple-element.68.middle_ref, bf16[1024,2048]{1,0:T(8,128)(2,1)} %cotangent_ref.5, ...), custom_call_target="tpu_custom_call" | custom-call | flops 99999997952 | bytes 25165824 | tf_op jit(solution)/shard_map/sum_middle_back/pallas_call | solution.py:377
  473.8 9.0 %reduce-scatter.4.cloned.1.call-done = bf16[2,256,2048]{2,1,0:T(8,128)(2,1)} async-done(((bf16[2,2048,2048]{2,1,0:T(8,128)(2,1)}), bf16[2,256,2048]{2,1,0:T(8,128)(2,1)}) %reduce-scatter.4.cloned.1.call-update) | async-done | bytes 2097168 | tf_op jit(solution)/shard_map/reduce_scatter | solution.py:972
  482.9 10.2 %multiply_subtract_fusion = (f32[2,256,2048]{2,1,0:T(8,128)}, f32[2,256,2048]{2,1,0:T(8,128)}, f32[2,256,2048]{2,1,0:T(8,128)}, f32[2,256,2048]{2,1,0:T(8,128)}) fusion(f32[2,256,2048]{2,1,0:T(8,128)} %param.23, f32[2,256,2048]{2,1,0:T(8,128)} %param.28, f32[2,256,2048]{2,1,0:T(8,128)} %param.33, bf16[2,256,2048]{2,1,0:T(8,128)(2,1)} %reduce-scatter.4.cloned.1.call-done), kind=kLoop, calls=%fused_computation.2 | loop fusion | flops 16777216 | bytes 31457280 | tf_op jit(solution)/shard_map/sub | solution.py:1075
  493.1 6.2 fusion.5.do_ref
  499.3 137.2 %attend_back.1 = (bf16[1024,512]{1,0:T(8,128)(2,1)}, bf16[1024,512]{1,0:T(8,128)(2,1)}, bf16[1024,512]{1,0:T(8,128)(2,1)}, bf16[1024,2048]{1,0:T(8,128)(2,1)}) custom-call(s32[1]{0:T(128)S(6)} %copy.50.live_ref, bf16[1024,512]{1,0:T(8,128)(2,1)} %get-tuple-element.55.q_ref, bf16[1024,512]{1,0:T(8,128)(2,1)} %get-tuple-element.56.k_ref, ...), custom_call_target="tpu_custom_call" | custom-call | flops 99999997952 | bytes 41943040 | tf_op jit(solution)/shard_map/attend_back/pallas_call | solution.py:814
  636.6 24.8 %projection_back.1 = (bf16[4,2048,512]{2,1,0:T(8,128)(2,1)}, bf16[1024,2048]{1,0:T(8,128)(2,1)}) custom-call(bf16[1024,2048]{1,0:T(8,128)(2,1)} %get-tuple-element.73.normed_ref, bf16[3,2048,512]{2,1,0:T(8,128)(2,1)} %all-gather.4.cloned.1.call-done.weight_ref, bf16[1024,512]{1,0:T(8,128)(2,1)} %get-tuple-element.74.dq_ref, ...), custom_call_target="tpu_custom_call" | custom-call | flops 15032385536 | bytes 41943040 | tf_op jit(solution)/shard_map/projection_back/pallas_call | solution.py:944
  661.5 6.3 multiply_subtract_fusion.1
  670.1 123.0 %sum_input_back.1 = (bf16[1024,2048]{1,0:T(8,128)(2,1)}, f32[2,256]{1,0:T(2,128)}) custom-call(bf16[1024,2048]{1,0:T(8,128)(2,1)} %get-tuple-element.82.part_ref, bf16[1024,2048]{1,0:T(8,128)(2,1)} %tokens_ref.5, f32[512,2048]{1,0:T(8,128)} %get-tuple-element.83.grad_ref, f32[1,2048]{1,0:T(1,128)} %get-tuple-element.128.gain_ref, ...), custom_call_target="tpu_custom_call" | custom-call | flops 99999997952 | bytes 25165824 | tf_op jit(solution)/shard_map/sum_input_back/pallas_call | solution.py:377
  798.1 2.2 copy.44
  800.2 2.0 copy.45
  803.3 2.0 copy.43
  805.3 5.3 multiply_subtract_fusion.2
  810.6 2.1 copy.51
  812.8 1.6 copy-done.5
  814.3 2.0 copy.52
  (61 shorter events, 12.6 us)
Async XLA Ops:
  7.2 2.7 copy-start
  7.2 51.6 %all-gather.4.cloned.1.call-start = ((), (), s32[]{:S(2)}) async-start(), calls=%async_computation.3 | async-start | bytes 7077888 | tf_op jit(solution)/shard_map/all_gather | solution.py:1020
  9.8 1.0 copy-start.6
  9.8 152.7 %all-gather.6.cloned.1.call-start = ((), (), s32[]{:S(2)}) async-start(), calls=%async_computation.4 | async-start | bytes 11796480 | tf_op jit(solution)/shard_map/all_gather | solution.py:1020
  10.8 48.6 %copy-start.10 = (f32[2,256]{1,0:T(2,128)S(1)}, f32[2,256]{1,0:T(2,128)}, u32[]{:S(2)}) copy-start(f32[2,256]{1,0:T(2,128)} %param.25) | copy-start | bytes 6148
  58.8 226.5 %all-gather.8.cloned.1.call-start = ((), (), s32[]{:S(2)}) async-start(), calls=%async_computation.5 | async-start | bytes 18874368 | tf_op jit(solution)/shard_map/all_gather | solution.py:1020
  162.5 320.4 %reduce-scatter.4.cloned.1.call-start = ((), (), s32[]{:S(2)}) async-start(), calls=%async_computation.6 | async-start | bytes 18874368 | tf_op jit(solution)/shard_map/reduce_scatter | solution.py:972
  359.1 302.4 %reduce-scatter.6.cloned.1.call-start = ((), (), s32[]{:S(2)}) async-start(), calls=%async_computation.7 | async-start | bytes 9437184 | tf_op jit(solution)/shard_map/reduce_scatter | solution.py:972
  493.1 301.3 %reduce-scatter.8.cloned.1.call-start = ((), (), s32[]{:S(2)}) async-start(), calls=%async_computation.8 | async-start | bytes 9437184 | tf_op jit(solution)/shard_map/reduce_scatter | solution.py:972
  636.6 24.9 %copy-start.1 = (f32[2048,256]{1,0:T(8,128)S(1)}, f32[2048,256]{1,0:T(8,128)}, u32[]{:S(2)}) copy-start(f32[2048,256]{1,0:T(8,128)} %param.24) | copy-start | bytes 6291460
  667.7 1.0 copy-start.7
  667.7 1.2 copy-start.8
  668.8 1.1 copy-start.9
  670.1 123.0 %copy-start.11 = (f32[2,256]{1,0:T(2,128)S(1)}, f32[2,256]{1,0:T(2,128)}, u32[]{:S(2)}) copy-start(f32[2,256]{1,0:T(2,128)} %param.25) | copy-start | bytes 6148
  670.1 123.0 %copy-start.13 = (f32[2,256]{1,0:T(2,128)S(1)}, f32[2,256]{1,0:T(2,128)}, u32[]{:S(2)}) copy-start(f32[2,256]{1,0:T(2,128)} %param.30) | copy-start | bytes 6148
  670.1 123.0 %copy-start.14 = (f32[2,256]{1,0:T(2,128)S(1)}, f32[2,256]{1,0:T(2,128)}, u32[]{:S(2)}) copy-start(f32[2,256]{1,0:T(2,128)} %param.35) | copy-start | bytes 6148
  798.1 7.3 copy-start.2
  798.1 7.3 copy-start.3
  805.3 5.3 copy-start.4
  810.6 3.7 copy-start.5
  814.3 2.0 copy-start.12
Sparse Core Ops, SparseCore 0:
  10.5 48.2 all-gather.3
  61.2 88.8 all-gather.5
  162.6 99.4 all-gather.7
  359.2 123.6 reduce-scatter.3
  493.2 104.7 reduce-scatter.5
  667.9 70.9 reduce-scatter.7

commit v4 on v3

--- a/solution.py
+++ b/solution.py
@@ -11,15 +11,17 @@
 BLOCK = 256
 CHUNK = 16
 LAG = 2
-BACK_CHUNK = 16
-BACK_LAG = 4
+BACK_CHUNK = 32
+BACK_LAG = 3
 WIDE = 256
-BACK_TICKS = 2
 SPACING = 5
+LEAD = 1
+MLP_WIDE = 256
 MASKED = -1e30
 MESH = pl.DeviceIdType.MESH
 VMEM_SPEC = pl.BlockSpec(memory_space=pltpu.VMEM)
 SMEM_SPEC = pl.BlockSpec(memory_space=pltpu.SMEM)
+HBM_SPEC = pl.BlockSpec(memory_space=pl.ANY)
 
 
 norm_eps = 1e-05
@@ -39,12 +41,6 @@
     return (jnp.cos(angle)[:, None, :], jnp.sin(angle)[:, None, :])
 
 
-def back_dot(grad, weight):
-    return lax.dot_general(
-        grad, weight, (((1,), (1,)), ((), ())), preferred_element_type=jnp.float32
-    )
-
-
 def dot(left, right, contract):
     return lax.dot_general(
         left, right, ((contract[:1], contract[1:]), ((), ())), preferred_element_type=jnp.float32
@@ -90,7 +86,7 @@
         pl.semaphore_wait(barrier, 1 + more + more_ends)
 
 
-def chain_parts(count, part_ref, out_ref, slots, send, recv, finish, size, lag=1, land=None):
+def chain_parts(count, part_ref, out_ref, slots, send, recv, finish, size, lag=1, land=None, stored=None):
     me = lax.axis_index("tp")
     apart = land is not None
     land = land if apart else out_ref
@@ -117,6 +113,10 @@
         rows = pl.ds(pl.multiple_of(base + at * size, size), size)
         return copy(2 if way == 1 else 3, at, land.at[rows], land.at[rows], device)
 
+    def store_copy(index, at):
+        rows = pl.ds(pl.multiple_of(index * half + at * size, size), size)
+        return pltpu.make_async_copy(land.at[rows], out_ref.at[rows], stored.at[index, at])
+
     def reduce_step(way, tick):
         place, ahead = ends(way)
         index = 0 if way == 1 else 1
@@ -149,9 +149,9 @@
             @pl.when(place == count - 1)
             def _():
                 total = slots[index, local].astype(jnp.float32) + part_ref[rows].astype(jnp.float32)
-                land[rows] = finish(rows, local, total)
+                land[rows] = finish(rows, local, total, at)
                 if apart:
-                    out_ref[rows] = land[rows]
+                    store_copy(1 if way == 1 else 0, at).start()
                 spread_copy(-way, at, me - way).start()
 
     def spread_step(way, tick):
@@ -167,9 +167,7 @@
                 spread_copy(way, at, ahead).start()
 
             if apart:
-                base = 0 if way == 1 else half
-                rows = pl.ds(pl.multiple_of(base + at * size, size), size)
-                out_ref[rows] = land[rows]
+                store_copy(0 if way == 1 else 1, at).start()
 
     def step(tick):
         for way in (1, -1):
@@ -180,6 +178,10 @@
     def drain():
         @pl.loop(0, chunks)
         def _(at):
+            if apart:
+                for index in range(2):
+                    store_copy(index, at).wait()
+
             for way in (1, -1):
                 place, ahead = ends(way)
 
@@ -191,12 +193,18 @@
     return step, drain, chunks + 2 * lag * (count - 1)
 
 
-def run_ticks(parts, start):
+def run_ticks(parts, start, wait, finally_drain):
     step, drain, ticks = parts
     tick = pl.program_id(0)
     pl.when(tick == 0)(start)
+    pl.when(tick == SPACING - 2)(wait)
     step(tick)
-    pl.when(tick == ticks - 1)(drain)
+
+    @pl.when(tick == ticks - 1)
+    def _():
+        drain()
+        finally_drain()
+
     return tick
 
 
@@ -220,11 +228,51 @@
     return grad, gain_grad
 
 
+def loads_of(pairs, sems):
+    copies = [
+        pltpu.make_async_copy(source, target, sems.at[at])
+        for at, (source, target) in enumerate(pairs)
+    ]
+
+    def start():
+        for copy in copies:
+            copy.start()
+
+    def wait():
+        for copy in copies:
+            copy.wait()
+
+    return start, wait
+
+
+def half_store(source, target, sems, count):
+    chunks = source.shape[0] // CHUNK
+    me = lax.axis_index("tp")
+
+    def copy(at):
+        rows = pl.ds(pl.multiple_of(at * CHUNK, CHUNK), CHUNK)
+        return pltpu.make_async_copy(source.at[rows], target.at[rows], sems.at[at])
+
+    def drain():
+        @pl.when((me == 0) | (me == count - 1))
+        def _():
+            @pl.loop(0, chunks)
+            def _(at):
+                copy(at).wait()
+
+    return copy, drain
+
+
 def middle_kernel(
-    count, blocks, mixed_ref, weight_ref, tokens_ref, gain_ref, cotangent_ref, down_ref,
-    out_ref, middle_ref, hidden_grad_ref, slots, land, part_ref, send, recv,
+    count, blocks, mixed_ref, weight_ref, tokens_hbm, gain_ref, cotangent_hbm, down_ref,
+    out_ref, middle_ref, hidden_grad_ref,
+    slots, land, send, recv, stored, part_ref, tokens_ref, cotangent_ref, middle, load_sem, half_sem,
 ):
+    load, wait = loads_of([(tokens_hbm, tokens_ref), (cotangent_hbm, cotangent_ref)], load_sem)
+    half_copy, half_drain = half_store(middle, middle_ref, half_sem, count)
+
     def start():
+        load()
         greet(lax.axis_index("tp"), count)
 
         @pl.loop(0, part_ref.shape[0] // BLOCK)
@@ -232,53 +280,72 @@
             here = pl.ds(pl.multiple_of(at * BLOCK, BLOCK), BLOCK)
             part_ref[here] = dot(mixed_ref[here], weight_ref[...], (1, 0)).astype(jnp.bfloat16)
 
-    def finish(rows, local, total):
-        middle = tokens_ref[rows].astype(jnp.float32) + total
-        middle_ref[local] = middle
-        return (middle * unit_scale(middle) * gain_ref[...]).astype(jnp.bfloat16)
-
-    parts = chain_parts(count, part_ref, out_ref, slots, send, recv, finish, CHUNK, LAG, land)
-    tick = run_ticks(parts, start)
-
-    @pl.when((tick % SPACING == 1) & (tick < blocks * SPACING))
+    def finish(rows, local, total, at):
+        value = tokens_ref[rows].astype(jnp.float32) + total
+        middle[local] = value
+        half_copy(at).start()
+        return (value * unit_scale(value) * gain_ref[...]).astype(jnp.bfloat16)
+
+    parts = chain_parts(
+        count, part_ref, out_ref, slots, send, recv, finish, CHUNK, LAG, land, stored
+    )
+    tick = run_ticks(parts, start, wait, half_drain)
+
+    @pl.when((tick % SPACING == SPACING - 1) & (tick < blocks * SPACING))
     def _():
         hidden_grad_ref[...] = dot(cotangent_ref[...], down_ref[...], (1, 1))
 
 
 def middle_back_kernel(
-    count, part_ref, middle_ref, cotangent_ref, gain_ref, hidden_ref, down_ref,
-    out_ref, grad_ref, gain_grad_ref, layer_ref, slots, land, send, recv,
+    count, part_ref, middle_hbm, cotangent_hbm, gain_ref, hidden_hbm, down_ref,
+    out_ref, grad_ref, gain_grad_ref, layer_ref,
+    slots, land, send, recv, stored, middle_ref, cotangent_ref, hidden_ref, grad, load_sem, half_sem,
 ):
+    load, wait = loads_of(
+        [(middle_hbm, middle_ref), (cotangent_hbm, cotangent_ref), (hidden_hbm, hidden_ref)],
+        load_sem,
+    )
+    half_copy, half_drain = half_store(grad, grad_ref, half_sem, count)
+
     def start():
+        load()
         greet(lax.axis_index("tp"), count)
         gain_grad_ref[...] = jnp.zeros_like(gain_grad_ref)
 
-    def finish(rows, local, total):
-        grad, gain_grad = norm_back(middle_ref[local], gain_ref[...], total)
+    def finish(rows, local, total, at):
+        value, gain_grad = norm_back(middle_ref[local], gain_ref[...], total)
         gain_grad_ref[...] += gain_grad
-        grad = cotangent_ref[rows].astype(jnp.float32) + grad
-        grad_ref[local] = grad
-        return grad.astype(jnp.bfloat16)
-
-    parts = chain_parts(count, part_ref, out_ref, slots, send, recv, finish, CHUNK, LAG, land)
-    tick = run_ticks(parts, start)
-
-    @pl.when((tick % SPACING == 1) & (tick < part_ref.shape[1] // WIDE * SPACING))
+        value = cotangent_ref[rows].astype(jnp.float32) + value
+        grad[local] = value
+        half_copy(at).start()
+        return value.astype(jnp.bfloat16)
+
+    parts = chain_parts(
+        count, part_ref, out_ref, slots, send, recv, finish, CHUNK, LAG, land, stored
+    )
+    tick = run_ticks(parts, start, wait, half_drain)
+
+    @pl.when((tick % SPACING == SPACING - 1) & (tick < part_ref.shape[1] // WIDE * SPACING))
     def _():
         skip = down_ref.shape[0] - hidden_ref.shape[1]
         layer_ref[...] = dot(hidden_ref[...], down_ref[skip:], (1, 0)).astype(jnp.bfloat16)
 
 
 def input_back_kernel(
-    count, part_ref, tokens_ref, grad_ref, gain_ref, other_ref,
-    out_ref, gains_ref, slots, land, local, landed, along, send, recv, plane_send, plane_recv, line_send, line_recv,
+    count, part_ref, tokens_hbm, grad_hbm, gain_ref, other_ref, out_ref, gains_ref,
+    slots, land, send, recv, stored, tokens_ref, grad_ref, local, landed, along,
+    load_sem, plane_send, plane_recv, line_send, line_recv,
 ):
+    load, wait = loads_of([(tokens_hbm, tokens_ref), (grad_hbm, grad_ref)], load_sem)
+
     me = lax.axis_index("tp")
     size, index, peer = plane_peers()
     width = gains_ref.shape[1]
     last = (me == 0) | (me == count - 1)
 
     def start():
+        load()
+
         @pl.when(last)
         def _():
             greet_plane(size, peer)
@@ -287,13 +354,13 @@
         local[0:8] = jnp.zeros((8, local.shape[1]), jnp.float32)
         local[8:16] = other_ref[...]
 
-    def finish(rows, part, total):
+    def finish(rows, part, total, at):
         grad, gain_grad = norm_back(tokens_ref[rows].astype(jnp.float32), gain_ref[...], total)
         local[0:8] += gain_grad
         return (grad_ref[part] + grad).astype(jnp.bfloat16)
 
     step, drain, ticks = chain_parts(
-        count, part_ref, out_ref, slots, send, recv, finish, CHUNK, LAG, land
+        count, part_ref, out_ref, slots, send, recv, finish, CHUNK, LAG, land, stored
     )
 
     def columns(at):
@@ -319,6 +386,7 @@
 
     tick = pl.program_id(0)
     pl.when(tick == 0)(start)
+    pl.when(tick == SPACING - 2)(wait)
     step(tick)
 
     @pl.when(last & (tick == done - 1))
@@ -343,19 +411,19 @@
             along[1] = total
             line_copy(-1).start()
 
-    @pl.when(tick == ticks - 1)
-    def _():
-        for way in (1, -1):
-            place = me if way == 1 else count - 1 - me
-
-            @pl.when(place > 0)
-            def _():
-                line_copy(way).wait_recv()
-
-            @pl.when((place > 0) & (place < count - 1))
+    for way in (1, -1):
+        place = me if way == 1 else count - 1 - me
+
+        @pl.when((place > 0) & (tick == jnp.minimum(done + LAG + place, ticks - 1)))
+        def _():
+            line_copy(way).wait_recv()
+
+            @pl.when(place < count - 1)
             def _():
                 line_copy(way).start()
 
+    @pl.when(tick == ticks - 1)
+    def _():
         for way in (1, -1):
             place = me if way == 1 else count - 1 - me
 
@@ -383,10 +451,10 @@
         scratch_shapes=[
             pltpu.VMEM((2, rows // 2, width), jnp.bfloat16),
             pltpu.VMEM((rows, width), jnp.bfloat16),
-            *scratch[:3],
             pltpu.SemaphoreType.DMA((4, chunks)),
             pltpu.SemaphoreType.DMA((4, chunks)),
-            *scratch[3:],
+            pltpu.SemaphoreType.DMA((2, chunks)),
+            *scratch,
         ],
         compiler_params=pltpu.CompilerParams(
             collective_id=number, has_side_effects=True, vmem_limit_bytes=60 * 2**20
@@ -396,6 +464,10 @@
         ),
         name=name,
     )(*arrays)
+
+
+def far(shape, dtype):
+    return jax.ShapeDtypeStruct(shape, dtype), HBM_SPEC
 
 
 def kept(shape, dtype):
@@ -413,18 +485,23 @@
         [
             (mixed, VMEM_SPEC),
             (both, pl.BlockSpec((inner, width), lambda i: (0, 0), pipeline_mode=pl.Buffered(1))),
-            (tokens, VMEM_SPEC), (gain, VMEM_SPEC), (cotangent, VMEM_SPEC),
+            (tokens, HBM_SPEC), (gain, VMEM_SPEC), (cotangent, HBM_SPEC),
             (both, pl.BlockSpec((WIDE, width), lambda i: (inner // WIDE + at(i), 0))),
         ],
         [
-            kept(tokens.shape, jnp.bfloat16),
-            kept((rows // 2, width), jnp.float32),
+            far(tokens.shape, jnp.bfloat16),
+            far((rows // 2, width), jnp.float32),
             (
                 jax.ShapeDtypeStruct((rows, hidden), jnp.float32),
                 pl.BlockSpec((rows, WIDE), lambda i: (0, at(i))),
             ),
         ],
-        [pltpu.VMEM(tokens.shape, jnp.bfloat16)],
+        [
+            *[pltpu.VMEM(tokens.shape, jnp.bfloat16)] * 3,
+            pltpu.VMEM((rows // 2, width), jnp.float32),
+            pltpu.SemaphoreType.DMA((2,)),
+            pltpu.SemaphoreType.DMA((rows // 2 // CHUNK,)),
+        ],
     )
 
 
@@ -435,19 +512,26 @@
     return chain_call(
         functools.partial(middle_back_kernel, count), "sum_middle_back", 2, count, part.shape,
         [
-            (part, VMEM_SPEC), (middle, VMEM_SPEC), (cotangent, VMEM_SPEC), (gain, VMEM_SPEC),
-            (hidden, VMEM_SPEC), (both, pl.BlockSpec((both.shape[0], WIDE), lambda i: (0, at(i)))),
+            (part, VMEM_SPEC), (middle, HBM_SPEC), (cotangent, HBM_SPEC), (gain, VMEM_SPEC),
+            (hidden, HBM_SPEC), (both, pl.BlockSpec((both.shape[0], WIDE), lambda i: (0, at(i)))),
         ],
         [
-            kept(part.shape, jnp.bfloat16),
-            kept((rows // 2, width), jnp.float32),
+            far(part.shape, jnp.bfloat16),
+            far((rows // 2, width), jnp.float32),
             kept((8, width), jnp.float32),
             (
                 jax.ShapeDtypeStruct(part.shape, jnp.bfloat16),
                 pl.BlockSpec((rows, WIDE), lambda i: (0, at(i))),
             ),
         ],
-        [],
+        [
+            pltpu.VMEM((rows // 2, width), jnp.float32),
+            pltpu.VMEM(part.shape, jnp.bfloat16),
+            pltpu.VMEM(hidden.shape, jnp.bfloat16),
+            pltpu.VMEM((rows // 2, width), jnp.float32),
+            pltpu.SemaphoreType.DMA((3,)),
+            pltpu.SemaphoreType.DMA((rows // 2 // CHUNK,)),
+        ],
     )
 
 
@@ -456,12 +540,18 @@
     plane = width // size
     return chain_call(
         functools.partial(input_back_kernel, count), "sum_input_back", 3, count, part.shape,
-        [(a, VMEM_SPEC) for a in (part, tokens, grad, gain, other)],
-        [kept(part.shape, jnp.bfloat16), kept((2, size), jnp.float32)],
         [
+            (part, VMEM_SPEC), (tokens, HBM_SPEC), (grad, HBM_SPEC), (gain, VMEM_SPEC),
+            (other, VMEM_SPEC),
+        ],
+        [far(part.shape, jnp.bfloat16), kept((2, size), jnp.float32)],
+        [
+            pltpu.VMEM(part.shape, jnp.bfloat16),
+            pltpu.VMEM(grad.shape, jnp.float32),
             pltpu.VMEM((16, width), jnp.float32),
             pltpu.VMEM((plane, 16, size), jnp.float32),
             pltpu.VMEM((2, 16, size), jnp.float32),
+            pltpu.SemaphoreType.DMA((2,)),
             pltpu.SemaphoreType.DMA((plane,)),
             pltpu.SemaphoreType.DMA((plane,)),
             pltpu.SemaphoreType.DMA((2,)),
@@ -650,9 +740,9 @@
 
 
 def attend_back_kernel(
-    count, live_ref, q_ref, k_ref, v_ref, kp_ref, vp_ref, o_ref, do_ref, l_ref, cos_ref, sin_ref,
-    part_ref, middle_ref, dq_ref, dk_ref, dv_ref, out_ref,
-    dq_acc, dk_acc, dv_acc, dkp_acc, dvp_acc, leave, arrive, slots, send, recv, chain_send, chain_recv,
+    count, live_ref, q_ref, k_ref, v_ref, kp_ref, vp_ref, o_ref, l_ref, cos_ref, sin_ref,
+    part_ref, middle_ref, grad_ref, weight_ref, dq_ref, dk_ref, dv_ref, out_ref,
+    do_ref, dq_acc, dk_acc, dv_acc, dkp_acc, dvp_acc, leave, arrive, slots, send, recv, chain_send, chain_recv,
 ):
     late = lax.axis_index("ctx")
     me = lax.axis_index("tp")
@@ -665,7 +755,7 @@
     greet(me, count, 1)
     tick, drain, ticks = chain_parts(
         count, part_ref, out_ref, slots, chain_send, chain_recv,
-        lambda rows, part, total: (middle_ref[part] + total).astype(jnp.bfloat16), BACK_CHUNK, BACK_LAG,
+        lambda rows, part, total, at: (middle_ref[part] + total).astype(jnp.bfloat16), BACK_CHUNK, BACK_LAG,
     )
 
     def here(at):
@@ -762,15 +852,20 @@
     def _():
         dq_acc[...] = jnp.zeros_like(dq_acc)
 
+    @pl.loop(0, blocks)
+    def _(at):
+        for more in range(LEAD):
+            tick(at * LEAD + more)
+        do_ref[here(at)] = dot(grad_ref[here(at)], weight_ref[...], (1, 1)).astype(jnp.bfloat16)
+
     steps = pairs * blocks
+    lead = blocks * LEAD
 
     @pl.loop(0, 2 * steps)
     def _(at):
-        for more in range(BACK_TICKS):
-
-            @pl.when(at * BACK_TICKS + more < ticks)
-            def _():
-                tick(at * BACK_TICKS + more)
+        @pl.when(lead + at < ticks)
+        def _():
+            tick(lead + at)
 
         @pl.when((late == 1) & (at < steps))
         def _():
@@ -780,8 +875,8 @@
         def _():
             own_step((at - steps) // blocks, at % blocks)
 
-    if ticks > 2 * steps * BACK_TICKS:
-        pl.loop(2 * steps * BACK_TICKS, ticks)(tick)
+    if ticks > lead + 2 * steps:
+        pl.loop(lead + 2 * steps, ticks)(tick)
 
     @pl.loop(0, pairs)
     def _(pair):
@@ -805,18 +900,21 @@
     drain()
 
 
-def attend_back(live, arrays, cosine, sine, out_part, middle, count):
+def attend_back(live, arrays, cosine, sine, out_part, middle, grad, both, count):
     rows, width = arrays[0].shape
     pairs = width // PAIR
     part = jax.ShapeDtypeStruct((rows, width), jnp.bfloat16)
-    outs = (part, part, part, jax.ShapeDtypeStruct(out_part.shape, jnp.bfloat16))
+    outs = (
+        part, part, part, jax.ShapeDtypeStruct(out_part.shape, jnp.bfloat16),
+    )
     chunks = rows // 2 // BACK_CHUNK
     return pl.pallas_call(
         functools.partial(attend_back_kernel, count),
         out_shape=outs,
-        in_specs=[SMEM_SPEC] + [VMEM_SPEC] * 12,
+        in_specs=[SMEM_SPEC] + [VMEM_SPEC] * 13,
         out_specs=(VMEM_SPEC,) * len(outs),
         scratch_shapes=[
+            pltpu.VMEM((rows, width), jnp.bfloat16),
             pltpu.VMEM((pairs, PAIR, rows), jnp.float32),
             pltpu.VMEM((rows, width), jnp.float32),
             pltpu.VMEM((rows, width), jnp.float32),
@@ -837,7 +935,31 @@
             flops=100 * 10**9, bytes_accessed=40 * 2**20, transcendentals=0
         ),
         name="attend_back",
-    )(live, *arrays, cosine, sine, out_part, middle)
+    )(live, *arrays, cosine, sine, out_part, middle, grad, both)
+
+
+def narrow_kernel(out_ref, down_ref, gate_up_ref, both_ref, low_ref):
+    split = out_ref.shape[0]
+    both_ref[:split] = out_ref[...].astype(jnp.bfloat16)
+    both_ref[split:] = down_ref[...].astype(jnp.bfloat16)
+    low_ref[...] = gate_up_ref[...].astype(jnp.bfloat16)
+
+
+def narrow(out_weight, down_weight, gate_up_weight):
+    return pl.pallas_call(
+        narrow_kernel,
+        out_shape=(
+            jax.ShapeDtypeStruct(
+                (out_weight.shape[0] + down_weight.shape[0], out_weight.shape[1]), jnp.bfloat16
+            ),
+            jax.ShapeDtypeStruct(gate_up_weight.shape, jnp.bfloat16),
+        ),
+        in_specs=[VMEM_SPEC] * 3,
+        out_specs=(VMEM_SPEC,) * 2,
+        compiler_params=pltpu.CompilerParams(vmem_limit_bytes=40 * 2**20),
+        cost_estimate=pl.CostEstimate(flops=40 * 10**9, bytes_accessed=2**24, transcendentals=0),
+        name="narrow",
+    )(out_weight, down_weight, gate_up_weight)
 
 
 def mlp_kernel(
@@ -884,17 +1006,17 @@
             jax.ShapeDtypeStruct((2, depth, width), jnp.bfloat16),
             jax.ShapeDtypeStruct((rows, depth), jnp.bfloat16),
         ),
-        grid=(width // WIDE,),
+        grid=(width // MLP_WIDE,),
         in_specs=[
             whole,
-            pl.BlockSpec((2, depth, WIDE), lambda j: (0, 0, j)),
-            pl.BlockSpec((rows, WIDE), lambda j: (0, j)),
+            pl.BlockSpec((2, depth, MLP_WIDE), lambda j: (0, 0, j)),
+            pl.BlockSpec((rows, MLP_WIDE), lambda j: (0, j)),
             whole,
         ],
         out_specs=(
-            pl.BlockSpec((rows, WIDE), lambda j: (0, j)),
-            pl.BlockSpec((WIDE, depth), lambda j: (j, 0)),
-            pl.BlockSpec((2, depth, WIDE), lambda j: (0, 0, j)),
+            pl.BlockSpec((rows, MLP_WIDE), lambda j: (0, j)),
+            pl.BlockSpec((MLP_WIDE, depth), lambda j: (j, 0)),
+            pl.BlockSpec((2, depth, MLP_WIDE), lambda j: (0, 0, j)),
             pl.BlockSpec((rows, depth), lambda j: (0, 0)),
         ),
         scratch_shapes=[
@@ -1012,14 +1134,12 @@
     offset = lax.axis_index("ctx") * row_count
     query_index = offset + jnp.arange(row_count, dtype=jnp.int32)
     qkv_low = qkv_weight.astype(jnp.bfloat16)
-    out_low = out_weight.astype(jnp.bfloat16)
-    gate_up_low = gate_up_weight.astype(jnp.bfloat16)
-    down_low = down_weight.astype(jnp.bfloat16)
+    both_low, gate_up_low = narrow(out_weight, down_weight, gate_up_weight)
     gains_low = norm_gains.astype(jnp.bfloat16).astype(jnp.float32)
     gains_low = jnp.concatenate([gains_low] * 4, 0)
     gather = lambda a: lax.all_gather(a, ("shard", "ctx"), axis=1, tiled=True)
     qkv_full = gather(qkv_low)
-    both_full = gather(after(jnp.concatenate([out_low, down_low], 0), qkv_full))
+    both_full = gather(after(both_low, qkv_full))
     cosine, sine = rotation(query_index, HEAD)
     cosine, sine = (jnp.concatenate([c[:, 0]] * 4, 1) for c in (cosine, sine))
     normed_one, query, keys, values, keys_prev, values_prev, mixed_low, totals, gains_full = layer_front(
@@ -1038,11 +1158,10 @@
         mlp_back_part, middle, cotangent, gain_two, hidden, both_full, count
     )
     down_grad = scatter_low(after(down_grad_local, gate_up_grad, middle_low))
-    mixed_grad = back_dot(middle_low, both_full[: mixed_low.shape[1]]).astype(jnp.bfloat16)
     query_low, key_low, value_low, out_tokens = attend_back(
         lengths,
-        [query, keys, values, keys_prev, values_prev, mixed_low, mixed_grad, totals],
-        cosine, sine, out_part, middle, count,
+        [query, keys, values, keys_prev, values_prev, mixed_low, totals],
+        cosine, sine, out_part, middle, middle_low, both_full[: mixed_low.shape[1]], count,
     )
     qkv_grad_local, attn_back_part = projection_back(
         normed_one, qkv_full, query_low, key_low, value_low, mixed_low, middle_low
@@ -1051,7 +1170,7 @@
         (attn_back_part, qkv_grad_local, down_grad)
     )
     qkv_grad = scatter_low(qkv_grad_local)
-    out_grad = qkv_grad[3].T
+    out_grad = lax.optimization_barrier(qkv_grad[3].T)
     qkv_grad = qkv_grad[:3]
     input_grad, gains_grad = sum_input_back(
         attn_back_part, tokens, middle_grad, gain_one, gain_two_grad, norm_gains.shape[1], count

time: 829 us -> 818 us (0.987)
    pallas_call x3, Pallas kernels: 358 us -> 343 us  [chain_call(): pl.pallas_call(kernel, out_shape=out_shape, grid=(tick_count(rows, count)...]
where the time goes in v4:
time: 818 us; the launch traced here: 813 us
  Pallas kernels  681 us (83%)
  waiting for transfers between devices  57.7 us (7%)
  other arithmetic  34 us (4%)
  local copies, waits for them, and re-layouts  24.8 us (3%)
  between operations  15.5 us (2%)
    pallas_call x3, Pallas kernels, chain_call(): pl.pallas_call(kernel, out_shape=out_shape, grid=(tick_count(rows, count)...  343 us
    pallas_call x1, Pallas kernels, attend_back(): pl.pallas_call(functools.partial(attend_back_kernel, count), out_shape=ou...  140 us
    pallas_call x1, Pallas kernels, layer_front(): pl.pallas_call(front_kernel, out_shape=outs, in_specs=[SMEM_SPEC] + [VMEM...  98.4 us
    pallas_call x1, Pallas kernels, mlp(): pl.pallas_call(mlp_kernel, out_shape=(jax.ShapeDtypeStruct((rows, width),...  73.8 us
    all_gather x3, waiting for transfers between devices, body(): gather = lambda a: lax.all_gather(a, ('shard', 'ctx'), axis=1, tiled=True)  44 us
    pallas_call x1, Pallas kernels, projection_back(): pl.pallas_call(projection_back_kernel, out_shape=(jax.ShapeDtypeStruct((4...  24.7 us
    unnamed x40, local copies, waits for them, and re-layouts  20.1 us
  transfers between devices with their start and end apart: 6, of which 2 were waited for; matrix products, arithmetic and copies ran while one was open for 2% of the time, Pallas kernels for 75%

profile of v4, /device:TPU:0, one launch (start us, length us, event | category | flops | bytes accessed | tf_op | source)
XLA Modules:
  0.0 813.4 jit_solution(9621169625240118438)
XLA Ops:
  7.3 2.5 convert_element_type.23
  9.9 2.2 copy-done
  14.8 44.0 %all-gather.4.cloned.1.call-done.weight_ref = bf16[3,2048,512]{2,1,0:T(8,128)(2,1)} async-done(((bf16[3,256,512]{2,1,0:T(8,128)(2,1)}), bf16[3,2048,512]{2,1,0:T(8,128)(2,1)}) %all-gather.4.cloned.1.call-update) | async-done | bytes 6291472 | tf_op jit(solution)/shard_map/all_gather | solution.py:1140
  60.2 1.9 multiply_sine_fusion
  62.0 1.8 pad_maximum_fusion
  63.9 98.4 %layer_front.1 = (bf16[1024,2048]{1,0:T(8,128)(2,1)}, bf16[1024,512]{1,0:T(8,128)(2,1)}, bf16[1024,512]{1,0:T(8,128)(2,1)}, bf16[1024,512]{1,0:T(8,128)(2,1)}, b...) custom-call(s32[1]{0:T(128)S(6)} %copy.50.live_ref, ...), custom_call_target="tpu_custom_call" | custom-call | flops 80000000000 | bytes 41943040 | tf_op jit(solution)/shard_map/layer_front/pallas_call | solution.py:725
  164.3 117.1 %sum_middle.1 = (bf16[1024,2048]{1,0:T(8,128)(2,1)}, f32[512,2048]{1,0:T(8,128)}, f32[1024,2048]{1,0:T(8,128)}) custom-call(bf16[1024,512]{1,0:T(8,128)(2,1)} %get-tuple-element.62.mixed_ref.o_ref, bf16[2560,2048]{1,0:T(8,128)(2,1)} %all-gather.6.cloned.1.call-done.weight_ref.down_ref, bf16[1024,2048]{1,0:T(8,128)(2,1)} %tokens_hbm.3, ...), custom_call_target="tpu_custom_call" | custom-call | flops 99999997952 | bytes 25165824 | tf_op jit(solution)/shard_map/sum_middle/pallas_call | solution.py:445
  281.4 73.8 %mlp.1 = (bf16[1024,2048]{1,0:T(8,128)(2,1)}, bf16[2048,2048]{1,0:T(8,128)(2,1)}, bf16[2,2048,2048]{2,1,0:T(8,128)(2,1)}, bf16[1024,2048]{1,0:T(8,128)(2,1)}) custom-call(bf16[1024,2048]{1,0:T(8,128)(2,1)} %get-tuple-element.67.normed_ref, bf16[2,2048,2048]{2,1,0:T(8,128)(2,1)} %all-gather.8.cloned.1.call-done.weight_ref, ...), custom_call_target="tpu_custom_call" | custom-call | flops 60129542144 | bytes 83886080 | tf_op jit(solution)/shard_map/mlp/pallas_call | solution.py:1001
  355.4 109.3 %sum_middle_back.1 = (bf16[1024,2048]{1,0:T(8,128)(2,1)}, f32[512,2048]{1,0:T(8,128)}, f32[8,2048]{1,0:T(8,128)}, bf16[1024,2048]{1,0:T(8,128)(2,1)}) custom-call(bf16[1024,2048]{1,0:T(8,128)(2,1)} %get-tuple-element.71.part_ref, f32[512,2048]{1,0:T(8,128)} %get-tuple-element.72.middle_hbm.middle_ref, bf16[1024,2048]{1,0:T(8,128)(2,1)} %cotangent_hbm.3, ...), custom_call_target="tpu_custom_call" | custom-call | flops 99999997952 | bytes 25165824 | tf_op jit(solution)/shard_map/sum_middle_back/pallas_call | solution.py:445
  464.8 13.5 %reduce-scatter.4.cloned.1.call-done = bf16[2,256,2048]{2,1,0:T(8,128)(2,1)} async-done(((bf16[2,2048,2048]{2,1,0:T(8,128)(2,1)}), bf16[2,256,2048]{2,1,0:T(8,128)(2,1)}) %reduce-scatter.4.cloned.1.call-update) | async-done | bytes 2097168 | tf_op jit(solution)/shard_map/reduce_scatter | solution.py:1094
  478.3 10.2 %multiply_subtract_fusion = (f32[2,256,2048]{2,1,0:T(8,128)}, f32[2,256,2048]{2,1,0:T(8,128)}, f32[2,256,2048]{2,1,0:T(8,128)}, f32[2,256,2048]{2,1,0:T(8,128)}) fusion(f32[2,256,2048]{2,1,0:T(8,128)} %gate_up_ref.1, f32[2,256,2048]{2,1,0:T(8,128)} %param.28, f32[2,256,2048]{2,1,0:T(8,128)} %param.33, bf16[2,256,2048]{2,1,0:T(8,128)(2,1)} %reduce-scatter.4.cloned.1.call-done), kind=kLoop, calls=%fused_computation.2 | loop fusion | flops 16777216 | bytes 31457280 | tf_op jit(solution)/shard_map/sub | solution.py:1194
  488.6 3.2 slice.20.weight_ref
  491.7 139.6 %attend_back.1 = (bf16[1024,512]{1,0:T(8,128)(2,1)}, bf16[1024,512]{1,0:T(8,128)(2,1)}, bf16[1024,512]{1,0:T(8,128)(2,1)}, bf16[1024,2048]{1,0:T(8,128)(2,1)}) custom-call(s32[1]{0:T(128)S(6)} %copy.50.live_ref, bf16[1024,512]{1,0:T(8,128)(2,1)} %get-tuple-element.57.q_ref, bf16[1024,512]{1,0:T(8,128)(2,1)} %get-tuple-element.58.k_ref, ...), custom_call_target="tpu_custom_call" | custom-call | flops 99999997952 | bytes 41943040 | tf_op jit(solution)/shard_map/attend_back/pallas_call | solution.py:911
  631.4 24.7 %projection_back.1 = (bf16[4,2048,512]{2,1,0:T(8,128)(2,1)}, bf16[1024,2048]{1,0:T(8,128)(2,1)}) custom-call(bf16[1024,2048]{1,0:T(8,128)(2,1)} %get-tuple-element.77.normed_ref, bf16[3,2048,512]{2,1,0:T(8,128)(2,1)} %all-gather.4.cloned.1.call-done.weight_ref, bf16[1024,512]{1,0:T(8,128)(2,1)} %get-tuple-element.78.dq_ref, ...), custom_call_target="tpu_custom_call" | custom-call | flops 15032385536 | bytes 41943040 | tf_op jit(solution)/shard_map/projection_back/pallas_call | solution.py:1066
  656.1 6.3 multiply_subtract_fusion.1
  665.4 116.3 %sum_input_back.1 = (bf16[1024,2048]{1,0:T(8,128)(2,1)}, f32[2,256]{1,0:T(2,128)}) custom-call(bf16[1024,2048]{1,0:T(8,128)(2,1)} %get-tuple-element.86.part_ref, bf16[1024,2048]{1,0:T(8,128)(2,1)} %tokens_hbm.3, f32[512,2048]{1,0:T(8,128)} %get-tuple-element.87.grad_hbm, f32[1,2048]{1,0:T(1,128)} %get-tuple-element.132.gain_ref, ...), custom_call_target="tpu_custom_call" | custom-call | flops 99999997952 | bytes 25165824 | tf_op jit(solution)/shard_map/sum_input_back/pallas_call | solution.py:445
  785.6 2.6 add_multiply_fusion
  788.2 2.2 copy.44
  790.4 2.0 copy.45
  792.5 2.0 copy.46
  794.5 5.3 multiply_subtract_fusion.2
  799.8 2.1 copy.51
  801.9 1.6 copy-done.7
  803.5 2.0 copy.52
  (58 shorter events, 13.3 us)
Async XLA Ops:
  7.2 2.7 copy-start.3
  7.2 2.7 copy-start.1
  7.2 51.6 %all-gather.4.cloned.1.call-start = ((), (), s32[]{:S(2)}) async-start(), calls=%async_computation.3 | async-start | bytes 7077888 | tf_op jit(solution)/shard_map/all_gather | solution.py:1140
  9.8 152.5 %all-gather.6.cloned.1.call-start = ((), (), s32[]{:S(2)}) async-start(), calls=%async_computation.4 | async-start | bytes 11796480 | tf_op jit(solution)/shard_map/all_gather | solution.py:1140
  9.9 2.2 copy-start
  12.1 47.4 %copy-start.10 = (f32[2,256]{1,0:T(2,128)S(1)}, f32[2,256]{1,0:T(2,128)}, u32[]{:S(2)}) copy-start(f32[2,256]{1,0:T(2,128)} %param.25) | copy-start | bytes 6148
  13.5 1.3 copy-start.2
  58.8 222.6 %all-gather.8.cloned.1.call-start = ((), (), s32[]{:S(2)}) async-start(), calls=%async_computation.5 | async-start | bytes 18874368 | tf_op jit(solution)/shard_map/all_gather | solution.py:1140
  162.4 316.0 %reduce-scatter.4.cloned.1.call-start = ((), (), s32[]{:S(2)}) async-start(), calls=%async_computation.6 | async-start | bytes 18874368 | tf_op jit(solution)/shard_map/reduce_scatter | solution.py:1094
  355.2 300.9 %reduce-scatter.6.cloned.1.call-start = ((), (), s32[]{:S(2)}) async-start(), calls=%async_computation.7 | async-start | bytes 9437184 | tf_op jit(solution)/shard_map/reduce_scatter | solution.py:1094
  488.5 294.6 %reduce-scatter.8.cloned.1.call-start = ((), (), s32[]{:S(2)}) async-start(), calls=%async_computation.8 | async-start | bytes 9437184 | tf_op jit(solution)/shard_map/reduce_scatter | solution.py:1094
  662.4 1.0 copy-start.8
  662.4 2.0 copy-start.9
  665.4 116.3 %copy-start.11 = (f32[2,256]{1,0:T(2,128)S(1)}, f32[2,256]{1,0:T(2,128)}, u32[]{:S(2)}) copy-start(f32[2,256]{1,0:T(2,128)} %param.25) | copy-start | bytes 6148
  665.4 116.3 %copy-start.13 = (f32[2,256]{1,0:T(2,128)S(1)}, f32[2,256]{1,0:T(2,128)}, u32[]{:S(2)}) copy-start(f32[2,256]{1,0:T(2,128)} %param.30) | copy-start | bytes 6148
  665.4 116.4 %copy-start.14 = (f32[2,256]{1,0:T(2,128)S(1)}, f32[2,256]{1,0:T(2,128)}, u32[]{:S(2)}) copy-start(f32[2,256]{1,0:T(2,128)} %param.35) | copy-start | bytes 6148
  788.2 6.3 copy-start.4
  788.2 6.3 copy-start.5
  794.5 5.3 copy-start.6
  799.8 3.7 copy-start.7
  803.5 2.0 copy-start.12
Sparse Core Ops, SparseCore 0:
  10.5 48.2 all-gather.3
  61.2 93.0 all-gather.5
  162.5 99.2 all-gather.7
  355.3 122.9 reduce-scatter.3
  488.6 102.6 reduce-scatter.5
  662.5 70.1 reduce-scatter.7

commit v5 on v4

--- a/solution.py
+++ b/solution.py
@@ -740,9 +740,10 @@
 
 
 def attend_back_kernel(
-    count, live_ref, q_ref, k_ref, v_ref, kp_ref, vp_ref, o_ref, l_ref, cos_ref, sin_ref,
-    part_ref, middle_ref, grad_ref, weight_ref, dq_ref, dk_ref, dv_ref, out_ref,
-    do_ref, dq_acc, dk_acc, dv_acc, dkp_acc, dvp_acc, leave, arrive, slots, send, recv, chain_send, chain_recv,
+    count, live_ref, q_hbm, k_hbm, v_hbm, kp_hbm, vp_hbm, o_hbm, l_ref, cos_ref, sin_ref,
+    part_ref, middle_hbm, grad_ref, both_hbm, dq_ref, dk_ref, dv_ref, out_ref,
+    q_ref, k_ref, v_ref, kp_ref, vp_ref, o_ref, do_ref, weight_ref, middle_ref, early_sem, late_sem,
+    dq_acc, dk_acc, dv_acc, dkp_acc, dvp_acc, leave, arrive, slots, send, recv, chain_send, chain_recv,
 ):
     late = lax.axis_index("ctx")
     me = lax.axis_index("tp")
@@ -750,6 +751,18 @@
     block = min(BLOCK, rows)
     blocks = rows // block
     pairs = width // PAIR
+    load_early, wait_early = loads_of(
+        [(both_hbm.at[pl.ds(0, width)], weight_ref), (middle_hbm, middle_ref)], early_sem
+    )
+    load_late, wait_late = loads_of(
+        [
+            (o_hbm, o_ref), (q_hbm, q_ref), (kp_hbm, kp_ref), (vp_hbm, vp_ref), (k_hbm, k_ref),
+            (v_hbm, v_ref),
+        ],
+        late_sem,
+    )
+    load_early()
+    load_late()
     barrier = pltpu.get_barrier_semaphore()
     pl.semaphore_signal(barrier, inc=1, device_id={"ctx": 1 - late}, device_id_type=MESH)
     greet(me, count, 1)
@@ -852,12 +865,15 @@
     def _():
         dq_acc[...] = jnp.zeros_like(dq_acc)
 
+    wait_early()
+
     @pl.loop(0, blocks)
     def _(at):
         for more in range(LEAD):
             tick(at * LEAD + more)
         do_ref[here(at)] = dot(grad_ref[here(at)], weight_ref[...], (1, 1)).astype(jnp.bfloat16)
 
+    wait_late()
     steps = pairs * blocks
     lead = blocks * LEAD
 
@@ -911,10 +927,14 @@
     return pl.pallas_call(
         functools.partial(attend_back_kernel, count),
         out_shape=outs,
-        in_specs=[SMEM_SPEC] + [VMEM_SPEC] * 13,
+        in_specs=[SMEM_SPEC] + [HBM_SPEC] * 6 + [VMEM_SPEC] * 4 + [HBM_SPEC, VMEM_SPEC, HBM_SPEC],
         out_specs=(VMEM_SPEC,) * len(outs),
         scratch_shapes=[
-            pltpu.VMEM((rows, width), jnp.bfloat16),
+            *[pltpu.VMEM((rows, width), jnp.bfloat16)] * 7,
+            pltpu.VMEM((width, middle.shape[1]), jnp.bfloat16),
+            pltpu.VMEM(middle.shape, jnp.float32),
+            pltpu.SemaphoreType.DMA((2,)),
+            pltpu.SemaphoreType.DMA((6,)),
             pltpu.VMEM((pairs, PAIR, rows), jnp.float32),
             pltpu.VMEM((rows, width), jnp.float32),
             pltpu.VMEM((rows, width), jnp.float32),
@@ -1088,6 +1108,50 @@
         ),
         name="projection_back",
     )(normed, weight, dq, dk, dv, mixed, middle)
+
+
+def tail_kernel(
+    grad_ref, out_grad_ref, w_ref, m_ref, s_ref, ow_ref, om_ref, os_ref,
+    g_out, w_out, m_out, s_out, og_out, step_out, om_out, os_out,
+):
+    grad = grad_ref[0:3].astype(jnp.float32)
+    update, first, second = adam_update(w_ref[...], m_ref[...], s_ref[...], grad, decay_rate)
+    g_out[...] = grad
+    w_out[...] = w_ref[...] - update
+    m_out[...] = first
+    s_out[...] = second
+    grad = out_grad_ref[0].astype(jnp.float32).T
+    update, first, second = adam_update(ow_ref[...], om_ref[...], os_ref[...], grad, decay_rate)
+    og_out[...] = grad
+    step_out[...] = update
+    om_out[...] = first
+    os_out[...] = second
+
+
+def adam_tail(grads, qkv, out):
+    planes, rows, width = qkv[0].shape
+    steps = width // PAIR
+    mine = pl.BlockSpec((planes, rows // steps, width), lambda i: (0, i, 0))
+    other = pl.BlockSpec((PAIR, rows), lambda i: (i, 0))
+    shapes = [jax.ShapeDtypeStruct(qkv[0].shape, jnp.float32)] * 4
+    shapes += [jax.ShapeDtypeStruct(out[0].shape, jnp.float32)] * 4
+    results = pl.pallas_call(
+        tail_kernel,
+        out_shape=tuple(shapes),
+        grid=(steps,),
+        in_specs=[
+            pl.BlockSpec((planes + 1, rows // steps, width), lambda i: (0, i, 0)),
+            pl.BlockSpec((1, rows, PAIR), lambda i: (planes, 0, i)),
+            mine, mine, mine, other, other, other,
+        ],
+        out_specs=(mine,) * 4 + (other,) * 4,
+        compiler_params=pltpu.CompilerParams(vmem_limit_bytes=40 * 2**20),
+        cost_estimate=pl.CostEstimate(
+            flops=10**7, bytes_accessed=16 * 2**20, transcendentals=0
+        ),
+        name="adam_tail",
+    )(grads, grads, *qkv, *out)
+    return results[:4], results[4:]
 
 
 def scatter_low(grad, axis=1):
@@ -1153,33 +1217,35 @@
     hidden, down_grad_local, gate_up_grad_local, mlp_back_part = mlp(
         normed_two, gate_up_full, hidden_grad, cotangent
     )
-    gate_up_grad = scatter_low(gate_up_grad_local)
+    down_grad = scatter_low(down_grad_local)
     middle_low, middle_grad, gain_two_grad, out_part = sum_middle_back(
         mlp_back_part, middle, cotangent, gain_two, hidden, both_full, count
     )
-    down_grad = scatter_low(after(down_grad_local, gate_up_grad, middle_low))
+    gate_up_grad = scatter_low(after(gate_up_grad_local, down_grad, middle_low))
     query_low, key_low, value_low, out_tokens = attend_back(
         lengths,
         [query, keys, values, keys_prev, values_prev, mixed_low, totals],
-        cosine, sine, out_part, middle, middle_low, both_full[: mixed_low.shape[1]], count,
+        cosine, sine, out_part, middle, middle_low, both_full, count,
     )
     qkv_grad_local, attn_back_part = projection_back(
         normed_one, qkv_full, query_low, key_low, value_low, mixed_low, middle_low
     )
     attn_back_part, qkv_grad_local, _ = lax.optimization_barrier(
-        (attn_back_part, qkv_grad_local, down_grad)
-    )
-    qkv_grad = scatter_low(qkv_grad_local)
-    out_grad = lax.optimization_barrier(qkv_grad[3].T)
-    qkv_grad = qkv_grad[:3]
+        (attn_back_part, qkv_grad_local, gate_up_grad)
+    )
+    tail_grads = lax.psum_scatter(
+        qkv_grad_local, ("shard", "ctx"), scatter_dimension=1, tiled=True
+    )
     input_grad, gains_grad = sum_input_back(
         attn_back_part, tokens, middle_grad, gain_one, gain_two_grad, norm_gains.shape[1], count
     )
-    qkv_step, qkv_first_new, qkv_second_new = adam_update(
-        qkv_weight, qkv_first, qkv_second, qkv_grad, decay_rate
-    )
-    out_step, out_first_new, out_second_new = adam_update(
-        out_weight, out_first, out_second, out_grad, decay_rate
+    tail_grads, _ = lax.optimization_barrier((tail_grads, gains_grad))
+    (qkv_grad, qkv_new, qkv_first_new, qkv_second_new), (
+        out_grad, out_step, out_first_new, out_second_new,
+    ) = adam_tail(
+        tail_grads,
+        (qkv_weight, qkv_first, qkv_second),
+        (out_weight, out_first, out_second),
     )
     gate_up_step, gate_up_first_new, gate_up_second_new = adam_update(
         gate_up_weight, gate_up_first, gate_up_second, gate_up_grad, decay_rate
@@ -1190,7 +1256,6 @@
     gains_step, gains_first_new, gains_second_new = adam_update(
         norm_gains, gains_first, gains_second, gains_grad, 0.0
     )
-    qkv_new = qkv_weight - qkv_step
     gate_up_new = gate_up_weight - gate_up_step
     down_new = down_weight - down_step
     return (

time: 818 us -> 793 us (0.969)
  waiting for transfers between devices: 57.7 us -> 42.3 us
  other arithmetic: 34 us -> 24.4 us
    reduce_scatter x3 -> x2, waiting for transfers between devices: 13.5 us -> 0.04 us  [scatter_low(): lax.psum_scatter(grad.astype(jnp.bfloat16), ('shard', 'ctx'), scatter_dim...]
    pallas_call x1, Pallas kernels: 140 us -> 131 us  [attend_back(): pl.pallas_call(functools.partial(attend_back_kernel, count), out_shape=ou...]
    pallas_call x3, Pallas kernels: 343 us -> 351 us  [chain_call(): pl.pallas_call(kernel, out_shape=out_shape, grid=(tick_count(rows, count)...]
    unnamed x40 -> x39, local copies, waits for them, and re-layouts: 20.1 us -> 16.9 us
  transfers between devices with their start and end apart: 6 -> 6, of which waited for: 2 -> 1; matrix products, arithmetic and copies ran while one was open for 2% -> 1% of each run, Pallas kernels for 75% -> 77%
where the time goes in v5:
time: 793 us; the launch traced here: 788 us
  Pallas kernels  687 us (87%)
  waiting for transfers between devices  42.3 us (5%)
  other arithmetic  24.4 us (3%)
  local copies, waits for them, and re-layouts  18.4 us (2%)
  between operations  15.2 us (2%)
    pallas_call x3, Pallas kernels, chain_call(): pl.pallas_call(kernel, out_shape=out_shape, grid=(tick_count(rows, count)...  351 us
    pallas_call x1, Pallas kernels, attend_back(): pl.pallas_call(functools.partial(attend_back_kernel, count), out_shape=ou...  131 us
    pallas_call x1, Pallas kernels, layer_front(): pl.pallas_call(front_kernel, out_shape=outs, in_specs=[SMEM_SPEC] + [VMEM...  98.4 us
    pallas_call x1, Pallas kernels, mlp(): pl.pallas_call(mlp_kernel, out_shape=(jax.ShapeDtypeStruct((rows, width),...  73.8 us
    all_gather x3, waiting for transfers between devices, body(): gather = lambda a: lax.all_gather(a, ('shard', 'ctx'), axis=1, tiled=True)  42.2 us
    pallas_call x1, Pallas kernels, projection_back(): pl.pallas_call(projection_back_kernel, out_shape=(jax.ShapeDtypeStruct((4...  25.4 us
    unnamed x39, local copies, waits for them, and re-layouts  16.9 us
  transfers between devices with their start and end apart: 6, of which 1 were waited for; matrix products, arithmetic and copies ran while one was open for 1% of the time, Pallas kernels for 77%

profile of v5, /device:TPU:0, one launch (start us, length us, event | category | flops | bytes accessed | tf_op | source)
XLA Modules:
  0.0 788.2 jit_solution(9453602040934430199)
XLA Ops:
  7.2 2.4 convert_element_type.20
  9.7 2.2 copy-done.1
  11.9 1.6 copy-done.3
  14.5 2.1 narrow.1
  16.6 42.1 %all-gather.4.cloned.1.call-done.weight_ref = bf16[3,2048,512]{2,1,0:T(8,128)(2,1)} async-done(((bf16[3,256,512]{2,1,0:T(8,128)(2,1)}), bf16[3,2048,512]{2,1,0:T(8,128)(2,1)}) %all-gather.4.cloned.1.call-update) | async-done | bytes 6291472 | tf_op jit(solution)/shard_map/all_gather | solution.py:1204
  60.1 1.9 multiply_sine_fusion
  62.0 1.8 pad_maximum_fusion
  63.9 98.4 %layer_front.1 = (bf16[1024,2048]{1,0:T(8,128)(2,1)}, bf16[1024,512]{1,0:T(8,128)(2,1)}, bf16[1024,512]{1,0:T(8,128)(2,1)}, bf16[1024,512]{1,0:T(8,128)(2,1)}, b...) custom-call(s32[1]{0:T(128)S(6)} %copy.43.live_ref, ...), custom_call_target="tpu_custom_call" | custom-call | flops 80000000000 | bytes 41943040 | tf_op jit(solution)/shard_map/layer_front/pallas_call | solution.py:725
  162.5 1.5 fusion.6
  164.1 117.1 %sum_middle.1 = (bf16[1024,2048]{1,0:T(8,128)(2,1)}, f32[512,2048]{1,0:T(8,128)}, f32[1024,2048]{1,0:T(8,128)}) custom-call(bf16[1024,512]{1,0:T(8,128)(2,1)} %get-tuple-element.71.mixed_ref.o_hbm, bf16[2560,2048]{1,0:T(8,128)(2,1)} %all-gather.6.cloned.1.call-done.weight_ref.down_ref.both_hbm, bf16[1024,2048]{1,0:T(8,128)(2,1)} %tokens_hbm.3, ...), custom_call_target="tpu_custom_call" | custom-call | flops 99999997952 | bytes 25165824 | tf_op jit(solution)/shard_map/sum_middle/pallas_call | solution.py:445
  281.2 73.8 %mlp.1 = (bf16[1024,2048]{1,0:T(8,128)(2,1)}, bf16[2048,2048]{1,0:T(8,128)(2,1)}, bf16[2,2048,2048]{2,1,0:T(8,128)(2,1)}, bf16[1024,2048]{1,0:T(8,128)(2,1)}) custom-call(bf16[1024,2048]{1,0:T(8,128)(2,1)} %get-tuple-element.76.normed_ref, bf16[2,2048,2048]{2,1,0:T(8,128)(2,1)} %all-gather.8.cloned.1.call-done.weight_ref, ...), custom_call_target="tpu_custom_call" | custom-call | flops 60129542144 | bytes 83886080 | tf_op jit(solution)/shard_map/mlp/pallas_call | solution.py:1021
  355.3 109.6 %sum_middle_back.1 = (bf16[1024,2048]{1,0:T(8,128)(2,1)}, f32[512,2048]{1,0:T(8,128)}, f32[8,2048]{1,0:T(8,128)}, bf16[1024,2048]{1,0:T(8,128)(2,1)}) custom-call(bf16[1024,2048]{1,0:T(8,128)(2,1)} %get-tuple-element.80.part_ref, f32[512,2048]{1,0:T(8,128)} %get-tuple-element.81.middle_hbm, bf16[1024,2048]{1,0:T(8,128)(2,1)} %cotangent_hbm.3, ...), custom_call_target="tpu_custom_call" | custom-call | flops 99999997952 | bytes 25165824 | tf_op jit(solution)/shard_map/sum_middle_back/pallas_call | solution.py:445
  464.9 6.3 multiply_subtract_fusion.1
  471.3 131.2 %attend_back.1 = (bf16[1024,512]{1,0:T(8,128)(2,1)}, bf16[1024,512]{1,0:T(8,128)(2,1)}, bf16[1024,512]{1,0:T(8,128)(2,1)}, bf16[1024,2048]{1,0:T(8,128)(2,1)}) custom-call(s32[1]{0:T(128)S(6)} %copy.43.live_ref, bf16[1024,512]{1,0:T(8,128)(2,1)} %get-tuple-element.66.q_hbm, bf16[1024,512]{1,0:T(8,128)(2,1)} %get-tuple-element.67.k_hbm, ...), custom_call_target="tpu_custom_call" | custom-call | flops 99999997952 | bytes 41943040 | tf_op jit(solution)/shard_map/attend_back/pallas_call | solution.py:927
  602.5 25.4 %projection_back.1 = (bf16[4,2048,512]{2,1,0:T(8,128)(2,1)}, bf16[1024,2048]{1,0:T(8,128)(2,1)}) custom-call(bf16[1024,2048]{1,0:T(8,128)(2,1)} %get-tuple-element.86.normed_ref, bf16[3,2048,512]{2,1,0:T(8,128)(2,1)} %all-gather.4.cloned.1.call-done.weight_ref, bf16[1024,512]{1,0:T(8,128)(2,1)} %get-tuple-element.87.dq_ref, ...), custom_call_target="tpu_custom_call" | custom-call | flops 15032385536 | bytes 41943040 | tf_op jit(solution)/shard_map/projection_back/pallas_call | solution.py:1086
  627.9 10.2 %multiply_subtract_fusion = (f32[2,256,2048]{2,1,0:T(8,128)}, f32[2,256,2048]{2,1,0:T(8,128)}, f32[2,256,2048]{2,1,0:T(8,128)}, f32[2,256,2048]{2,1,0:T(8,128)}) fusion(f32[2,256,2048]{2,1,0:T(8,128)} %gate_up_ref.1, f32[2,256,2048]{2,1,0:T(8,128)} %param.28, f32[2,256,2048]{2,1,0:T(8,128)} %param.33, bf16[2,256,2048]{2,1,0:T(8,128)(2,1)} %reduce-scatter.6.cloned.1.call-done), kind=kLoop, calls=%fused_computation.2 | loop fusion | flops 16777216 | bytes 31457280 | tf_op jit(solution)/shard_map/sub | solution.py:1259
  638.2 124.2 %sum_input_back.1 = (bf16[1024,2048]{1,0:T(8,128)(2,1)}, f32[2,256]{1,0:T(2,128)}) custom-call(bf16[1024,2048]{1,0:T(8,128)(2,1)} %get-tuple-element.95.part_ref, bf16[1024,2048]{1,0:T(8,128)(2,1)} %tokens_hbm.3, f32[512,2048]{1,0:T(8,128)} %get-tuple-element.96.grad_hbm, f32[1,2048]{1,0:T(1,128)} %get-tuple-element.121.gain_ref, ...), custom_call_target="tpu_custom_call" | custom-call | flops 99999997952 | bytes 25165824 | tf_op jit(solution)/shard_map/sum_input_back/pallas_call | solution.py:445
  762.5 1.2 add_multiply_fusion
  763.7 1.2 copy-done.2
  764.9 1.4 copy-done.6
  769.5 5.4 adam_tail.1
  774.9 2.1 copy.44
  777.0 1.6 copy-done.12
  778.6 2.0 copy.45
  (53 shorter events, 6.2 us)
Async XLA Ops:
  7.2 51.6 %all-gather.4.cloned.1.call-start = ((), (), s32[]{:S(2)}) async-start(), calls=%async_computation.3 | async-start | bytes 7077888 | tf_op jit(solution)/shard_map/all_gather | solution.py:1204
  9.6 152.6 %all-gather.6.cloned.1.call-start = ((), (), s32[]{:S(2)}) async-start(), calls=%async_computation.4 | async-start | bytes 11796480 | tf_op jit(solution)/shard_map/all_gather | solution.py:1204
  9.7 2.2 copy-start.1
  11.9 1.6 copy-start.3
  13.5 1.0 copy-start.7
  14.5 45.0 %copy-start.13 = (f32[2,256]{1,0:T(2,128)S(1)}, f32[2,256]{1,0:T(2,128)}, u32[]{:S(2)}) copy-start(f32[2,256]{1,0:T(2,128)} %param.25) | copy-start | bytes 6148
  58.8 222.4 %all-gather.8.cloned.1.call-start = ((), (), s32[]{:S(2)}) async-start(), calls=%async_computation.5 | async-start | bytes 18874368 | tf_op jit(solution)/shard_map/all_gather | solution.py:1204
  162.3 302.6 %reduce-scatter.4.cloned.1.call-start = ((), (), s32[]{:S(2)}) async-start(), calls=%async_computation.6 | async-start | bytes 9437184 | tf_op jit(solution)/shard_map/reduce_scatter | solution.py:1158
  355.0 272.9 %reduce-scatter.6.cloned.1.call-start = ((), (), s32[]{:S(2)}) async-start(), calls=%async_computation.7 | async-start | bytes 18874368 | tf_op jit(solution)/shard_map/reduce_scatter | solution.py:1158
  355.3 109.7 %copy-start.4 = (f32[2048,256]{1,0:T(8,128)S(1)}, f32[2048,256]{1,0:T(8,128)}, u32[]{:S(2)}) copy-start(f32[2048,256]{1,0:T(8,128)} %down_ref.1) | copy-start | bytes 6291460
  471.2 292.5 %reduce-scatter.8.cloned.1.call-start = ((), (), s32[]{:S(2)}) async-start(), calls=%async_computation.8 | async-start | bytes 9437184 | tf_op jit(solution)/shard_map/reduce_scatter | solution.py:1236
  638.1 124.3 %copy-start.14 = (f32[2,256]{1,0:T(2,128)S(1)}, f32[2,256]{1,0:T(2,128)}, u32[]{:S(2)}) copy-start(f32[2,256]{1,0:T(2,128)} %param.25) | copy-start | bytes 6148
  638.2 124.3 %copy-start.16 = (f32[2,256]{1,0:T(2,128)S(1)}, f32[2,256]{1,0:T(2,128)}, u32[]{:S(2)}) copy-start(f32[2,256]{1,0:T(2,128)} %param.30) | copy-start | bytes 6148
  638.2 124.3 %copy-start.17 = (f32[2,256]{1,0:T(2,128)S(1)}, f32[2,256]{1,0:T(2,128)}, u32[]{:S(2)}) copy-start(f32[2,256]{1,0:T(2,128)} %param.35) | copy-start | bytes 6148
  638.2 125.5 %copy-start = (f32[3,256,512]{2,1,0:T(8,128)S(1)}, f32[3,256,512]{2,1,0:T(8,128)}, u32[]{:S(2)}) copy-start(f32[3,256,512]{2,1,0:T(8,128)} %w_ref.1) | copy-start | bytes 4718596
  638.2 125.5 %copy-start.5 = (f32[3,256,512]{2,1,0:T(8,128)S(1)}, f32[3,256,512]{2,1,0:T(8,128)}, u32[]{:S(2)}) copy-start(f32[3,256,512]{2,1,0:T(8,128)} %m_ref.1) | copy-start | bytes 4718596
  763.7 1.2 copy-start.2
  764.9 1.4 copy-start.6
  766.3 1.0 copy-start.8
  767.4 1.0 copy-start.9
  768.4 1.0 copy-start.10
  769.5 5.4 copy-start.11
  774.9 3.7 copy-start.12
  778.6 2.0 copy-start.15
Sparse Core Ops, SparseCore 0:
  10.5 48.2 all-gather.3
  61.2 93.0 all-gather.5
  162.4 99.2 all-gather.7
  355.1 78.1 reduce-scatter.3
  471.4 149.7 reduce-scatter.5
  638.3 77.9 reduce-scatter.7

commit v6 on v5

--- a/solution.py
+++ b/solution.py
@@ -275,21 +275,29 @@
         load()
         greet(lax.axis_index("tp"), count)
 
-        @pl.loop(0, part_ref.shape[0] // BLOCK)
-        def _(at):
-            here = pl.ds(pl.multiple_of(at * BLOCK, BLOCK), BLOCK)
+        project(0)
+
+    half_blocks = part_ref.shape[0] // 2 // BLOCK
+
+    def project(at):
+        for half in range(2):
+            here = pl.ds(pl.multiple_of((half * half_blocks + at) * BLOCK, BLOCK), BLOCK)
             part_ref[here] = dot(mixed_ref[here], weight_ref[...], (1, 0)).astype(jnp.bfloat16)
 
     def finish(rows, local, total, at):
         value = tokens_ref[rows].astype(jnp.float32) + total
         middle[local] = value
         half_copy(at).start()
-        return (value * unit_scale(value) * gain_ref[...]).astype(jnp.bfloat16)
+        return (value * unit_scale(value) * gain_ref[1:2]).astype(jnp.bfloat16)
 
     parts = chain_parts(
         count, part_ref, out_ref, slots, send, recv, finish, CHUNK, LAG, land, stored
     )
     tick = run_ticks(parts, start, wait, half_drain)
+
+    @pl.when((tick >= 1) & (tick < half_blocks))
+    def _():
+        project(tick)
 
     @pl.when((tick % SPACING == SPACING - 1) & (tick < blocks * SPACING))
     def _():
@@ -313,7 +321,7 @@
         gain_grad_ref[...] = jnp.zeros_like(gain_grad_ref)
 
     def finish(rows, local, total, at):
-        value, gain_grad = norm_back(middle_ref[local], gain_ref[...], total)
+        value, gain_grad = norm_back(middle_ref[local], gain_ref[1:2], total)
         gain_grad_ref[...] += gain_grad
         value = cotangent_ref[rows].astype(jnp.float32) + value
         grad[local] = value
@@ -355,7 +363,7 @@
         local[8:16] = other_ref[...]
 
     def finish(rows, part, total, at):
-        grad, gain_grad = norm_back(tokens_ref[rows].astype(jnp.float32), gain_ref[...], total)
+        grad, gain_grad = norm_back(tokens_ref[rows].astype(jnp.float32), gain_ref[0:1], total)
         local[0:8] += gain_grad
         return (grad_ref[part] + grad).astype(jnp.bfloat16)
 
@@ -958,14 +966,18 @@
     )(live, *arrays, cosine, sine, out_part, middle, grad, both)
 
 
-def narrow_kernel(out_ref, down_ref, gate_up_ref, both_ref, low_ref):
+def narrow_kernel(
+    out_ref, down_ref, gate_up_ref, cos_in, sin_in, both_ref, low_ref, cos_ref, sin_ref
+):
+    cos_ref[...] = cos_in[...]
+    sin_ref[...] = sin_in[...]
     split = out_ref.shape[0]
     both_ref[:split] = out_ref[...].astype(jnp.bfloat16)
     both_ref[split:] = down_ref[...].astype(jnp.bfloat16)
     low_ref[...] = gate_up_ref[...].astype(jnp.bfloat16)
 
 
-def narrow(out_weight, down_weight, gate_up_weight):
+def narrow(out_weight, down_weight, gate_up_weight, cosine, sine):
     return pl.pallas_call(
         narrow_kernel,
         out_shape=(
@@ -973,13 +985,15 @@
                 (out_weight.shape[0] + down_weight.shape[0], out_weight.shape[1]), jnp.bfloat16
             ),
             jax.ShapeDtypeStruct(gate_up_weight.shape, jnp.bfloat16),
-        ),
-        in_specs=[VMEM_SPEC] * 3,
-        out_specs=(VMEM_SPEC,) * 2,
+            jax.ShapeDtypeStruct(cosine.shape, jnp.float32),
+            jax.ShapeDtypeStruct(sine.shape, jnp.float32),
+        ),
+        in_specs=[VMEM_SPEC] * 5,
+        out_specs=(VMEM_SPEC,) * 4,
         compiler_params=pltpu.CompilerParams(vmem_limit_bytes=40 * 2**20),
         cost_estimate=pl.CostEstimate(flops=40 * 10**9, bytes_accessed=2**24, transcendentals=0),
         name="narrow",
-    )(out_weight, down_weight, gate_up_weight)
+    )(out_weight, down_weight, gate_up_weight, cosine, sine)
 
 
 def mlp_kernel(
@@ -1145,7 +1159,7 @@
             mine, mine, mine, other, other, other,
         ],
         out_specs=(mine,) * 4 + (other,) * 4,
-        compiler_params=pltpu.CompilerParams(vmem_limit_bytes=40 * 2**20),
+        compiler_params=pltpu.CompilerParams(vmem_limit_bytes=60 * 2**20),
         cost_estimate=pl.CostEstimate(
             flops=10**7, bytes_accessed=16 * 2**20, transcendentals=0
         ),
@@ -1198,28 +1212,29 @@
     offset = lax.axis_index("ctx") * row_count
     query_index = offset + jnp.arange(row_count, dtype=jnp.int32)
     qkv_low = qkv_weight.astype(jnp.bfloat16)
-    both_low, gate_up_low = narrow(out_weight, down_weight, gate_up_weight)
+    cosine, sine = rotation(query_index, HEAD)
+    cosine, sine = (jnp.concatenate([c[:, 0]] * 4, 1) for c in (cosine, sine))
+    both_low, gate_up_low, cosine, sine = narrow(
+        out_weight, down_weight, gate_up_weight, cosine, sine
+    )
     gains_low = norm_gains.astype(jnp.bfloat16).astype(jnp.float32)
     gains_low = jnp.concatenate([gains_low] * 4, 0)
     gather = lambda a: lax.all_gather(a, ("shard", "ctx"), axis=1, tiled=True)
     qkv_full = gather(qkv_low)
     both_full = gather(after(both_low, qkv_full))
-    cosine, sine = rotation(query_index, HEAD)
-    cosine, sine = (jnp.concatenate([c[:, 0]] * 4, 1) for c in (cosine, sine))
     normed_one, query, keys, values, keys_prev, values_prev, mixed_low, totals, gains_full = layer_front(
         lengths, tokens, qkv_full, gains_low, cosine, sine
     )
-    gain_one, gain_two = gains_full[0:1], gains_full[1:2]
     gate_up_full = gather(after(gate_up_low, both_full, totals))
     normed_two, middle, hidden_grad = sum_middle(
-        mixed_low, both_full, tokens, gain_two, cotangent, count
+        mixed_low, both_full, tokens, gains_full, cotangent, count
     )
     hidden, down_grad_local, gate_up_grad_local, mlp_back_part = mlp(
         normed_two, gate_up_full, hidden_grad, cotangent
     )
     down_grad = scatter_low(down_grad_local)
     middle_low, middle_grad, gain_two_grad, out_part = sum_middle_back(
-        mlp_back_part, middle, cotangent, gain_two, hidden, both_full, count
+        mlp_back_part, middle, cotangent, gains_full, hidden, both_full, count
     )
     gate_up_grad = scatter_low(after(gate_up_grad_local, down_grad, middle_low))
     query_low, key_low, value_low, out_tokens = attend_back(
@@ -1237,7 +1252,7 @@
         qkv_grad_local, ("shard", "ctx"), scatter_dimension=1, tiled=True
     )
     input_grad, gains_grad = sum_input_back(
-        attn_back_part, tokens, middle_grad, gain_one, gain_two_grad, norm_gains.shape[1], count
+        attn_back_part, tokens, middle_grad, gains_full, gain_two_grad, norm_gains.shape[1], count
     )
     tail_grads, _ = lax.optimization_barrier((tail_grads, gains_grad))
     (qkv_grad, qkv_new, qkv_first_new, qkv_second_new), (

time: 793 us -> 787 us (level)
    unnamed x39 -> x27, local copies, waits for them, and re-layouts: 16.9 us -> 12.7 us
  transfers between devices with their start and end apart: 6 -> 6, of which waited for: 1 -> 1; matrix products, arithmetic and copies ran while one was open for 1% -> 1% of each run, Pallas kernels for 77% -> 78%
where the time goes in v6:
time: 787 us; the launch traced here: 782 us
  Pallas kernels  691 us (88%)
  waiting for transfers between devices  39.7 us (5%)
  other arithmetic  23.6 us (3%)
  between operations  15.2 us (2%)
  local copies, waits for them, and re-layouts  12.7 us (2%)
    pallas_call x3, Pallas kernels, chain_call(): pl.pallas_call(kernel, out_shape=out_shape, grid=(tick_count(rows, count)...  349 us
    pallas_call x1, Pallas kernels, attend_back(): pl.pallas_call(functools.partial(attend_back_kernel, count), out_shape=ou...  131 us
    pallas_call x1, Pallas kernels, layer_front(): pl.pallas_call(front_kernel, out_shape=outs, in_specs=[SMEM_SPEC] + [VMEM...  102 us
    pallas_call x1, Pallas kernels, mlp(): pl.pallas_call(mlp_kernel, out_shape=(jax.ShapeDtypeStruct((rows, width),...  73.8 us
    all_gather x3, waiting for transfers between devices, body(): gather = lambda a: lax.all_gather(a, ('shard', 'ctx'), axis=1, tiled=True)  39.6 us
    pallas_call x1, Pallas kernels, projection_back(): pl.pallas_call(projection_back_kernel, out_shape=(jax.ShapeDtypeStruct((4...  25.4 us
  transfers between devices with their start and end apart: 6, of which 1 were waited for; matrix products, arithmetic and copies ran while one was open for 1% of the time, Pallas kernels for 78%

profile of v6, /device:TPU:0, one launch (start us, length us, event | category | flops | bytes accessed | tf_op | source)
XLA Modules:
  0.0 782.3 jit_solution(5234213948050100175)
XLA Ops:
  7.3 2.5 convert_element_type.20
  9.9 1.9 multiply_sine_fusion
  11.8 0.9 pad_maximum_fusion
  12.7 2.2 copy-done
  14.9 1.5 narrow.1
  16.3 1.3 copy-done.2
  17.7 0.8 copy-done.4
  18.5 0.8 copy-done.5
  19.2 39.5 %all-gather.4.cloned.1.call-done.weight_ref = bf16[3,2048,512]{2,1,0:T(8,128)(2,1)} async-done(((bf16[3,256,512]{2,1,0:T(8,128)(2,1)}), bf16[3,2048,512]{2,1,0:T(8,128)(2,1)}) %all-gather.4.cloned.1.call-update) | async-done | bytes 6291472 | tf_op jit(solution)/shard_map/all_gather | solution.py:1222
  59.5 0.6 maximum_convert_fusion.own_gain_ref
  60.1 101.6 %layer_front.1 = (bf16[1024,2048]{1,0:T(8,128)(2,1)}, bf16[1024,512]{1,0:T(8,128)(2,1)}, bf16[1024,512]{1,0:T(8,128)(2,1)}, bf16[1024,512]{1,0:T(8,128)(2,1)}, b...) custom-call(s32[1]{0:T(128)S(6)} %copy.43.live_ref, ...), custom_call_target="tpu_custom_call" | custom-call | flops 80000000000 | bytes 41943040 | tf_op jit(solution)/shard_map/layer_front/pallas_call | solution.py:733
  162.0 115.0 %sum_middle.1 = (bf16[1024,2048]{1,0:T(8,128)(2,1)}, f32[512,2048]{1,0:T(8,128)}, f32[1024,2048]{1,0:T(8,128)}) custom-call(bf16[1024,512]{1,0:T(8,128)(2,1)} %get-tuple-element.75.mixed_ref.o_hbm, bf16[2560,2048]{1,0:T(8,128)(2,1)} %all-gather.6.cloned.1.call-done.weight_ref.down_ref.both_hbm, bf16[1024,2048]{1,0:T(8,128)(2,1)} %tokens_hbm.3, ...), custom_call_target="tpu_custom_call" | custom-call | flops 99999997952 | bytes 25165824 | tf_op jit(solution)/shard_map/sum_middle/pallas_call | solution.py:453
  277.1 73.8 %mlp.1 = (bf16[1024,2048]{1,0:T(8,128)(2,1)}, bf16[2048,2048]{1,0:T(8,128)(2,1)}, bf16[2,2048,2048]{2,1,0:T(8,128)(2,1)}, bf16[1024,2048]{1,0:T(8,128)(2,1)}) custom-call(bf16[1024,2048]{1,0:T(8,128)(2,1)} %get-tuple-element.80.normed_ref, bf16[2,2048,2048]{2,1,0:T(8,128)(2,1)} %all-gather.8.cloned.1.call-done.weight_ref, ...), custom_call_target="tpu_custom_call" | custom-call | flops 60129542144 | bytes 83886080 | tf_op jit(solution)/shard_map/mlp/pallas_call | solution.py:1035
  350.9 110.4 %sum_middle_back.1 = (bf16[1024,2048]{1,0:T(8,128)(2,1)}, f32[512,2048]{1,0:T(8,128)}, f32[8,2048]{1,0:T(8,128)}, bf16[1024,2048]{1,0:T(8,128)(2,1)}) custom-call(bf16[1024,2048]{1,0:T(8,128)(2,1)} %get-tuple-element.84.part_ref, f32[512,2048]{1,0:T(8,128)} %get-tuple-element.85.middle_hbm, bf16[1024,2048]{1,0:T(8,128)(2,1)} %cotangent_hbm.3, ...), custom_call_target="tpu_custom_call" | custom-call | flops 99999997952 | bytes 25165824 | tf_op jit(solution)/shard_map/sum_middle_back/pallas_call | solution.py:453
  461.4 6.3 multiply_subtract_fusion.1
  467.7 131.2 %attend_back.1 = (bf16[1024,512]{1,0:T(8,128)(2,1)}, bf16[1024,512]{1,0:T(8,128)(2,1)}, bf16[1024,512]{1,0:T(8,128)(2,1)}, bf16[1024,2048]{1,0:T(8,128)(2,1)}) custom-call(s32[1]{0:T(128)S(6)} %copy.43.live_ref, bf16[1024,512]{1,0:T(8,128)(2,1)} %get-tuple-element.70.q_hbm, bf16[1024,512]{1,0:T(8,128)(2,1)} %get-tuple-element.71.k_hbm, ...), custom_call_target="tpu_custom_call" | custom-call | flops 99999997952 | bytes 41943040 | tf_op jit(solution)/shard_map/attend_back/pallas_call | solution.py:935
  598.9 25.4 %projection_back.1 = (bf16[4,2048,512]{2,1,0:T(8,128)(2,1)}, bf16[1024,2048]{1,0:T(8,128)(2,1)}) custom-call(bf16[1024,2048]{1,0:T(8,128)(2,1)} %get-tuple-element.90.normed_ref, bf16[3,2048,512]{2,1,0:T(8,128)(2,1)} %all-gather.4.cloned.1.call-done.weight_ref, bf16[1024,512]{1,0:T(8,128)(2,1)} %get-tuple-element.91.dq_ref, ...), custom_call_target="tpu_custom_call" | custom-call | flops 15032385536 | bytes 41943040 | tf_op jit(solution)/shard_map/projection_back/pallas_call | solution.py:1100
  624.3 10.2 %multiply_subtract_fusion = (f32[2,256,2048]{2,1,0:T(8,128)}, f32[2,256,2048]{2,1,0:T(8,128)}, f32[2,256,2048]{2,1,0:T(8,128)}, f32[2,256,2048]{2,1,0:T(8,128)}) fusion(f32[2,256,2048]{2,1,0:T(8,128)} %gate_up_ref.1, f32[2,256,2048]{2,1,0:T(8,128)} %param.28, f32[2,256,2048]{2,1,0:T(8,128)} %param.33, bf16[2,256,2048]{2,1,0:T(8,128)(2,1)} %reduce-scatter.6.cloned.1.call-done), kind=kLoop, calls=%fused_computation.2 | loop fusion | flops 16777216 | bytes 31457280 | tf_op jit(solution)/shard_map/sub | solution.py:1274
  634.5 123.7 %sum_input_back.1 = (bf16[1024,2048]{1,0:T(8,128)(2,1)}, f32[2,256]{1,0:T(2,128)}) custom-call(bf16[1024,2048]{1,0:T(8,128)(2,1)} %get-tuple-element.99.part_ref, bf16[1024,2048]{1,0:T(8,128)(2,1)} %tokens_hbm.3, f32[512,2048]{1,0:T(8,128)} %get-tuple-element.100.grad_hbm, f32[8,2048]{1,0:T(8,128)} %get-tuple-element.79.gain_ref, ...), custom_call_target="tpu_custom_call" | custom-call | flops 99999997952 | bytes 25165824 | tf_op jit(solution)/shard_map/sum_input_back/pallas_call | solution.py:453
  758.2 1.2 add_multiply_fusion
  759.5 8.3 %adam_tail.1 = (f32[3,256,512]{2,1,0:T(8,128)}, f32[3,256,512]{2,1,0:T(8,128)}, f32[3,256,512]{2,1,0:T(8,128)}, f32[3,256,512]{2,1,0:T(8,128)}, f32[512,256]{1,0...) custom-call(bf16[4,256,512]{2,1,0:T(8,128)(2,1)} %reduce-scatter.8.cloned.1.call-done.grad_ref.out_grad_ref, ...), custom_call_target="tpu_custom_call" | custom-call | flops 10000000 | bytes 16777216 | tf_op jit(solution)/shard_map/adam_tail/pallas_call | solution.py:1152
  767.8 4.9 copy.44
  772.7 2.0 copy.45
  774.7 0.6 copy.46
  (40 shorter events, 0.7 us)
Async XLA Ops:
  7.2 5.5 copy-start.1
  7.2 5.5 copy-start.3
  7.2 51.6 %all-gather.4.cloned.1.call-start = ((), (), s32[]{:S(2)}) async-start(), calls=%async_computation.3 | async-start | bytes 7077888 | tf_op jit(solution)/shard_map/all_gather | solution.py:1222
  9.8 152.0 %all-gather.6.cloned.1.call-start = ((), (), s32[]{:S(2)}) async-start(), calls=%async_computation.4 | async-start | bytes 11796480 | tf_op jit(solution)/shard_map/all_gather | solution.py:1222
  12.7 2.2 copy-start
  14.9 44.6 %copy-start.7 = (f32[2,256]{1,0:T(2,128)S(1)}, f32[2,256]{1,0:T(2,128)}, u32[]{:S(2)}) copy-start(f32[2,256]{1,0:T(2,128)} %param.25) | copy-start | bytes 6148
  16.3 1.3 copy-start.2
  17.7 0.8 copy-start.4
  18.5 0.8 copy-start.5
  58.8 218.2 %all-gather.8.cloned.1.call-start = ((), (), s32[]{:S(2)}) async-start(), calls=%async_computation.5 | async-start | bytes 18874368 | tf_op jit(solution)/shard_map/all_gather | solution.py:1222
  161.8 299.5 %reduce-scatter.4.cloned.1.call-start = ((), (), s32[]{:S(2)}) async-start(), calls=%async_computation.6 | async-start | bytes 9437184 | tf_op jit(solution)/shard_map/reduce_scatter | solution.py:1172
  350.9 273.4 %reduce-scatter.6.cloned.1.call-start = ((), (), s32[]{:S(2)}) async-start(), calls=%async_computation.7 | async-start | bytes 18874368 | tf_op jit(solution)/shard_map/reduce_scatter | solution.py:1172
  467.6 291.8 %reduce-scatter.8.cloned.1.call-start = ((), (), s32[]{:S(2)}) async-start(), calls=%async_computation.8 | async-start | bytes 9437184 | tf_op jit(solution)/shard_map/reduce_scatter | solution.py:1251
  634.5 123.7 %copy-start.8 = (f32[2,256]{1,0:T(2,128)S(1)}, f32[2,256]{1,0:T(2,128)}, u32[]{:S(2)}) copy-start(f32[2,256]{1,0:T(2,128)} %param.25) | copy-start | bytes 6148
  634.5 123.7 %copy-start.10 = (f32[2,256]{1,0:T(2,128)S(1)}, f32[2,256]{1,0:T(2,128)}, u32[]{:S(2)}) copy-start(f32[2,256]{1,0:T(2,128)} %param.30) | copy-start | bytes 6148
  634.5 123.7 %copy-start.11 = (f32[2,256]{1,0:T(2,128)S(1)}, f32[2,256]{1,0:T(2,128)}, u32[]{:S(2)}) copy-start(f32[2,256]{1,0:T(2,128)} %param.35) | copy-start | bytes 6148
  767.7 5.0 copy-start.6
  772.7 2.0 copy-start.9
Sparse Core Ops, SparseCore 0:
  10.5 48.2 all-gather.3
  61.2 96.2 all-gather.5
  161.9 99.4 all-gather.7
  351.0 79.0 reduce-scatter.3
  467.8 149.3 reduce-scatter.5
  634.6 77.3 reduce-scatter.7

commit v7 on v6

--- a/solution.py
+++ b/solution.py
@@ -595,10 +595,12 @@
 
 
 def front_kernel(
-    live_ref, tokens_ref, weight_ref, own_gain_ref, cos_ref, sin_ref,
-    h_ref, q_ref, k_ref, v_ref, kp_ref, vp_ref, o_ref, l_ref, gain_ref,
-    send, recv, gain_send, gain_recv,
+    live_ref, tokens_hbm, weight_hbm, own_gain_ref, cos_ref, sin_ref,
+    h_hbm, q_ref, k_ref, v_ref, kp_ref, vp_ref, o_ref, l_ref, gain_ref,
+    send, recv, gain_send, gain_recv, tokens_ref, weight_ref, h_ref, load_sem, store_sem,
 ):
+    load, wait = loads_of([(tokens_hbm, tokens_ref), (weight_hbm, weight_ref)], load_sem)
+    load()
     late = lax.axis_index("ctx")
     rows, width = q_ref.shape
     block = min(BLOCK, rows)
@@ -622,18 +624,23 @@
         gain_copy(distance).start()
     for distance in range(1, size):
         gain_copy(distance).wait()
+    wait()
 
     def here(at):
         return pl.ds(pl.multiple_of(at * block, block), block)
 
     def lanes(pair):
         return pl.ds(pl.multiple_of(pair * PAIR, PAIR), PAIR)
+
+    def h_store(at):
+        return pltpu.make_async_copy(h_ref.at[here(at)], h_hbm.at[here(at)], store_sem.at[at])
 
     @pl.loop(0, blocks)
     def _(at):
         stream = tokens_ref[here(at)].astype(jnp.float32)
         normed = (stream * unit_scale(stream) * gain_ref[0:1]).astype(jnp.bfloat16)
         h_ref[here(at)] = normed
+        h_store(at).start()
         keys = dot(normed, weight_ref[1], (1, 0))
         k_ref[here(at)] = rotate_pairs(keys, cos_ref[here(at)], sin_ref[here(at)]).astype(jnp.bfloat16)
         v_ref[here(at)] = dot(normed, weight_ref[2], (1, 0)).astype(jnp.bfloat16)
@@ -718,6 +725,10 @@
             for copy in exchange(pair):
                 copy.wait_send()
 
+    @pl.loop(0, blocks)
+    def _(at):
+        h_store(at).wait()
+
 
 def layer_front(live, tokens, weight, gain, cosine, sine):
     rows, depth = tokens.shape
@@ -733,10 +744,17 @@
     return pl.pallas_call(
         front_kernel,
         out_shape=outs,
-        in_specs=[SMEM_SPEC] + [VMEM_SPEC] * 5,
-        out_specs=(VMEM_SPEC,) * len(outs),
+        in_specs=[SMEM_SPEC, HBM_SPEC, HBM_SPEC] + [VMEM_SPEC] * 3,
+        out_specs=(HBM_SPEC,) + (VMEM_SPEC,) * (len(outs) - 1),
         scratch_shapes=[pltpu.SemaphoreType.DMA((2, pairs))] * 2
-        + [pltpu.SemaphoreType.DMA((size,))] * 2,
+        + [pltpu.SemaphoreType.DMA((size,))] * 2
+        + [
+            pltpu.VMEM(tokens.shape, jnp.bfloat16),
+            pltpu.VMEM(weight.shape, jnp.bfloat16),
+            pltpu.VMEM(tokens.shape, jnp.bfloat16),
+            pltpu.SemaphoreType.DMA((2,)),
+            pltpu.SemaphoreType.DMA((rows // BLOCK,)),
+        ],
         compiler_params=pltpu.CompilerParams(
             collective_id=4, has_side_effects=True, vmem_limit_bytes=56 * 2**20
         ),

time: 787 us -> 783 us (level)
  no operation moved by 1% of the time
where the time goes in v7:
time: 783 us; the launch traced here: 778 us
  Pallas kernels  686 us (88%)
  waiting for transfers between devices  39.7 us (5%)
  other arithmetic  23.6 us (3%)
  between operations  15.2 us (2%)
  local copies, waits for them, and re-layouts  12.7 us (2%)
    pallas_call x3, Pallas kernels, chain_call(): pl.pallas_call(kernel, out_shape=out_shape, grid=(tick_count(rows, count)...  349 us
    pallas_call x1, Pallas kernels, attend_back(): pl.pallas_call(functools.partial(attend_back_kernel, count), out_shape=ou...  131 us
    pallas_call x1, Pallas kernels, layer_front(): pl.pallas_call(front_kernel, out_shape=outs, in_specs=[SMEM_SPEC, HBM_SPE...  97.6 us
    pallas_call x1, Pallas kernels, mlp(): pl.pallas_call(mlp_kernel, out_shape=(jax.ShapeDtypeStruct((rows, width),...  73.8 us
    all_gather x3, waiting for transfers between devices, body(): gather = lambda a: lax.all_gather(a, ('shard', 'ctx'), axis=1, tiled=True)  39.6 us
    pallas_call x1, Pallas kernels, projection_back(): pl.pallas_call(projection_back_kernel, out_shape=(jax.ShapeDtypeStruct((4...  25.2 us
  transfers between devices with their start and end apart: 6, of which 1 were waited for; matrix products, arithmetic and copies ran while one was open for 1% of the time, Pallas kernels for 78%

profile of v7, /device:TPU:0, one launch (start us, length us, event | category | flops | bytes accessed | tf_op | source)
XLA Modules:
  0.0 778.0 jit_solution(8706198455002250212)
XLA Ops:
  7.3 2.5 convert_element_type.20
  9.9 1.9 multiply_sine_fusion
  11.8 0.9 pad_maximum_fusion
  12.7 2.2 copy-done
  14.9 1.5 narrow.1
  16.3 1.3 copy-done.2
  17.7 0.8 copy-done.4
  18.5 0.8 copy-done.5
  19.2 39.5 %all-gather.4.cloned.1.call-done.weight_hbm.weight_ref = bf16[3,2048,512]{2,1,0:T(8,128)(2,1)} async-done(((bf16[3,256,512]{2,1,0:T(8,128)(2,1)}), bf16[3,2048,512]{2,1,0:T(8,128)(2,1)}) %all-gather.4.cloned.1.call-update) | async-done | bytes 6291472 | tf_op jit(solution)/shard_map/all_gather | solution.py:1240
  59.5 0.6 maximum_convert_fusion.own_gain_ref
  60.1 97.6 %layer_front.1 = (bf16[1024,2048]{1,0:T(8,128)(2,1)}, bf16[1024,512]{1,0:T(8,128)(2,1)}, bf16[1024,512]{1,0:T(8,128)(2,1)}, bf16[1024,512]{1,0:T(8,128)(2,1)}, b...) custom-call(s32[1]{0:T(128)S(6)} %copy.43.live_ref, ...), custom_call_target="tpu_custom_call" | custom-call | flops 80000000000 | bytes 41943040 | tf_op jit(solution)/shard_map/layer_front/pallas_call | solution.py:744
  158.0 115.6 %sum_middle.1 = (bf16[1024,2048]{1,0:T(8,128)(2,1)}, f32[512,2048]{1,0:T(8,128)}, f32[1024,2048]{1,0:T(8,128)}) custom-call(bf16[1024,512]{1,0:T(8,128)(2,1)} %get-tuple-element.75.mixed_ref.o_hbm, bf16[2560,2048]{1,0:T(8,128)(2,1)} %all-gather.6.cloned.1.call-done.weight_ref.down_ref.both_hbm, bf16[1024,2048]{1,0:T(8,128)(2,1)} %tokens_hbm.5, ...), custom_call_target="tpu_custom_call" | custom-call | flops 99999997952 | bytes 25165824 | tf_op jit(solution)/shard_map/sum_middle/pallas_call | solution.py:453
  273.6 73.8 %mlp.1 = (bf16[1024,2048]{1,0:T(8,128)(2,1)}, bf16[2048,2048]{1,0:T(8,128)(2,1)}, bf16[2,2048,2048]{2,1,0:T(8,128)(2,1)}, bf16[1024,2048]{1,0:T(8,128)(2,1)}) custom-call(bf16[1024,2048]{1,0:T(8,128)(2,1)} %get-tuple-element.80.normed_ref, bf16[2,2048,2048]{2,1,0:T(8,128)(2,1)} %all-gather.8.cloned.1.call-done.weight_ref, ...), custom_call_target="tpu_custom_call" | custom-call | flops 60129542144 | bytes 83886080 | tf_op jit(solution)/shard_map/mlp/pallas_call | solution.py:1053
  347.5 109.3 %sum_middle_back.1 = (bf16[1024,2048]{1,0:T(8,128)(2,1)}, f32[512,2048]{1,0:T(8,128)}, f32[8,2048]{1,0:T(8,128)}, bf16[1024,2048]{1,0:T(8,128)(2,1)}) custom-call(bf16[1024,2048]{1,0:T(8,128)(2,1)} %get-tuple-element.84.part_ref, f32[512,2048]{1,0:T(8,128)} %get-tuple-element.85.middle_hbm, bf16[1024,2048]{1,0:T(8,128)(2,1)} %cotangent_hbm.3, ...), custom_call_target="tpu_custom_call" | custom-call | flops 99999997952 | bytes 25165824 | tf_op jit(solution)/shard_map/sum_middle_back/pallas_call | solution.py:453
  456.8 6.3 multiply_subtract_fusion.1
  463.1 130.9 %attend_back.1 = (bf16[1024,512]{1,0:T(8,128)(2,1)}, bf16[1024,512]{1,0:T(8,128)(2,1)}, bf16[1024,512]{1,0:T(8,128)(2,1)}, bf16[1024,2048]{1,0:T(8,128)(2,1)}) custom-call(s32[1]{0:T(128)S(6)} %copy.43.live_ref, bf16[1024,512]{1,0:T(8,128)(2,1)} %get-tuple-element.70.q_hbm, bf16[1024,512]{1,0:T(8,128)(2,1)} %get-tuple-element.71.k_hbm, ...), custom_call_target="tpu_custom_call" | custom-call | flops 99999997952 | bytes 41943040 | tf_op jit(solution)/shard_map/attend_back/pallas_call | solution.py:953
  594.0 25.2 %projection_back.1 = (bf16[4,2048,512]{2,1,0:T(8,128)(2,1)}, bf16[1024,2048]{1,0:T(8,128)(2,1)}) custom-call(bf16[1024,2048]{1,0:T(8,128)(2,1)} %get-tuple-element.90.normed_ref, bf16[3,2048,512]{2,1,0:T(8,128)(2,1)} %all-gather.4.cloned.1.call-done.weight_hbm.weight_ref, bf16[1024,512]{1,0:T(8,128)(2,1)} %get-tuple-element.91.dq_ref, ...), custom_call_target="tpu_custom_call" | custom-call | flops 15032385536 | bytes 41943040 | tf_op jit(solution)/shard_map/projection_back/pallas_call | solution.py:1118
  619.2 10.2 %multiply_subtract_fusion = (f32[2,256,2048]{2,1,0:T(8,128)}, f32[2,256,2048]{2,1,0:T(8,128)}, f32[2,256,2048]{2,1,0:T(8,128)}, f32[2,256,2048]{2,1,0:T(8,128)}) fusion(f32[2,256,2048]{2,1,0:T(8,128)} %gate_up_ref.1, f32[2,256,2048]{2,1,0:T(8,128)} %param.28, f32[2,256,2048]{2,1,0:T(8,128)} %param.33, bf16[2,256,2048]{2,1,0:T(8,128)(2,1)} %reduce-scatter.6.cloned.1.call-done), kind=kLoop, calls=%fused_computation.2 | loop fusion | flops 16777216 | bytes 31457280 | tf_op jit(solution)/shard_map/sub | solution.py:1292
  629.4 124.5 %sum_input_back.1 = (bf16[1024,2048]{1,0:T(8,128)(2,1)}, f32[2,256]{1,0:T(2,128)}) custom-call(bf16[1024,2048]{1,0:T(8,128)(2,1)} %get-tuple-element.99.part_ref, bf16[1024,2048]{1,0:T(8,128)(2,1)} %tokens_hbm.5, f32[512,2048]{1,0:T(8,128)} %get-tuple-element.100.grad_hbm, f32[8,2048]{1,0:T(8,128)} %get-tuple-element.79.gain_ref, ...), custom_call_target="tpu_custom_call" | custom-call | flops 99999997952 | bytes 25165824 | tf_op jit(solution)/shard_map/sum_input_back/pallas_call | solution.py:453
  753.9 1.2 add_multiply_fusion
  755.2 8.3 %adam_tail.1 = (f32[3,256,512]{2,1,0:T(8,128)}, f32[3,256,512]{2,1,0:T(8,128)}, f32[3,256,512]{2,1,0:T(8,128)}, f32[3,256,512]{2,1,0:T(8,128)}, f32[512,256]{1,0...) custom-call(bf16[4,256,512]{2,1,0:T(8,128)(2,1)} %reduce-scatter.8.cloned.1.call-done.grad_ref.out_grad_ref, ...), custom_call_target="tpu_custom_call" | custom-call | flops 10000000 | bytes 16777216 | tf_op jit(solution)/shard_map/adam_tail/pallas_call | solution.py:1170
  763.5 4.9 copy.44
  768.4 2.0 copy.45
  770.4 0.6 copy.46
  (40 shorter events, 0.7 us)
Async XLA Ops:
  7.2 5.5 copy-start.1
  7.2 5.5 copy-start.3
  7.2 51.6 %all-gather.4.cloned.1.call-start = ((), (), s32[]{:S(2)}) async-start(), calls=%async_computation.3 | async-start | bytes 7077888 | tf_op jit(solution)/shard_map/all_gather | solution.py:1240
  9.8 147.9 %all-gather.6.cloned.1.call-start = ((), (), s32[]{:S(2)}) async-start(), calls=%async_computation.4 | async-start | bytes 11796480 | tf_op jit(solution)/shard_map/all_gather | solution.py:1240
  12.7 2.2 copy-start
  14.9 44.6 %copy-start.7 = (f32[2,256]{1,0:T(2,128)S(1)}, f32[2,256]{1,0:T(2,128)}, u32[]{:S(2)}) copy-start(f32[2,256]{1,0:T(2,128)} %param.25) | copy-start | bytes 6148
  16.3 1.3 copy-start.2
  17.7 0.8 copy-start.4
  18.5 0.8 copy-start.5
  58.8 214.8 %all-gather.8.cloned.1.call-start = ((), (), s32[]{:S(2)}) async-start(), calls=%async_computation.5 | async-start | bytes 18874368 | tf_op jit(solution)/shard_map/all_gather | solution.py:1240
  157.8 299.0 %reduce-scatter.4.cloned.1.call-start = ((), (), s32[]{:S(2)}) async-start(), calls=%async_computation.6 | async-start | bytes 9437184 | tf_op jit(solution)/shard_map/reduce_scatter | solution.py:1190
  347.4 271.8 %reduce-scatter.6.cloned.1.call-start = ((), (), s32[]{:S(2)}) async-start(), calls=%async_computation.7 | async-start | bytes 18874368 | tf_op jit(solution)/shard_map/reduce_scatter | solution.py:1190
  463.1 292.1 %reduce-scatter.8.cloned.1.call-start = ((), (), s32[]{:S(2)}) async-start(), calls=%async_computation.8 | async-start | bytes 9437184 | tf_op jit(solution)/shard_map/reduce_scatter | solution.py:1269
  629.4 124.5 %copy-start.8 = (f32[2,256]{1,0:T(2,128)S(1)}, f32[2,256]{1,0:T(2,128)}, u32[]{:S(2)}) copy-start(f32[2,256]{1,0:T(2,128)} %param.25) | copy-start | bytes 6148
  629.4 124.5 %copy-start.10 = (f32[2,256]{1,0:T(2,128)S(1)}, f32[2,256]{1,0:T(2,128)}, u32[]{:S(2)}) copy-start(f32[2,256]{1,0:T(2,128)} %param.30) | copy-start | bytes 6148
  629.4 124.5 %copy-start.11 = (f32[2,256]{1,0:T(2,128)S(1)}, f32[2,256]{1,0:T(2,128)}, u32[]{:S(2)}) copy-start(f32[2,256]{1,0:T(2,128)} %param.35) | copy-start | bytes 6148
  763.5 5.0 copy-start.6
  768.4 2.0 copy-start.9
Sparse Core Ops, SparseCore 0:
  10.5 48.2 all-gather.3
  61.2 96.3 all-gather.5
  160.1 97.1 all-gather.7
  347.5 77.7 reduce-scatter.3
  463.2 150.2 reduce-scatter.5
  629.5 78.6 reduce-scatter.7

commit v8 on v7

--- a/solution.py
+++ b/solution.py
@@ -767,7 +767,8 @@
 
 def attend_back_kernel(
     count, live_ref, q_hbm, k_hbm, v_hbm, kp_hbm, vp_hbm, o_hbm, l_ref, cos_ref, sin_ref,
-    part_ref, middle_hbm, grad_ref, both_hbm, dq_ref, dk_ref, dv_ref, out_ref,
+    part_hbm, middle_hbm, grad_hbm, both_hbm, dq_ref, dk_ref, dv_ref, out_ref,
+    part_ref, grad_ref,
     q_ref, k_ref, v_ref, kp_ref, vp_ref, o_ref, do_ref, weight_ref, middle_ref, early_sem, late_sem,
     dq_acc, dk_acc, dv_acc, dkp_acc, dvp_acc, leave, arrive, slots, send, recv, chain_send, chain_recv,
 ):
@@ -778,7 +779,11 @@
     blocks = rows // block
     pairs = width // PAIR
     load_early, wait_early = loads_of(
-        [(both_hbm.at[pl.ds(0, width)], weight_ref), (middle_hbm, middle_ref)], early_sem
+        [
+            (part_hbm, part_ref), (grad_hbm, grad_ref), (both_hbm.at[pl.ds(0, width)], weight_ref),
+            (middle_hbm, middle_ref),
+        ],
+        early_sem,
     )
     load_late, wait_late = loads_of(
         [
@@ -953,13 +958,14 @@
     return pl.pallas_call(
         functools.partial(attend_back_kernel, count),
         out_shape=outs,
-        in_specs=[SMEM_SPEC] + [HBM_SPEC] * 6 + [VMEM_SPEC] * 4 + [HBM_SPEC, VMEM_SPEC, HBM_SPEC],
+        in_specs=[SMEM_SPEC] + [HBM_SPEC] * 6 + [VMEM_SPEC] * 3 + [HBM_SPEC] * 4,
         out_specs=(VMEM_SPEC,) * len(outs),
         scratch_shapes=[
+            *[pltpu.VMEM(out_part.shape, jnp.bfloat16)] * 2,
             *[pltpu.VMEM((rows, width), jnp.bfloat16)] * 7,
             pltpu.VMEM((width, middle.shape[1]), jnp.bfloat16),
             pltpu.VMEM(middle.shape, jnp.float32),
-            pltpu.SemaphoreType.DMA((2,)),
+            pltpu.SemaphoreType.DMA((4,)),
             pltpu.SemaphoreType.DMA((6,)),
             pltpu.VMEM((pairs, PAIR, rows), jnp.float32),
             pltpu.VMEM((rows, width), jnp.float32),

time: 783 us -> 782 us (level)
  no operation moved by 1% of the time
where the time goes in v8:
time: 782 us; the launch traced here: 778 us
  Pallas kernels  686 us (88%)
  waiting for transfers between devices  39.7 us (5%)
  other arithmetic  23.6 us (3%)
  between operations  15.2 us (2%)
  local copies, waits for them, and re-layouts  12.7 us (2%)
    pallas_call x3, Pallas kernels, chain_call(): pl.pallas_call(kernel, out_shape=out_shape, grid=(tick_count(rows, count)...  351 us
    pallas_call x1, Pallas kernels, attend_back(): pl.pallas_call(functools.partial(attend_back_kernel, count), out_shape=ou...  129 us
    pallas_call x1, Pallas kernels, layer_front(): pl.pallas_call(front_kernel, out_shape=outs, in_specs=[SMEM_SPEC, HBM_SPE...  97.6 us
    pallas_call x1, Pallas kernels, mlp(): pl.pallas_call(mlp_kernel, out_shape=(jax.ShapeDtypeStruct((rows, width),...  73.8 us
    all_gather x3, waiting for transfers between devices, body(): gather = lambda a: lax.all_gather(a, ('shard', 'ctx'), axis=1, tiled=True)  39.6 us
    pallas_call x1, Pallas kernels, projection_back(): pl.pallas_call(projection_back_kernel, out_shape=(jax.ShapeDtypeStruct((4...  25.4 us
  transfers between devices with their start and end apart: 6, of which 1 were waited for; matrix products, arithmetic and copies ran while one was open for 1% of the time, Pallas kernels for 78%

profile of v8, /device:TPU:0, one launch (start us, length us, event | category | flops | bytes accessed | tf_op | source)
XLA Modules:
  0.0 777.8 jit_solution(3708660159076060389)
XLA Ops:
  7.3 2.5 convert_element_type.20
  9.9 1.9 multiply_sine_fusion
  11.8 0.9 pad_maximum_fusion
  12.7 2.2 copy-done
  14.9 1.5 narrow.1
  16.3 1.3 copy-done.2
  17.7 0.8 copy-done.4
  18.5 0.8 copy-done.5
  19.2 39.5 %all-gather.4.cloned.1.call-done.weight_hbm.weight_ref = bf16[3,2048,512]{2,1,0:T(8,128)(2,1)} async-done(((bf16[3,256,512]{2,1,0:T(8,128)(2,1)}), bf16[3,2048,512]{2,1,0:T(8,128)(2,1)}) %all-gather.4.cloned.1.call-update) | async-done | bytes 6291472 | tf_op jit(solution)/shard_map/all_gather | solution.py:1246
  59.5 0.6 maximum_convert_fusion.own_gain_ref
  60.1 97.6 %layer_front.1 = (bf16[1024,2048]{1,0:T(8,128)(2,1)}, bf16[1024,512]{1,0:T(8,128)(2,1)}, bf16[1024,512]{1,0:T(8,128)(2,1)}, bf16[1024,512]{1,0:T(8,128)(2,1)}, b...) custom-call(s32[1]{0:T(128)S(6)} %copy.43.live_ref, ...), custom_call_target="tpu_custom_call" | custom-call | flops 80000000000 | bytes 41943040 | tf_op jit(solution)/shard_map/layer_front/pallas_call | solution.py:744
  158.0 115.6 %sum_middle.1 = (bf16[1024,2048]{1,0:T(8,128)(2,1)}, f32[512,2048]{1,0:T(8,128)}, f32[1024,2048]{1,0:T(8,128)}) custom-call(bf16[1024,512]{1,0:T(8,128)(2,1)} %get-tuple-element.75.mixed_ref.o_hbm, bf16[2560,2048]{1,0:T(8,128)(2,1)} %all-gather.6.cloned.1.call-done.weight_ref.down_ref.both_hbm, bf16[1024,2048]{1,0:T(8,128)(2,1)} %tokens_hbm.5, ...), custom_call_target="tpu_custom_call" | custom-call | flops 99999997952 | bytes 25165824 | tf_op jit(solution)/shard_map/sum_middle/pallas_call | solution.py:453
  273.6 73.8 %mlp.1 = (bf16[1024,2048]{1,0:T(8,128)(2,1)}, bf16[2048,2048]{1,0:T(8,128)(2,1)}, bf16[2,2048,2048]{2,1,0:T(8,128)(2,1)}, bf16[1024,2048]{1,0:T(8,128)(2,1)}) custom-call(bf16[1024,2048]{1,0:T(8,128)(2,1)} %get-tuple-element.80.normed_ref, bf16[2,2048,2048]{2,1,0:T(8,128)(2,1)} %all-gather.8.cloned.1.call-done.weight_ref, ...), custom_call_target="tpu_custom_call" | custom-call | flops 60129542144 | bytes 83886080 | tf_op jit(solution)/shard_map/mlp/pallas_call | solution.py:1059
  347.5 109.3 %sum_middle_back.1 = (bf16[1024,2048]{1,0:T(8,128)(2,1)}, f32[512,2048]{1,0:T(8,128)}, f32[8,2048]{1,0:T(8,128)}, bf16[1024,2048]{1,0:T(8,128)(2,1)}) custom-call(bf16[1024,2048]{1,0:T(8,128)(2,1)} %get-tuple-element.84.part_ref, f32[512,2048]{1,0:T(8,128)} %get-tuple-element.85.middle_hbm, bf16[1024,2048]{1,0:T(8,128)(2,1)} %cotangent_hbm.3, ...), custom_call_target="tpu_custom_call" | custom-call | flops 99999997952 | bytes 25165824 | tf_op jit(solution)/shard_map/sum_middle_back/pallas_call | solution.py:453
  456.8 6.3 multiply_subtract_fusion.1
  463.1 128.7 %attend_back.1 = (bf16[1024,512]{1,0:T(8,128)(2,1)}, bf16[1024,512]{1,0:T(8,128)(2,1)}, bf16[1024,512]{1,0:T(8,128)(2,1)}, bf16[1024,2048]{1,0:T(8,128)(2,1)}) custom-call(s32[1]{0:T(128)S(6)} %copy.43.live_ref, bf16[1024,512]{1,0:T(8,128)(2,1)} %get-tuple-element.70.q_hbm, bf16[1024,512]{1,0:T(8,128)(2,1)} %get-tuple-element.71.k_hbm, ...), custom_call_target="tpu_custom_call" | custom-call | flops 99999997952 | bytes 41943040 | tf_op jit(solution)/shard_map/attend_back/pallas_call | solution.py:958
  591.8 25.4 %projection_back.1 = (bf16[4,2048,512]{2,1,0:T(8,128)(2,1)}, bf16[1024,2048]{1,0:T(8,128)(2,1)}) custom-call(bf16[1024,2048]{1,0:T(8,128)(2,1)} %get-tuple-element.90.normed_ref, bf16[3,2048,512]{2,1,0:T(8,128)(2,1)} %all-gather.4.cloned.1.call-done.weight_hbm.weight_ref, bf16[1024,512]{1,0:T(8,128)(2,1)} %get-tuple-element.91.dq_ref, ...), custom_call_target="tpu_custom_call" | custom-call | flops 15032385536 | bytes 41943040 | tf_op jit(solution)/shard_map/projection_back/pallas_call | solution.py:1124
  617.2 10.2 %multiply_subtract_fusion = (f32[2,256,2048]{2,1,0:T(8,128)}, f32[2,256,2048]{2,1,0:T(8,128)}, f32[2,256,2048]{2,1,0:T(8,128)}, f32[2,256,2048]{2,1,0:T(8,128)}) fusion(f32[2,256,2048]{2,1,0:T(8,128)} %gate_up_ref.1, f32[2,256,2048]{2,1,0:T(8,128)} %param.28, f32[2,256,2048]{2,1,0:T(8,128)} %param.33, bf16[2,256,2048]{2,1,0:T(8,128)(2,1)} %reduce-scatter.6.cloned.1.call-done), kind=kLoop, calls=%fused_computation.2 | loop fusion | flops 16777216 | bytes 31457280 | tf_op jit(solution)/shard_map/sub | solution.py:1298
  627.5 126.2 %sum_input_back.1 = (bf16[1024,2048]{1,0:T(8,128)(2,1)}, f32[2,256]{1,0:T(2,128)}) custom-call(bf16[1024,2048]{1,0:T(8,128)(2,1)} %get-tuple-element.99.part_ref, bf16[1024,2048]{1,0:T(8,128)(2,1)} %tokens_hbm.5, f32[512,2048]{1,0:T(8,128)} %get-tuple-element.100.grad_hbm, f32[8,2048]{1,0:T(8,128)} %get-tuple-element.79.gain_ref, ...), custom_call_target="tpu_custom_call" | custom-call | flops 99999997952 | bytes 25165824 | tf_op jit(solution)/shard_map/sum_input_back/pallas_call | solution.py:453
  753.7 1.2 add_multiply_fusion
  754.9 8.3 %adam_tail.1 = (f32[3,256,512]{2,1,0:T(8,128)}, f32[3,256,512]{2,1,0:T(8,128)}, f32[3,256,512]{2,1,0:T(8,128)}, f32[3,256,512]{2,1,0:T(8,128)}, f32[512,256]{1,0...) custom-call(bf16[4,256,512]{2,1,0:T(8,128)(2,1)} %reduce-scatter.8.cloned.1.call-done.grad_ref.out_grad_ref, ...), custom_call_target="tpu_custom_call" | custom-call | flops 10000000 | bytes 16777216 | tf_op jit(solution)/shard_map/adam_tail/pallas_call | solution.py:1176
  763.2 4.9 copy.44
  768.2 2.0 copy.45
  770.2 0.6 copy.46
  (40 shorter events, 0.7 us)
Async XLA Ops:
  7.2 5.5 copy-start.1
  7.2 5.5 copy-start.3
  7.2 51.6 %all-gather.4.cloned.1.call-start = ((), (), s32[]{:S(2)}) async-start(), calls=%async_computation.3 | async-start | bytes 7077888 | tf_op jit(solution)/shard_map/all_gather | solution.py:1246
  9.8 147.9 %all-gather.6.cloned.1.call-start = ((), (), s32[]{:S(2)}) async-start(), calls=%async_computation.4 | async-start | bytes 11796480 | tf_op jit(solution)/shard_map/all_gather | solution.py:1246
  12.7 2.2 copy-start
  14.9 44.6 %copy-start.7 = (f32[2,256]{1,0:T(2,128)S(1)}, f32[2,256]{1,0:T(2,128)}, u32[]{:S(2)}) copy-start(f32[2,256]{1,0:T(2,128)} %param.25) | copy-start | bytes 6148
  16.3 1.3 copy-start.2
  17.7 0.8 copy-start.4
  18.5 0.8 copy-start.5
  58.8 214.8 %all-gather.8.cloned.1.call-start = ((), (), s32[]{:S(2)}) async-start(), calls=%async_computation.5 | async-start | bytes 18874368 | tf_op jit(solution)/shard_map/all_gather | solution.py:1246
  157.8 299.0 %reduce-scatter.4.cloned.1.call-start = ((), (), s32[]{:S(2)}) async-start(), calls=%async_computation.6 | async-start | bytes 9437184 | tf_op jit(solution)/shard_map/reduce_scatter | solution.py:1196
  347.4 269.8 %reduce-scatter.6.cloned.1.call-start = ((), (), s32[]{:S(2)}) async-start(), calls=%async_computation.7 | async-start | bytes 18874368 | tf_op jit(solution)/shard_map/reduce_scatter | solution.py:1196
  463.1 291.8 %reduce-scatter.8.cloned.1.call-start = ((), (), s32[]{:S(2)}) async-start(), calls=%async_computation.8 | async-start | bytes 9437184 | tf_op jit(solution)/shard_map/reduce_scatter | solution.py:1275
  627.4 126.2 %copy-start.8 = (f32[2,256]{1,0:T(2,128)S(1)}, f32[2,256]{1,0:T(2,128)}, u32[]{:S(2)}) copy-start(f32[2,256]{1,0:T(2,128)} %param.25) | copy-start | bytes 6148
  627.5 126.2 %copy-start.10 = (f32[2,256]{1,0:T(2,128)S(1)}, f32[2,256]{1,0:T(2,128)}, u32[]{:S(2)}) copy-start(f32[2,256]{1,0:T(2,128)} %param.30) | copy-start | bytes 6148
  627.5 126.2 %copy-start.11 = (f32[2,256]{1,0:T(2,128)S(1)}, f32[2,256]{1,0:T(2,128)}, u32[]{:S(2)}) copy-start(f32[2,256]{1,0:T(2,128)} %param.35) | copy-start | bytes 6148
  763.2 5.0 copy-start.6
  768.1 2.0 copy-start.9
Sparse Core Ops, SparseCore 0:
  10.5 48.2 all-gather.3
  61.2 96.3 all-gather.5
  160.1 97.1 all-gather.7
  347.5 77.7 reduce-scatter.3
  463.2 150.4 reduce-scatter.5
  627.6 80.4 reduce-scatter.7
